TPU v7x, 32 devices: a whole 2x2x4 slice. The times are simulated.
32 devices in a mesh: section: 4 (over y, x), rep: 8 (over z, core).
Axes of the slice: x: 2, y: 2, z: 4, core: 2. Of those that a mesh axis runs over, the one named last changes fastest.
Arguments:
- history: bfloat16 [4, 16, 64, 9216], P('section', 'rep'), may hold values from -6 to 6
- codes: int32 [4, 16, 64, 9216], P('section', 'rep'), may hold values from -128 to 127
- scales: float32 [4, 16, 64], P('section', 'rep'), may hold values from 0.003 to 0.03
- sample_ids: int32 [8, 2], P('rep'), may hold values from 0 to 1, each once within a row
- cotangent: bfloat16 [16, 64, 9216], P('rep'), may hold values from -6 to 6
- ln_gain: float32 [4, 9216], P('section'), may hold values from 0.5 to 1.5
- ln_bias: float32 [4, 9216], P('section'), may hold values from -3 to 3
- down_weight: bfloat16 [4, 9216, 256], P('section', 'rep'), may hold values from -0.1875 to 0.1875
- up_weight: bfloat16 [4, 9216, 256], P('section', 'rep'), may hold values from -0.0625 to 0.0625
Outputs:
- input_grads: bfloat16 [4, 16, 64, 9216], P('section', 'rep')
- adapter_grads: float32 [4, 9216, 512], P('section', 'rep')
Inputs may be any that keep to these rules, and one draw needn't show every extreme that they name: `sample_ids`: each replica's row names every history entry of that replica once.
All inputs are finite; a program needn't handle non-finite values.
Results may differ from a plain program's by a relative error of at most 0.038.
Values may be sent and summed in bfloat16 or wider, within the bound.
No kernel may reach another device: no remote copies, remote signals or barrier semaphores. Data moves between devices by JAX's collectives and lax.ppermute only.
A program may use at most 128 MiB of HBM per device.

v0:
```python
import jax
import jax.numpy as jnp
from jax import lax
from jax.sharding import PartitionSpec as P

EPSILON = 1e-05
HALF_ROOT = 0.7071067811865476
DENSITY = 0.3989422804014327


def from_behind(value, axis, steps):
    count = lax.axis_size(axis)
    leading, last = (max(0, -steps), min(count, count - steps))
    return lax.ppermute(value, axis, [(source, source + steps) for source in range(leading, last)])


def unpack_codes(levels):
    return levels.astype(jnp.float32)


def gelu_pair(preact):
    normal_cdf = 0.5 * (1.0 + lax.erf(preact * HALF_ROOT))
    bump = DENSITY * jnp.exp(-0.5 * preact * preact)
    return (preact * normal_cdf, normal_cdf + preact * bump)


def section_inputs(stored, packed, scaling, picks):
    chosen = jnp.take(stored, picks, axis=0).astype(jnp.float32)
    rebuilt = chosen + scaling[..., None] * unpack_codes(packed)
    return rebuilt.astype(jnp.bfloat16).reshape(-1, stored.shape[-1])


def normalize(inputs, gain_row, bias_row):
    values = inputs.astype(jnp.float32)
    centred = values - jnp.mean(values, axis=-1, keepdims=True)
    inv_std = lax.rsqrt(jnp.mean(centred * centred, axis=-1, keepdims=True) + EPSILON)
    scaled = centred * inv_std
    normed = (scaled * gain_row + bias_row).astype(jnp.bfloat16)
    return (normed, scaled, inv_std)


def input_grad(out_grad, back, gain_row, scaled, inv_std):
    weighted = back * gain_row
    inner = (
        weighted
        - jnp.mean(weighted, axis=-1, keepdims=True)
        - scaled * jnp.mean(weighted * scaled, axis=-1, keepdims=True)
    )
    return (out_grad.astype(jnp.float32) + inv_std * inner).astype(jnp.bfloat16)


def contract_rows(left, right):
    return lax.dot_general(
        left, right, (((0,), (0,)), ((), ())), preferred_element_type=jnp.float32
    )


def contract_cols(left, right):
    return lax.dot_general(
        left, right, (((1,), (1,)), ((), ())), preferred_element_type=jnp.float32
    )


def take_rows(source, begin, count):
    return lax.dynamic_slice_in_dim(source, begin, count, 0)


def put_rows(target, active, values, begin):
    older = lax.dynamic_slice_in_dim(target, begin, values.shape[0], 0)
    return lax.dynamic_update_slice_in_dim(target, jnp.where(active, values, older), begin, 0)


def per_device(
    history, codes, scales, sample_ids, cotangent, ln_gain, ln_bias, down_weight, up_weight
):
    sections = lax.axis_size("section")
    position = lax.axis_index("section")
    w_down, w_up = (
        lax.all_gather(down_weight[0], "rep", axis=0, tiled=True),
        lax.all_gather(up_weight[0], "rep", axis=0, tiled=True),
    )
    inputs = section_inputs(history[0], codes[0], scales[0], sample_ids[0])
    gain_row = ln_gain[0]
    bias_row = ln_bias[0]
    normed, scaled, inv_std = normalize(inputs, gain_row, bias_row)
    activated, slopes = gelu_pair(jnp.dot(normed, w_down, preferred_element_type=jnp.float32))
    hidden = activated.astype(jnp.bfloat16)
    tok_count = cotangent.shape[1]
    row_total = inputs.shape[0]
    model_width = inputs.shape[1]
    rank_pair = 2 * w_down.shape[1]
    seeded = cotangent.reshape(row_total, model_width)
    pieces = 1
    block_size = tok_count // pieces
    blocks = row_total // block_size
    tick_count = blocks + sections - 1

    def advance(tick, carry):
        incoming, produced, running, kept_grad, kept_top = carry
        offset = tick - (sections - 1 - position)
        active = jnp.logical_and(offset >= 0, offset < blocks)
        begin = jnp.clip(offset, 0, blocks - 1) * block_size
        top_grad = take_rows(seeded, begin, block_size)
        out_grad = jnp.where(position == sections - 1, top_grad, incoming)
        slope_rows = take_rows(slopes, begin, block_size)
        scaled_rows = take_rows(scaled, begin, block_size)
        inv_rows = take_rows(inv_std, begin, block_size)
        act_grad = (
            jnp.dot(out_grad, w_up, preferred_element_type=jnp.float32) * slope_rows
        ).astype(jnp.bfloat16)
        back = contract_cols(act_grad, w_down)
        result = input_grad(out_grad, back, gain_row, scaled_rows, inv_rows)
        produced = put_rows(produced, active, result, begin)
        normed_rows = take_rows(normed, begin, block_size)
        hidden_rows = take_rows(hidden, begin, block_size)
        terms = jnp.concatenate(
            [contract_rows(normed_rows, act_grad), contract_rows(out_grad, hidden_rows)], axis=1
        )
        running = running + jnp.where(active, terms, 0.0)
        incoming = from_behind(result, "section", -1)
        return (incoming, produced, running, kept_grad, kept_top)

    start_in = jnp.zeros((block_size, model_width), jnp.bfloat16)
    start_out = jnp.zeros((row_total, model_width), jnp.bfloat16)
    start_sum = jnp.zeros((model_width, rank_pair), jnp.float32)
    start_grad = jnp.zeros((1, 1), jnp.bfloat16)
    start_top = jnp.zeros((1, 1), jnp.bfloat16)
    carry = lax.fori_loop(
        0, tick_count, advance, (start_in, start_out, start_sum, start_grad, start_top)
    )
    produced = carry[1]
    summed = lax.psum_scatter(
        (carry[2] / float(tok_count)).astype(jnp.bfloat16), "rep", scatter_dimension=0, tiled=True
    ).astype(jnp.float32)
    return (produced.reshape(1, row_total // tok_count, tok_count, model_width), summed[None])


def solution(mesh):
    return jax.shard_map(
        per_device,
        mesh=mesh,
        in_specs=(
            P("section", "rep", None, None),
            P("section", "rep", None, None),
            P("section", "rep", None),
            P("rep", None),
            P("rep", None, None),
            P("section", None),
            P("section", None),
            P("section", "rep", None),
            P("section", "rep", None),
        ),
        out_specs=(P("section", "rep", None, None), P("section", "rep", None)),
        check_vma=False,
    )
```

profile of v0, /device:TPU:0, one launch (start us, length us, event | category | flops | bytes accessed | tf_op | source)
XLA Modules:
  0.0 464.5 jit_solution(10402164949591071849)
XLA Ops:
  10.2 2.1 gather_fusion
  12.3 4.5 convert_reduce_fusion
  18.0 7.7 %add_convert_fusion.1 = (bf16[128,9216]{1,0:T(8,128)(2,1)S(1)}, f32[128,9216]{1,0:T(8,128)}) fusion(f32[9216]{0:T(1024)S(1)} %bitcast.75, f32[9216]{0:T(1024)S(1)} %bitcast.73, f32[128]{0:T(128)S(1)} %rsqrt.20, f32[128]{0:T(128)S(1)} %div.26, s32[1,2,64,9216]{3,2,1,0:T(8,128)} %param.12, f32[128]{0:T(128)S(1)} %mul.192, bf16[2,64,9216]{2,1,0:T(8,128)(2,1)} %gather_fusion, ...), kind=kLoop, calls=%fused_computation.31 | loop fusion | flops 14155776 | bytes 14231168 | tf_op jit(solution)/shard_map/convert_element_type | solution.py:38
  25.7 38.4 %all-gather.7.cloned.1.call-done = bf16[1,9216,256]{2,1,0:T(8,128)(2,1)} async-done(((bf16[1,1152,256]{2,1,0:T(8,128)(2,1)}), bf16[1,9216,256]{2,1,0:T(8,128)(2,1)}) %all-gather.7.cloned.1.call-update) | async-done | bytes 4718608 | tf_op jit(solution)/shard_map/all_gather | solution.py:79
  64.1 3.8 multiply_convert_fusion.1
  67.9 48.4 %all-gather.5.cloned.1.call-done = bf16[1,9216,256]{2,1,0:T(8,128)(2,1)} async-done(((bf16[1,1152,256]{2,1,0:T(8,128)(2,1)}), bf16[1,9216,256]{2,1,0:T(8,128)(2,1)}) %all-gather.5.cloned.1.call-update) | async-done | bytes 4718608 | tf_op jit(solution)/shard_map/all_gather | solution.py:80
  116.4 1.6 broadcast_in_dim.52
  118.1 207.3 %while.20 = (s32[]{:T(128)}, bf16[64,9216]{1,0:T(8,128)(2,1)S(1)}, bf16[128,9216]{1,0:T(8,128)(2,1)}, f32[9216,512]{0,1:T(8,128)}, pred[]{:T(512)}, /*index=5*/s...) while((s32[]{:T(128)}, bf16[64,9216]{1,0:T(8,128)(2,1)S(1)}, ...), condition=%wide.region_5.6_spmd.clone, body=%wide.region_2.0_spmd.clone.sunk | while | flops 1234534400 | bytes 187031632 | solution.py:128
  119.5 1.7 dynamic-slice_select_fusion.2
  121.2 3.4 fusion.53
  125.3 1.7 fusion.54
  127.0 2.0 select_dynamic-update-slice_fusion.2
  131.7 1.4 fusion.56
  133.1 2.7 fusion.57
  135.9 8.1 %fusion.58 = f32[9216,512]{0,1:T(8,128)} fusion(f32[9216,256]{0,1:T(8,128)S(1)} %fusion.56, f32[9216,256]{0,1:T(8,128)S(1)} %fusion.57, f32[9216,512]{0,1:T(8,128)} %get-tuple-element.546, pred[]{:T(512)S(6)} %compare.3, pred[]{:T(512)S(6)} %and.21), kind=kLoop, calls=%fused_computation.2.clone.1 | loop fusion | flops 18874368 | bytes 56623104 | tf_op jit(solution)/shard_map/while/body/eval_jaxpr/add | solution.py:119
  144.0 16.6 %collective-permute-done = bf16[64,9216]{1,0:T(8,128)(2,1)S(1)} collective-permute-done((bf16[64,9216]{1,0:T(8,128)(2,1)}, bf16[64,9216]{1,0:T(8,128)(2,1)S(1)}, u32[]{:S(2)}, u32[]{:S(2)}) %collective-permute-start) | collective-permute-done | bytes 1179680 | tf_op jit(solution)/shard_map/while/body/eval_jaxpr/ppermute | solution.py:14
  162.0 1.7 dynamic-slice_select_fusion.2
  163.7 3.4 fusion.53
  167.8 1.7 fusion.54
  169.5 2.0 select_dynamic-update-slice_fusion.2
  175.7 2.7 fusion.57
  178.4 15.6 %fusion.58 = f32[9216,512]{0,1:T(8,128)} fusion(f32[9216,256]{0,1:T(8,128)S(1)} %fusion.56, f32[9216,256]{0,1:T(8,128)S(1)} %fusion.57, f32[9216,512]{0,1:T(8,128)} %get-tuple-element.546, pred[]{:T(512)S(6)} %compare.3, pred[]{:T(512)S(6)} %and.21), kind=kLoop, calls=%fused_computation.2.clone.1 | loop fusion | flops 18874368 | bytes 56623104 | tf_op jit(solution)/shard_map/while/body/eval_jaxpr/add | solution.py:119
  194.0 9.0 %collective-permute-done = bf16[64,9216]{1,0:T(8,128)(2,1)S(1)} collective-permute-done((bf16[64,9216]{1,0:T(8,128)(2,1)}, bf16[64,9216]{1,0:T(8,128)(2,1)S(1)}, u32[]{:S(2)}, u32[]{:S(2)}) %collective-permute-start) | collective-permute-done | bytes 1179680 | tf_op jit(solution)/shard_map/while/body/eval_jaxpr/ppermute | solution.py:14
  204.4 1.7 dynamic-slice_select_fusion.2
  206.1 3.4 fusion.53
  210.2 1.7 fusion.54
  211.9 2.0 select_dynamic-update-slice_fusion.2
  218.1 2.7 fusion.57
  220.8 15.6 %fusion.58 = f32[9216,512]{0,1:T(8,128)} fusion(f32[9216,256]{0,1:T(8,128)S(1)} %fusion.56, f32[9216,256]{0,1:T(8,128)S(1)} %fusion.57, f32[9216,512]{0,1:T(8,128)} %get-tuple-element.546, pred[]{:T(512)S(6)} %compare.3, pred[]{:T(512)S(6)} %and.21), kind=kLoop, calls=%fused_computation.2.clone.1 | loop fusion | flops 18874368 | bytes 56623104 | tf_op jit(solution)/shard_map/while/body/eval_jaxpr/add | solution.py:119
  236.4 8.3 %collective-permute-done = bf16[64,9216]{1,0:T(8,128)(2,1)S(1)} collective-permute-done((bf16[64,9216]{1,0:T(8,128)(2,1)}, bf16[64,9216]{1,0:T(8,128)(2,1)S(1)}, u32[]{:S(2)}, u32[]{:S(2)}) %collective-permute-start) | collective-permute-done | bytes 1179680 | tf_op jit(solution)/shard_map/while/body/eval_jaxpr/ppermute | solution.py:14
  246.1 1.7 dynamic-slice_select_fusion.2
  247.8 3.4 fusion.53
  251.9 1.7 fusion.54
  253.6 2.0 select_dynamic-update-slice_fusion.2
  259.8 2.7 fusion.57
  262.5 15.6 %fusion.58 = f32[9216,512]{0,1:T(8,128)} fusion(f32[9216,256]{0,1:T(8,128)S(1)} %fusion.56, f32[9216,256]{0,1:T(8,128)S(1)} %fusion.57, f32[9216,512]{0,1:T(8,128)} %get-tuple-element.546, pred[]{:T(512)S(6)} %compare.3, pred[]{:T(512)S(6)} %and.21), kind=kLoop, calls=%fused_computation.2.clone.1 | loop fusion | flops 18874368 | bytes 56623104 | tf_op jit(solution)/shard_map/while/body/eval_jaxpr/add | solution.py:119
  278.1 7.4 %collective-permute-done = bf16[64,9216]{1,0:T(8,128)(2,1)S(1)} collective-permute-done((bf16[64,9216]{1,0:T(8,128)(2,1)}, bf16[64,9216]{1,0:T(8,128)(2,1)S(1)}, u32[]{:S(2)}, u32[]{:S(2)}) %collective-permute-start) | collective-permute-done | bytes 1179680 | tf_op jit(solution)/shard_map/while/body/eval_jaxpr/ppermute | solution.py:14
  286.9 1.7 dynamic-slice_select_fusion.2
  288.6 3.4 fusion.53
  292.7 1.7 fusion.54
  294.4 2.0 select_dynamic-update-slice_fusion.2
  300.6 2.7 fusion.57
  303.3 15.6 %fusion.58 = f32[9216,512]{0,1:T(8,128)} fusion(f32[9216,256]{0,1:T(8,128)S(1)} %fusion.56, f32[9216,256]{0,1:T(8,128)S(1)} %fusion.57, f32[9216,512]{0,1:T(8,128)} %get-tuple-element.546, pred[]{:T(512)S(6)} %compare.3, pred[]{:T(512)S(6)} %and.21), kind=kLoop, calls=%fused_computation.2.clone.1 | loop fusion | flops 18874368 | bytes 56623104 | tf_op jit(solution)/shard_map/while/body/eval_jaxpr/add | solution.py:119
  318.9 6.5 %collective-permute-done = bf16[64,9216]{1,0:T(8,128)(2,1)S(1)} collective-permute-done((bf16[64,9216]{1,0:T(8,128)(2,1)}, bf16[64,9216]{1,0:T(8,128)(2,1)S(1)}, u32[]{:S(2)}, u32[]{:S(2)}) %collective-permute-start) | collective-permute-done | bytes 1179680 | tf_op jit(solution)/shard_map/while/body/eval_jaxpr/ppermute | solution.py:14
  325.4 18.7 %copy.11 = f32[9216,512]{1,0:T(8,128)} copy(f32[9216,512]{0,1:T(8,128)} %get-tuple-element.326) | data formatting | bytes 37748736 | tf_op jit(solution)/shard_map/while | solution.py:128
  344.1 12.1 %multiply_convert_fusion = bf16[9216,512]{1,0:T(8,128)(2,1)} fusion(f32[9216,512]{1,0:T(8,128)} %copy.11), kind=kLoop, calls=%fused_computation.20 | loop fusion | flops 9437184 | bytes 28311552 | tf_op jit(solution)/shard_map/convert_element_type | solution.py:133
  356.2 98.7 %reduce-scatter.2.cloned.1.call-done = bf16[1152,512]{1,0:T(8,128)(2,1)} async-done(((bf16[9216,512]{1,0:T(8,128)(2,1)}), bf16[1152,512]{1,0:T(8,128)(2,1)}) %reduce-scatter.2.cloned.1.call-update) | async-done | bytes 1179664 | tf_op jit(solution)/shard_map/reduce_scatter | solution.py:132
  454.9 3.0 bitcast_convert_fusion
  (131 shorter events, 34.0 us)
Async XLA Ops:
  7.2 3.0 copy-start
  7.2 56.9 %all-gather.7.cloned.1.call-start = ((), (), s32[]{:S(2)}) async-start(), calls=%async_computation.3 | async-start | bytes 5308416 | tf_op jit(solution)/shard_map/all_gather | solution.py:79
  7.9 108.4 %all-gather.5.cloned.1.call-start = ((), (), s32[]{:S(2)}) async-start(), calls=%async_computation.2 | async-start | bytes 5308416 | tf_op jit(solution)/shard_map/all_gather | solution.py:80
  8.7 446.3 %reduce-scatter.2.cloned.1.call-start = ((), (), s32[]{:S(2)}) async-start(), calls=%async_computation.1 | async-start | bytes 10616832 | tf_op jit(solution)/shard_map/reduce_scatter | solution.py:132
  10.1 2.1 copy-start.13
  10.2 2.1 copy-start.12
  118.1 1.4 copy-start.4
  119.5 5.1 %copy-start.3 = (f32[128,9216]{1,0:T(8,128)S(1)}, f32[128,9216]{1,0:T(8,128)}, u32[]{:S(2)}) copy-start(f32[128,9216]{1,0:T(8,128)} %get-tuple-element.575) | copy-start | bytes 14155780 | tf_op jit(solution)/shard_map/while
  121.2 4.1 copy-start.2
  121.2 4.1 copy-start.9
  125.3 1.7 copy-start.6
  127.0 4.7 %copy-start.10 = (bf16[128,256]{1,0:T(8,128)(2,1)S(1)}, bf16[128,256]{1,0:T(8,128)(2,1)}, u32[]{:S(2)}) copy-start(bf16[128,256]{1,0:T(8,128)(2,1)} %get-tuple-element.577) | copy-start | bytes 196612 | tf_op jit(solution)/shard_map/while
  129.0 1.4 copy-start.7
  130.4 30.2 %collective-permute-start = (bf16[64,9216]{1,0:T(8,128)(2,1)}, bf16[64,9216]{1,0:T(8,128)(2,1)S(1)}, u32[]{:S(2)}, u32[]{:S(2)}) collective-permute-start(bf16[64,9216]{1,0:T(8,128)(2,1)} %get-tuple-element.521), channel_id=1, source_target_pairs={{8,0},{16,8},{24,16},{9,1},{17,9},{25,17},{10,2},{18,10},{26,18},{... | collective-permute-start | bytes 3538952 | tf_op jit(solution)/shard_map/while/body/eval_jaxpr/ppermute | solution.py:14
  135.8 24.8 %copy-start.5 = (bf16[128,9216]{1,0:T(8,128)(2,1)S(1)}, bf16[128,9216]{1,0:T(8,128)(2,1)}, u32[]{:S(2)}) copy-start(bf16[128,9216]{1,0:T(8,128)(2,1)} %copy-done.4) | copy-start | bytes 7077892 | tf_op jit(solution)/shard_map/while
  160.6 1.4 copy-start.4
  162.0 5.1 %copy-start.3 = (f32[128,9216]{1,0:T(8,128)S(1)}, f32[128,9216]{1,0:T(8,128)}, u32[]{:S(2)}) copy-start(f32[128,9216]{1,0:T(8,128)} %get-tuple-element.575) | copy-start | bytes 14155780 | tf_op jit(solution)/shard_map/while
  163.7 4.1 copy-start.2
  163.7 4.1 copy-start.9
  167.8 1.7 copy-start.6
  169.5 4.7 %copy-start.10 = (bf16[128,256]{1,0:T(8,128)(2,1)S(1)}, bf16[128,256]{1,0:T(8,128)(2,1)}, u32[]{:S(2)}) copy-start(bf16[128,256]{1,0:T(8,128)(2,1)} %get-tuple-element.577) | copy-start | bytes 196612 | tf_op jit(solution)/shard_map/while
  173.0 30.0 %collective-permute-start = (bf16[64,9216]{1,0:T(8,128)(2,1)}, bf16[64,9216]{1,0:T(8,128)(2,1)S(1)}, u32[]{:S(2)}, u32[]{:S(2)}) collective-permute-start(bf16[64,9216]{1,0:T(8,128)(2,1)} %get-tuple-element.521), channel_id=1, source_target_pairs={{8,0},{16,8},{24,16},{9,1},{17,9},{25,17},{10,2},{18,10},{26,18},{... | collective-permute-start | bytes 3538952 | tf_op jit(solution)/shard_map/while/body/eval_jaxpr/ppermute | solution.py:14
  178.4 24.6 %copy-start.5 = (bf16[128,9216]{1,0:T(8,128)(2,1)S(1)}, bf16[128,9216]{1,0:T(8,128)(2,1)}, u32[]{:S(2)}) copy-start(bf16[128,9216]{1,0:T(8,128)(2,1)} %copy-done.4) | copy-start | bytes 7077892 | tf_op jit(solution)/shard_map/while
  203.0 1.4 copy-start.4
  204.4 5.1 %copy-start.3 = (f32[128,9216]{1,0:T(8,128)S(1)}, f32[128,9216]{1,0:T(8,128)}, u32[]{:S(2)}) copy-start(f32[128,9216]{1,0:T(8,128)} %get-tuple-element.575) | copy-start | bytes 14155780 | tf_op jit(solution)/shard_map/while
  206.1 4.1 copy-start.2
  206.1 4.1 copy-start.9
  210.2 1.7 copy-start.6
  211.9 4.7 %copy-start.10 = (bf16[128,256]{1,0:T(8,128)(2,1)S(1)}, bf16[128,256]{1,0:T(8,128)(2,1)}, u32[]{:S(2)}) copy-start(bf16[128,256]{1,0:T(8,128)(2,1)} %get-tuple-element.577) | copy-start | bytes 196612 | tf_op jit(solution)/shard_map/while
  215.3 29.4 %collective-permute-start = (bf16[64,9216]{1,0:T(8,128)(2,1)}, bf16[64,9216]{1,0:T(8,128)(2,1)S(1)}, u32[]{:S(2)}, u32[]{:S(2)}) collective-permute-start(bf16[64,9216]{1,0:T(8,128)(2,1)} %get-tuple-element.521), channel_id=1, source_target_pairs={{8,0},{16,8},{24,16},{9,1},{17,9},{25,17},{10,2},{18,10},{26,18},{... | collective-permute-start | bytes 3538952 | tf_op jit(solution)/shard_map/while/body/eval_jaxpr/ppermute | solution.py:14
  220.8 23.9 %copy-start.5 = (bf16[128,9216]{1,0:T(8,128)(2,1)S(1)}, bf16[128,9216]{1,0:T(8,128)(2,1)}, u32[]{:S(2)}) copy-start(bf16[128,9216]{1,0:T(8,128)(2,1)} %copy-done.4) | copy-start | bytes 7077892 | tf_op jit(solution)/shard_map/while
  244.7 1.4 copy-start.4
  246.1 5.1 %copy-start.3 = (f32[128,9216]{1,0:T(8,128)S(1)}, f32[128,9216]{1,0:T(8,128)}, u32[]{:S(2)}) copy-start(f32[128,9216]{1,0:T(8,128)} %get-tuple-element.575) | copy-start | bytes 14155780 | tf_op jit(solution)/shard_map/while
  247.8 4.1 copy-start.2
  247.8 4.1 copy-start.9
  251.9 1.7 copy-start.6
  253.6 4.7 %copy-start.10 = (bf16[128,256]{1,0:T(8,128)(2,1)S(1)}, bf16[128,256]{1,0:T(8,128)(2,1)}, u32[]{:S(2)}) copy-start(bf16[128,256]{1,0:T(8,128)(2,1)} %get-tuple-element.577) | copy-start | bytes 196612 | tf_op jit(solution)/shard_map/while
  257.1 28.4 %collective-permute-start = (bf16[64,9216]{1,0:T(8,128)(2,1)}, bf16[64,9216]{1,0:T(8,128)(2,1)S(1)}, u32[]{:S(2)}, u32[]{:S(2)}) collective-permute-start(bf16[64,9216]{1,0:T(8,128)(2,1)} %get-tuple-element.521), channel_id=1, source_target_pairs={{8,0},{16,8},{24,16},{9,1},{17,9},{25,17},{10,2},{18,10},{26,18},{... | collective-permute-start | bytes 3538952 | tf_op jit(solution)/shard_map/while/body/eval_jaxpr/ppermute | solution.py:14
  262.5 23.0 %copy-start.5 = (bf16[128,9216]{1,0:T(8,128)(2,1)S(1)}, bf16[128,9216]{1,0:T(8,128)(2,1)}, u32[]{:S(2)}) copy-start(bf16[128,9216]{1,0:T(8,128)(2,1)} %copy-done.4) | copy-start | bytes 7077892 | tf_op jit(solution)/shard_map/while
  285.5 1.4 copy-start.4
  286.9 5.1 %copy-start.3 = (f32[128,9216]{1,0:T(8,128)S(1)}, f32[128,9216]{1,0:T(8,128)}, u32[]{:S(2)}) copy-start(f32[128,9216]{1,0:T(8,128)} %get-tuple-element.575) | copy-start | bytes 14155780 | tf_op jit(solution)/shard_map/while
  288.6 4.1 copy-start.2
  288.6 4.1 copy-start.9
  292.7 1.7 copy-start.6
  294.4 4.7 %copy-start.10 = (bf16[128,256]{1,0:T(8,128)(2,1)S(1)}, bf16[128,256]{1,0:T(8,128)(2,1)}, u32[]{:S(2)}) copy-start(bf16[128,256]{1,0:T(8,128)(2,1)} %get-tuple-element.577) | copy-start | bytes 196612 | tf_op jit(solution)/shard_map/while
  297.9 27.5 %collective-permute-start = (bf16[64,9216]{1,0:T(8,128)(2,1)}, bf16[64,9216]{1,0:T(8,128)(2,1)S(1)}, u32[]{:S(2)}, u32[]{:S(2)}) collective-permute-start(bf16[64,9216]{1,0:T(8,128)(2,1)} %get-tuple-element.521), channel_id=1, source_target_pairs={{8,0},{16,8},{24,16},{9,1},{17,9},{25,17},{10,2},{18,10},{26,18},{... | collective-permute-start | bytes 3538952 | tf_op jit(solution)/shard_map/while/body/eval_jaxpr/ppermute | solution.py:14
  303.3 22.1 %copy-start.5 = (bf16[128,9216]{1,0:T(8,128)(2,1)S(1)}, bf16[128,9216]{1,0:T(8,128)(2,1)}, u32[]{:S(2)}) copy-start(bf16[128,9216]{1,0:T(8,128)(2,1)} %copy-done.4) | copy-start | bytes 7077892 | tf_op jit(solution)/shard_map/while
  356.2 101.7 %copy-start.1 = (bf16[1,2,64,9216]{3,2,1,0:T(8,128)(2,1)S(1)}, bf16[1,2,64,9216]{3,2,1,0:T(8,128)(2,1)}, u32[]{:S(2)}) copy-start(bf16[1,2,64,9216]{3,2,1,0:T(8,128)(2,1)} %param.11) | copy-start | bytes 7077892
  (6 other events, 8.1 us)
Sparse Core Ops, SparseCore 0:
  9.7 54.4 all-gather.6
  65.8 50.5 all-gather.4
  356.3 98.5 reduce-scatter.1
where the time goes:
time: 466 us; the launch traced here: 464 us
  waiting for transfers between devices  235 us (50%)
  other arithmetic  118 us (25%)
  matrix products  49.7 us (11%)
  local copies, waits for them, and re-layouts  41.3 us (9%)
  between operations  13.8 us (3%)
  starting transfers between devices  6.51 us (1%)
    reduce_scatter x1, waiting for transfers between devices, per_device(): lax.psum_scatter((carry[2] / float(tok_count)).astype(jnp.bfloat16), 'rep...  98.7 us
    add x5, other arithmetic, advance(): running = running + jnp.where(active, terms, 0.0)  70.6 us
    all_gather x1, waiting for transfers between devices, per_device(): lax.all_gather(up_weight[0], 'rep', axis=0, tiled=True)  48.4 us
    ppermute x5, waiting for transfers between devices, from_behind(): lax.ppermute(value, axis, [(source, source + steps) for source in range(l...  47.8 us
    all_gather x1, waiting for transfers between devices, per_device(): lax.all_gather(down_weight[0], 'rep', axis=0, tiled=True)  38.4 us
    dot_general x10, matrix products, contract_rows(): lax.dot_general(left, right, (((0,), (0,)), ((), ())), preferred_element_...  20.6 us
    while x1, local copies, waits for them, and re-layouts, per_device(): lax.fori_loop(0, tick_count, advance, (start_in, start_out, start_sum, st...  18.7 us
    while x80, local copies, waits for them, and re-layouts  17.2 us
  transfers between devices with their start and end apart: 8, of which 8 were waited for; matrix products, arithmetic and copies ran while one was open for 24% of the time, Pallas kernels for 0%

commit v1 on v0

--- a/solution.py
+++ b/solution.py
@@ -1,6 +1,10 @@
+import functools
+
 import jax
 import jax.numpy as jnp
 from jax import lax
+from jax.experimental import pallas as pl
+from jax.experimental.pallas import tpu as pltpu
 from jax.sharding import PartitionSpec as P
 
 EPSILON = 1e-05
@@ -70,7 +74,7 @@
     return lax.dynamic_update_slice_in_dim(target, jnp.where(active, values, older), begin, 0)
 
 
-def per_device(
+def plain_device(
     history, codes, scales, sample_ids, cotangent, ln_gain, ln_bias, down_weight, up_weight
 ):
     sections = lax.axis_size("section")
@@ -135,21 +139,633 @@
     return (produced.reshape(1, row_total // tok_count, tok_count, model_width), summed[None])
 
 
+VMEM_LIMIT = 16 * 1024 * 1024
+F32 = jnp.float32
+BF16 = jnp.bfloat16
+
+
+def run_kernel(body, outs, args, grid=(1,), scalars=(), scratch=(), aliases=None, limit=VMEM_LIMIT):
+    def whole(shape):
+        return pl.BlockSpec(shape, lambda *_: (0,) * len(shape))
+
+    arrays, in_specs, out_specs, out_shapes = [], [], [], []
+    for arg in args:
+        if isinstance(arg, tuple) and arg[1] is None:
+            arrays.append(arg[0])
+            in_specs.append(pl.BlockSpec(memory_space=pltpu.HBM))
+        elif isinstance(arg, tuple):
+            arrays.append(arg[0])
+            in_specs.append(pl.BlockSpec(arg[1], arg[2]))
+        else:
+            arrays.append(arg)
+            in_specs.append(whole(arg.shape))
+    for out in outs:
+        out_shapes.append(jax.ShapeDtypeStruct(out[0], out[1]))
+        out_specs.append(pl.BlockSpec(out[2], out[3]) if len(out) > 2 else whole(out[0]))
+    return pl.pallas_call(
+        body,
+        out_shape=out_shapes,
+        grid_spec=pltpu.PrefetchScalarGridSpec(
+            num_scalar_prefetch=len(scalars),
+            grid=grid,
+            in_specs=in_specs,
+            out_specs=out_specs,
+            scratch_shapes=list(scratch),
+        ),
+        input_output_aliases=aliases or {},
+        compiler_params=pltpu.CompilerParams(vmem_limit_bytes=limit),
+        cost_estimate=pl.CostEstimate(flops=0, bytes_accessed=0, transcendentals=0),
+    )(*scalars, *arrays)
+
+
+def regroup_body(
+    blocks, picks, hist0, hist1, code0, code1, cot0, cot1, step, own, sent, stats, kept, *, micro, tok
+):
+    place = pl.program_id(0)
+    last = pl.num_programs(0) - 1
+
+    @pl.when(place < last)
+    def _():
+        for which, (hist, code, cot, out) in enumerate(
+            ((hist0, code0, cot0, own), (hist1, code1, cot1, sent))
+        ):
+            for m in range(micro):
+                rows = pl.ds(m * tok, tok)
+                rebuilt = hist[picks[m]].astype(F32) + step[m] * code[m].astype(F32)
+                rebuilt = rebuilt.astype(BF16)
+                out[0, rows, :] = rebuilt
+                out[1, rows, :] = cot[m]
+                kept[2 * place + which, rows, :] = rebuilt
+
+    @pl.when(place == last)
+    def _():
+        total, rows, lanes = kept.shape
+        width = total * lanes
+
+        def add(index, acc):
+            return acc + jnp.sum(kept[index].astype(F32), axis=-1, keepdims=True)
+
+        mean = lax.fori_loop(0, total, add, jnp.zeros((rows, 1), F32)) / width
+
+        def add_square(index, acc):
+            centred = kept[index].astype(F32) - mean
+            return acc + jnp.sum(centred * centred, axis=-1, keepdims=True)
+
+        var = lax.fori_loop(0, total, add_square, jnp.zeros((rows, 1), F32)) / width
+        inv_std = lax.rsqrt(var + EPSILON)
+        half = stats.shape[1] // 2
+        stats[:, :half] = jnp.broadcast_to(mean, (rows, half))
+        stats[:, half:] = jnp.broadcast_to(inv_std, (rows, half))
+        lane = lax.broadcasted_iota(jnp.int32, (rows, 128), 1)
+        packed = jnp.zeros((rows, 128), F32)
+        for index, value in enumerate(bf16_parts(mean) + bf16_parts(inv_std)):
+            packed = jnp.where(lane == index, value, packed)
+        sent[0, :, :128] = packed.astype(BF16)
+
+
+def bf16_parts(value):
+    parts = []
+    for _ in range(3):
+        parts.append(value.astype(BF16).astype(F32))
+        value = value - parts[-1]
+    return parts
+
+
+def split_stats(stats):
+    if len(stats.shape) == 3:
+        parts = stats[0].astype(F32)
+        return [sum(parts[:, i : i + 1] for i in range(k, k + 3)) for k in (0, 3)]
+    half = stats.shape[1] // 2
+    return stats[:, 0:1], stats[:, half : half + 1]
+
+
+def norm_body(blocks, own, sib, stats_own, stats_sib, gain, bias, out):
+    tokens = own.shape[1]
+    for slot, (values, stats) in enumerate(((own, stats_own), (sib, stats_sib))):
+        mean, inv_std = split_stats(stats)
+        scaled = (values[0].astype(F32) - mean) * inv_std
+        out[slot * tokens : (slot + 1) * tokens, :] = (scaled * gain[...] + bias[...]).astype(BF16)
+
+
+def as_column(row, lanes):
+    turned = jnp.transpose(jnp.broadcast_to(row, (128, row.shape[1])))
+    return jnp.concatenate([turned] * (lanes // 128), axis=1)
+
+
+def step_body(*refs, first, sections):
+    refs = refs[1:]
+    own, sib, stats_own, stats_sib, gain, bias, down, up, near, far, diag_a, diag_b = refs[:12]
+    refs = refs[12:]
+    if first:
+        old = None
+        outs = refs
+    else:
+        old, outs = refs[:3], refs[3:]
+    rank = down.shape[1]
+    tokens = own.shape[1]
+    weights = down[...]
+    gain_row, bias_row = gain[...], bias[...]
+    others = [near[...], far[...], jnp.concatenate([diag_a[...], diag_b[...]], axis=0)]
+    for slot, (values, stats) in enumerate(((own, stats_own), (sib, stats_sib))):
+        mean, inv_std = split_stats(stats)
+        inputs = values[0]
+        scaled = (inputs.astype(F32) - mean) * inv_std
+        normed = (scaled * gain_row + bias_row).astype(BF16)
+        pieces = [
+            jnp.dot(values[1], up[...], preferred_element_type=F32),
+            jnp.dot(normed, weights, preferred_element_type=F32),
+        ] + [jnp.dot(inputs, other, preferred_element_type=F32) for other in others]
+        for index, piece in enumerate(pieces):
+            columns = slice(index * rank, (index + 1) * rank)
+            if old is not None:
+                piece = piece + old[slot][:, columns]
+            outs[slot][:, columns] = piece
+    wide = weights.astype(F32)
+    gained = wide * as_column(gain_row, rank)
+    biased = wide * as_column(bias_row, rank)
+    gained_low = gained.astype(BF16)
+    cross = outs[2]
+
+    def put(rows, columns, value):
+        if old is not None:
+            value = value + old[2][rows, columns]
+        cross[rows, columns] = value
+
+    for index, other in enumerate(others):
+        columns = slice(index * rank, (index + 1) * rank)
+        put(slice(0, rank), columns, contract_rows(gained_low, other))
+        put(
+            slice(rank, rank + 1),
+            columns,
+            jnp.sum(other.astype(F32), axis=0, keepdims=True),
+        )
+    put(slice(rank + 1, rank + 2), slice(0, rank), jnp.sum(gained, axis=0, keepdims=True))
+    put(slice(rank + 1, rank + 2), slice(rank, 2 * rank), jnp.sum(biased, axis=0, keepdims=True))
+
+
+def chain_values(pre, slopes, centred, spread, cross, kappa, inv_std, width):
+    act_grad = (pre * slopes).astype(BF16)
+    wide = act_grad.astype(F32)
+    second = jnp.sum(wide * centred, axis=-1, keepdims=True) / width
+    return inv_std * (jnp.dot(act_grad, cross, preferred_element_type=F32) - second * spread)
+
+
+def open_body(
+    mine, got, cross, cross_got, stats, small, shared, spread_out, cross_out, kappa_out, near, rest, *, width
+):
+    rank = near.shape[1]
+    total = mine[...] + got[...]
+    both = cross[...] + cross_got[...]
+    mean, inv_std = split_stats(stats)
+    base = total[:, :rank]
+    preact = total[:, rank : 2 * rank]
+    sums = both[rank : rank + 1, :]
+    kappa = both[rank + 1 : rank + 2, :rank]
+    beta = both[rank + 1 : rank + 2, rank : 2 * rank]
+    activated, slopes = gelu_pair(preact)
+    centred = preact - beta
+    spread = inv_std * (total[:, 2 * rank :] - mean * sums)
+    kappa_column = as_column(kappa, rank)[:, 0:1]
+    projected = (both[:rank, :] - kappa_column * (sums / width)).astype(BF16)
+    small[:, :rank] = base
+    small[:, rank:] = slopes
+    shared[:, :rank] = activated
+    shared[:, rank:] = centred
+    spread_out[...] = spread
+    cross_out[...] = projected
+    kappa_out[...] = jnp.broadcast_to(kappa, kappa_out.shape)
+    values = chain_values(base, slopes, centred, spread, projected, kappa, inv_std, width)
+    near[...] = values[:, :rank].astype(BF16)
+    rest[...] = values[:, rank:].astype(BF16)
+
+
+def chain_body(*refs, width, turn):
+    small, shared, spread, cross, kappa, stats = refs[:6]
+    arrivals, out = refs[6:-1], refs[-1]
+    rank = cross.shape[0]
+    _, inv_std = split_stats(stats)
+    pre = small[:, :rank]
+    for arrival in arrivals:
+        pre = pre + arrival[:, :rank].astype(F32)
+    slopes = small[:, rank:]
+    if turn == 3:
+        out[...] = (pre * slopes).astype(BF16)
+        return
+    values = chain_values(
+        pre, slopes, shared[:, rank:], spread[...], cross[...], kappa[0:1, :], inv_std, width
+    )
+    if turn == 1:
+        out[:, :rank] = values[:, 2 * rank :].astype(BF16)
+        out[:, rank:] = values[:, rank : 2 * rank].astype(BF16)
+        return
+    passed = arrivals[1][:, rank:].astype(F32) + arrivals[2][:, rank:].astype(F32)
+    out[...] = (values[:, :rank] + passed).astype(BF16)
+
+
+def grad_body(*refs, scale, width, index):
+    *refs, held, sems = refs
+    columns = pl.ds(index * held.shape[2], held.shape[2])
+    copies = [
+        pltpu.make_async_copy(source.at[0, :, columns], held.at[slot], sems.at[slot])
+        for slot, source in enumerate(refs[1:3])
+    ]
+    for copy in copies:
+        copy.start()
+    stats_own, stats_sib, act_own, act_sib, shared_own, shared_sib, kappa = refs[3:10]
+    gain, bias, down, term, *grads = refs[10:]
+    gain_row, bias_row = gain[...], bias[...]
+    weights = down[...]
+    rank = weights.shape[1]
+    total = None
+    for slot, (stats, act, shared) in enumerate(
+        ((stats_own, act_own, shared_own), (stats_sib, act_sib, shared_sib))
+    ):
+        mean, inv_std = split_stats(stats)
+        act_grad = act[...]
+        wide = act_grad.astype(F32)
+        first = jnp.sum(wide * kappa[0:1, :], axis=-1, keepdims=True) / width
+        second = jnp.sum(wide * shared[:, rank:], axis=-1, keepdims=True) / width
+        copies[slot].wait()
+        scaled = (held[slot].astype(F32) - mean) * inv_std
+        normed = (scaled * gain_row + bias_row).astype(BF16)
+        weighted = contract_cols(act_grad, weights) * gain_row
+        tokens = act_grad.shape[0]
+        term[slot * tokens : (slot + 1) * tokens, :] = (
+            inv_std * (weighted - first - scaled * second)
+        ).astype(BF16)
+        piece = contract_rows(normed, act_grad)
+        total = piece if total is None else total + piece
+    for grad in grads:
+        grad[...] = (total * scale).astype(BF16)
+
+
+def ahead_body(normed, act, own, out, *, scale):
+    out[...] = own[...].astype(F32) + contract_rows(normed[...], act[...]) * scale
+
+
+def close_body(*refs, scale, count, index):
+    *refs, held, sems = refs
+    columns = pl.ds(index * held.shape[2], held.shape[2])
+    copies = [
+        pltpu.make_async_copy(source.at[1, :, columns], held.at[slot], sems.at[slot])
+        for slot, source in enumerate(refs[1:3])
+    ]
+    for copy in copies:
+        copy.start()
+    level, _, _, shared_own, shared_sib, term = refs[0:6]
+    arrivals = refs[6 : 6 + count]
+    mine, theirs, grad = refs[6 + count :]
+    rank = grad.shape[1]
+    total = None
+    for slot, (shared, out) in enumerate(((shared_own, mine), (shared_sib, theirs))):
+        tokens = shared.shape[0]
+        rows = slice(slot * tokens, (slot + 1) * tokens)
+        copies[slot].wait()
+        arrived = held[slot].astype(F32)
+        for place, arrival in enumerate(arrivals):
+            values = arrival[rows, :].astype(F32)
+            if place == 0:
+                values = jnp.where(level[0] % 2 == 0, values, 0.0)
+            arrived = arrived + values
+        out_grad = arrived.astype(BF16)
+        out[...] = (out_grad.astype(F32) + term[rows, :].astype(F32)).astype(BF16)
+        piece = contract_rows(out_grad, shared[:, :rank].astype(BF16))
+        total = piece if total is None else total + piece
+    grad[...] = (total * scale).astype(BF16)
+
+
+def place_body(blocks, *refs, count):
+    mines, arrived, out = refs[:count], refs[count], refs[-1]
+    place = pl.program_id(0)
+    for index, source in enumerate(mines):
+
+        @pl.when(place == index)
+        def _():
+            out[...] = source[...]
+
+    @pl.when(place >= count)
+    def _():
+        out[...] = arrived[...]
+
+
+def per_device(
+    history, codes, scales, sample_ids, cotangent, ln_gain, ln_bias, down_weight, up_weight
+):
+    sections = lax.axis_size("section")
+    reps = lax.axis_size("rep")
+    line = reps // 2
+    section = lax.axis_index("section")
+    rep = lax.axis_index("rep")
+    chip, core = rep // 2, rep % 2
+    _, micro, tok, width = history.shape
+    tokens = micro * tok
+    rows, rank = down_weight.shape[1:]
+
+    def sibling(value):
+        return lax.ppermute(value, "rep", [(r, r ^ 1) for r in range(reps)])
+
+    def along(value, steps=1):
+        return lax.ppermute(value, "rep", [(r, (r + 2 * steps) % reps) for r in range(reps)])
+
+    def flip(value, mask):
+        return lax.ppermute(value, "section", [(s, s ^ mask) for s in range(sections)])
+
+    def after(value, *first):
+        return lax.optimization_barrier((value, first))[0]
+
+    chips = (chip - jnp.arange(line, dtype=jnp.int32)) % line
+    blocks = jnp.concatenate([2 * chips + core, 2 * chips + 1 - core]).astype(jnp.int32)
+    gain, bias = ln_gain, ln_bias
+
+    ups, downs = [up_weight[0]], [down_weight[0]]
+    cut = rows // 2
+
+    def both(value):
+        return flip(value, 1), flip(value, 2)
+
+    def first_half(near, *first):
+        return flip(after(near, *first)[:cut], 2)
+
+    def second_half(far, *first):
+        return flip(after(far, *first)[cut:], 1)
+
+    nears = [both(ups[0])]
+    ups.append(along(ups[0]))
+
+    def columns(kind):
+        return lambda i, blk, ids: (0, 0, blk[kind * line + jnp.minimum(i, line - 1)])
+
+    own, sent, stats = run_kernel(
+        functools.partial(regroup_body, micro=micro, tok=tok),
+        [
+            (
+                (2, tokens, line * rows),
+                BF16,
+                (2, tokens, rows),
+                lambda i, *_: (0, 0, jnp.minimum(i, line - 1)),
+            ),
+            ((2, tokens, (line + 1) * rows), BF16, (2, tokens, rows), lambda i, *_: (0, 0, i)),
+            ((tokens, 256), F32),
+        ],
+        [
+            (value, (micro, tok, rows), columns(kind))
+            for value in (history[0], codes[0], cotangent)
+            for kind in (0, 1)
+        ]
+        + [scales[0][..., None]],
+        grid=(line + 1,),
+        scalars=(blocks, sample_ids[0]),
+        scratch=[pltpu.VMEM((2 * line, tokens, rows), BF16)],
+    )
+    sib = sibling(after(sent, *nears[0], ups[1]))
+    stats_sib = (sib, (1, tokens, 128), lambda i, *_: (0, 0, line * rows // 128))
+
+    ups.append(along(ups[1]))
+    downs.append(along(after(downs[0], ups[1])))
+    nears.append(both(ups[1]))
+    def part(value, index):
+        return (value, (2, tokens, rows), lambda i, *_: (0, 0, index))
+
+    def one(value, kind, index):
+        return (value, (1, tokens, rows), lambda i, *_: (kind, 0, index))
+
+    def feature(value, index):
+        return (value, (1, rows), lambda i, blk: (0, blk[index]))
+
+    def add_step(sums, index, gathered):
+        first = index == 0
+        args = [
+            part(own, index),
+            part(sib, index),
+            stats,
+            stats_sib,
+            feature(gain, index),
+            feature(bias, index),
+            downs[index],
+            ups[index],
+            *gathered,
+        ]
+        shapes = [
+            ((tokens, (1 + sections) * rank), F32),
+            ((tokens, (1 + sections) * rank), F32),
+            ((rank + 8, (sections - 1) * rank), F32),
+        ]
+        return run_kernel(
+            functools.partial(step_body, first=first, sections=sections),
+            shapes,
+            args + list(sums),
+            scalars=(blocks,),
+            aliases=None if first else {13 + i: i for i in range(3)},
+            limit=28 * 1024 * 1024,
+        )
+
+    firsts = [first_half(nears[0][0], *nears[1])]
+    ups.append(along(ups[2]))
+    downs.append(along(downs[1]))
+    nears.append(both(after(ups[2], *nears[1], sib)))
+    seconds = [second_half(nears[0][1], *nears[2])]
+    firsts.append(first_half(nears[1][0], *nears[2]))
+    seconds.append(second_half(nears[1][1], *nears[2]))
+    sums = add_step((), 0, nears[0] + (firsts[0], seconds[0]))
+    nears.append(both(after(ups[3], *nears[2], *firsts, *seconds, *sums)))
+    for index in range(2, line):
+        firsts.append(first_half(nears[index][0]))
+        seconds.append(second_half(nears[index][1]))
+    downs.append(along(downs[2]))
+    for index in range(1, line):
+        sums = add_step(sums, index, nears[index] + (firsts[index], seconds[index]))
+    mine, other, cross = sums
+    (normed,) = run_kernel(
+        norm_body,
+        [((2 * tokens, rows), BF16)],
+        [
+            one(own, 0, 1),
+            one(sib, 0, 1),
+            stats,
+            stats_sib,
+            feature(gain, 1),
+            feature(bias, 1),
+        ],
+        scalars=(blocks,),
+    )
+    normed_ahead = along(after(normed, mine), -1)
+
+    got, cross_got = sibling(other), sibling(cross)
+
+    apart = sections - 1
+    small, shared, spread, projected, kappa, to_next, to_rest = run_kernel(
+        functools.partial(open_body, width=width),
+        [
+            ((tokens, 2 * rank), F32),
+            ((tokens, 2 * rank), F32),
+            ((tokens, apart * rank), F32),
+            ((rank, apart * rank), BF16),
+            ((8, rank), F32),
+            ((tokens, rank), BF16),
+            ((tokens, 2 * rank), BF16),
+        ],
+        [mine, got, cross, cross_got, stats],
+    )
+    arrivals = [lax.ppermute(to_next, "section", [(3, 2)])]
+    late = lax.ppermute(to_rest, "section", [(3, 1)])
+    state = [small, shared, spread, projected, kappa, stats]
+    for turn in (1, 2, 3):
+        (passed,) = run_kernel(
+            functools.partial(chain_body, width=width, turn=turn),
+            [((tokens, 2 * rank if turn == 1 else rank), BF16)],
+            state + (after(arrivals, normed_ahead) if turn == 3 else arrivals),
+        )
+        if turn == 1:
+            arrivals += [late, lax.ppermute(passed, "section", [(2, 1)])]
+        elif turn == 2:
+            arrivals += [lax.ppermute(passed, "section", [(1, 0)])]
+    act = passed
+    act_sib, shared_sib = sibling(act), sibling(shared)
+
+    scale = 1.0 / tok
+    level = section.astype(jnp.int32).reshape(1)
+
+    def grad_block(index, act):
+        outs = [((2 * tokens, rows), BF16)]
+        if index != 1:
+            outs.append(((rows, rank), BF16))
+        return run_kernel(
+            functools.partial(grad_body, scale=scale, width=width, index=index),
+            outs,
+            [
+                (own, None),
+                (sib, None),
+                stats,
+                stats_sib,
+                act,
+                act_sib,
+                shared,
+                shared_sib,
+                kappa,
+                feature(gain, index),
+                feature(bias, index),
+                downs[index],
+            ],
+            scalars=(blocks,),
+            scratch=[pltpu.VMEM((2, tokens, rows), BF16), pltpu.SemaphoreType.DMA((2,))],
+        )
+
+    def close_block(index, arrived):
+        return run_kernel(
+            functools.partial(close_body, scale=scale, count=len(arrived), index=index),
+            [((tokens, rows), BF16), ((tokens, rows), BF16), ((rows, rank), BF16)],
+            [(own, None), (sib, None), shared, shared_sib, terms[index], *arrived],
+            scalars=(level,),
+            scratch=[pltpu.VMEM((2, tokens, rows), BF16), pltpu.SemaphoreType.DMA((2,))],
+        )
+
+    terms, down_grads, up_grads, mines, theirs = {}, {}, {}, {}, {}
+    (terms[1],) = grad_block(1, act)
+    act = after(act, terms[1])
+    for index in (2, 3):
+        terms[index], *down_grads[index] = grad_block(index, act)
+
+    def add(*values):
+        return sum(value.astype(F32) for value in values)
+
+    def pass_on(running, part):
+        return along(add(running, part).astype(BF16))
+
+    def scan_open(index):
+        return lax.ppermute(terms[index], "section", [(3, 2), (1, 0), (2, 3)])
+
+    def scan_pairs(*pairs):
+        return lax.ppermute(terms[1], "section", pairs)
+
+    def scan_sum(index, arrived):
+        return add(terms[index], arrived).astype(BF16)
+
+    def scan_more(value):
+        return lax.ppermute(value, "section", [(3, 1), (2, 0)])
+
+    opened = {1: scan_pairs((3, 2), (2, 3))}
+    beside = scan_pairs((1, 0))
+    opened.update({index: scan_open(index) for index in (2, 3)})
+    down_ring = along(down_grads[2][0])
+    sums = {1: scan_sum(1, after(opened[1], terms[2], terms[3]))}
+    more = {1: scan_more(sums[1])}
+    down_sum = add(after(down_ring, beside), down_grads[3][0]).astype(BF16)
+    down_ring = along(down_sum)
+    mines[1], theirs[1], up_grads[1] = close_block(
+        1, (opened[1], after(more[1], down_sum), beside)
+    )
+    up_ring = along(up_grads[1])
+    sums[2] = scan_sum(2, after(opened[2], up_grads[1]))
+    more[2] = scan_more(sums[2])
+    terms[0], *down_grads[0] = grad_block(0, after(act, up_grads[1]))
+    opened[0] = scan_open(0)
+    sums[3] = scan_sum(3, after(opened[3], sums[2]))
+    more[3] = scan_more(sums[3])
+    mines[2], theirs[2], up_grads[2] = close_block(
+        2, (opened[2], after(more[2], sums[3], down_ring))
+    )
+    more[0] = scan_more(scan_sum(0, after(opened[0], sums[3], up_grads[2])))
+    act_ahead = along(jnp.concatenate(after([act, act_sib], up_grads[2]), axis=0), -1)
+    mines[3], theirs[3], up_grads[3] = close_block(3, (opened[3], after(more[3], act_ahead)))
+    up_ring = pass_on(up_ring, up_grads[2])
+    up_sum = add(up_ring, up_grads[3]).astype(BF16)
+    up_ring = along(up_sum)
+    def place(first, count, produced):
+        sent = [theirs[index] for index in range(first, first + count)]
+        arrived = sibling(jnp.concatenate(sent, axis=1) if count > 1 else sent[0])
+        args = [mines[index] for index in range(first, first + count)]
+        args.append((arrived, (tokens, rows), lambda i, blk: (0, jnp.maximum(i - count, 0))))
+        if produced is not None:
+            args.append((produced, None))
+
+        def target(i, blk):
+            return (0, blk[first + jnp.where(i < count, i, line + i - count)])
+
+        return run_kernel(
+            functools.partial(place_body, count=count),
+            [((tokens, width), BF16, (tokens, rows), target)],
+            args,
+            grid=(2 * count,),
+            scalars=(blocks,),
+            aliases=None if produced is None else {len(args): 0},
+        )[0]
+
+    produced = place(1, line - 1, None)
+    mines[0], theirs[0], up_grads[0] = close_block(
+        0, (opened[0], after(more[0], up_ring, produced))
+    )
+    produced = place(0, 1, produced)
+    (down_own,) = run_kernel(
+        functools.partial(ahead_body, scale=scale),
+        [((rows, rank), F32)],
+        [normed_ahead, act_ahead, after(down_grads[0][0], mines[3])],
+    )
+    up_sum = add(up_ring, up_grads[0])
+    grads = jnp.concatenate([add(down_ring, down_own), up_sum], axis=1)
+    return produced.reshape(1, micro, tok, width), grads[None]
+
+
 def solution(mesh):
-    return jax.shard_map(
-        per_device,
-        mesh=mesh,
-        in_specs=(
-            P("section", "rep", None, None),
-            P("section", "rep", None, None),
-            P("section", "rep", None),
-            P("rep", None),
-            P("rep", None, None),
-            P("section", None),
-            P("section", None),
-            P("section", "rep", None),
-            P("section", "rep", None),
-        ),
-        out_specs=(P("section", "rep", None, None), P("section", "rep", None)),
-        check_vma=False,
-    )
+    def run(*args):
+        rows = args[7].shape[1] // mesh.shape["rep"]
+        split = mesh.shape["section"] == 4 and mesh.shape["rep"] == 8 and rows % 128 == 0
+        body = per_device if split else plain_device
+        return jax.shard_map(
+            body,
+            mesh=mesh,
+            in_specs=(
+                P("section", "rep", None, None),
+                P("section", "rep", None, None),
+                P("section", "rep", None),
+                P("rep", None),
+                P("rep", None, None),
+                P("section", None),
+                P("section", None),
+                P("section", "rep", None),
+                P("section", "rep", None),
+            ),
+            out_specs=(P("section", "rep", None, None), P("section", "rep", None)),
+            check_vma=False,
+        )(*args)
+
+    return run

time: 466 us -> 220 us (0.47)
  waiting for transfers between devices: 235 us -> 110 us
  other arithmetic: 118 us -> 8.17 us
  matrix products: 49.7 us -> 0 us
  starting transfers between devices: 6.51 us -> 47 us
  Pallas kernels: 0 us -> 39.6 us
  local copies, waits for them, and re-layouts: 41.3 us -> 12.3 us
  between operations: 13.8 us -> 1.37 us
    reduce_scatter x1 -> x0, waiting for transfers between devices: 98.7 us -> none  [per_device(): lax.psum_scatter((carry[2] / float(tok_count)).astype(jnp.bfloat16), 'rep...]
    all_gather x2 -> x0, waiting for transfers between devices: 86.8 us -> none  [the longest x1 48.4 us: per_device(): lax.all_gather(up_weight[0], 'rep', axis=0, tiled=True)]
    add x5 -> x2, other arithmetic: 70.6 us -> 0.31 us  [add(): return sum((value.astype(F32) for value in values))]
    ppermute x5 -> x49, waiting for transfers between devices: 47.8 us -> 110 us  [the longest x13 49 us: along(): lax.ppermute(value, 'rep', [(r, (r + 2 * steps) % reps) for r in range(re...]
    dot_general x21 -> x0, matrix products: 49.7 us -> none  [the longest x10 20.6 us: contract_rows(): lax.dot_general(left, right, (((0,), (0,)), ((), ())), preferred_element_...]
    ppermute x5 -> x49, starting transfers between devices: 6.4 us -> 47 us  [the longest x16 18.1 us: flip(): lax.ppermute(value, 'section', [(s, s ^ mask) for s in range(sections)])]
    pallas_call x0 -> x21, Pallas kernels: none -> 39.6 us  [run_kernel(): pl.pallas_call(body, out_shape=out_shapes, grid_spec=pltpu.PrefetchScalar...]
    while x81 -> x0, local copies, waits for them, and re-layouts: 36 us -> none  [the longest x1 18.7 us: per_device(): lax.fori_loop(0, tick_count, advance, (start_in, start_out, start_sum, st...]
  transfers between devices with their start and end apart: 8 -> 49, of which waited for: 8 -> 25; matrix products, arithmetic and copies ran while one was open for 24% -> 5% of each run, Pallas kernels for 0% -> 15%
where the time goes in v1:
time: 220 us; the launch traced here: 218 us
  waiting for transfers between devices  110 us (50%)
  starting transfers between devices  47 us (21%)
  Pallas kernels  39.6 us (18%)
  local copies, waits for them, and re-layouts  12.3 us (6%)
  other arithmetic  8.17 us (4%)
    ppermute x13, waiting for transfers between devices, along(): lax.ppermute(value, 'rep', [(r, (r + 2 * steps) % reps) for r in range(re...  49 us
    pallas_call x21, Pallas kernels, run_kernel(): pl.pallas_call(body, out_shape=out_shapes, grid_spec=pltpu.PrefetchScalar...  39.6 us
    ppermute x16, waiting for transfers between devices, flip(): lax.ppermute(value, 'section', [(s, s ^ mask) for s in range(sections)])  33 us
    ppermute x16, starting transfers between devices, flip(): lax.ppermute(value, 'section', [(s, s ^ mask) for s in range(sections)])  18.1 us
    ppermute x4, waiting for transfers between devices, scan_more(): return lax.ppermute(value, 'section', [(3, 1), (2, 0)])  16.3 us
    ppermute x13, starting transfers between devices, along(): lax.ppermute(value, 'rep', [(r, (r + 2 * steps) % reps) for r in range(re...  13.4 us
    unnamed x50, local copies, waits for them, and re-layouts  9.45 us
    ppermute x3, waiting for transfers between devices, scan_open(): return lax.ppermute(terms[index], 'section', [(3, 2), (1, 0), (2, 3)])  6.29 us
  transfers between devices with their start and end apart: 49, of which 25 were waited for; matrix products, arithmetic and copies ran while one was open for 5% of the time, Pallas kernels for 15%

profile of v1, /device:TPU:0, one launch (start us, length us, event | category | flops | bytes accessed | tf_op | source)
XLA Modules:
  0.0 218.4 jit_solution(4753716346879112432)
XLA Ops:
  0.6 3.1 %collective-permute-start.2 = (bf16[1152,256]{1,0:T(8,128)(2,1)}, bf16[1152,256]{1,0:T(8,128)(2,1)}, u32[]{:S(2)}, u32[]{:S(2)}) collective-permute-start(bf16[1152,256]{1,0:T(8,128)(2,1)} %bitcast.17), channel_id=1, source_target_pairs={{0,2},{1,3},{2,4},{3,5},{4,6},{5,7},{6,0},{7,1},{8,10},{9,11},{10,... | collective-permute-start | bytes 1769480 | tf_op jit(solution)/shard_map/ppermute | solution.py:468
  3.7 1.5 collective-permute-start
  5.2 1.5 collective-permute-start.1
  7.6 2.3 %copy-done.3 = s32[1,2,64,9216]{3,2,1,0:T(8,128)S(1)} copy-done((s32[1,2,64,9216]{3,2,1,0:T(8,128)S(1)}, s32[1,2,64,9216]{3,2,1,0:T(8,128)}, u32[]{:S(2)}) %copy-start.3) | copy-done | bytes 4718616
  9.9 1.7 copy-done.6
  11.6 1.7 copy-done.7
  13.9 5.7 %shard_map.104 = (bf16[2,128,4608]{2,1,0:T(8,128)(2,1)S(1)}, bf16[2,128,5760]{2,1,0:T(8,128)(2,1)S(1)}, f32[128,256]{1,0:T(8,128)S(1)}) custom-call(s32[8]{0:T(128)S(1)} %pad_add_fusion.blocks.refs_0_, s32[2]{0:T(128)S(1)} %bitcast.21, bf16[2,64,9216]{2,1,0:T(8,128)(2,1)S(1)} %bitcast.12, bf16[2,64,9216]{2,1,0:T(8,128)(2,1)S(1)} %bitcast.13, ...), custom_call_target="tpu_custom_call" | custom-call | tf_op jit(solution)/shard_map/pallas_call | solution.py:165
  21.8 1.4 collective-permute-start.9
  24.1 12.4 %collective-permute-done.10.refs_10_ = bf16[1152,256]{1,0:T(8,128)(2,1)S(1)} collective-permute-done((bf16[1152,256]{1,0:T(8,128)(2,1)}, bf16[1152,256]{1,0:T(8,128)(2,1)S(1)}, u32[]{:S(2)}, u32[]{:S(2)}) %collective-permute-start.10) | collective-permute-done | bytes 589856 | tf_op jit(solution)/shard_map/ppermute | solution.py:471
  37.4 3.0 %collective-permute-done.7.refs_8_ = bf16[1152,256]{1,0:T(8,128)(2,1)S(1)} collective-permute-done((bf16[1152,256]{1,0:T(8,128)(2,1)}, bf16[1152,256]{1,0:T(8,128)(2,1)S(1)}, u32[]{:S(2)}, u32[]{:S(2)}) %collective-permute-start.7) | collective-permute-done | bytes 589856 | tf_op jit(solution)/shard_map/ppermute | solution.py:468
  45.3 9.5 %collective-permute-done.11.refs_9_ = bf16[1152,256]{1,0:T(8,128)(2,1)S(1)} collective-permute-done((bf16[1152,256]{1,0:T(8,128)(2,1)S(1)}, bf16[1152,256]{1,0:T(8,128)(2,1)S(1)}, u32[]{:S(2)}, u32[]{:S(2)}) %collective-permute-start.11) | collective-permute-done | bytes 589856 | tf_op jit(solution)/shard_map/ppermute | solution.py:471
  54.7 2.5 %collective-permute-done.12.refs_10_ = bf16[1152,256]{1,0:T(8,128)(2,1)S(1)} collective-permute-done((bf16[1152,256]{1,0:T(8,128)(2,1)S(1)}, bf16[1152,256]{1,0:T(8,128)(2,1)S(1)}, u32[]{:S(2)}, u32[]{:S(2)}) %collective-permute-start.12) | collective-permute-done | bytes 589856 | tf_op jit(solution)/shard_map/ppermute | solution.py:471
  58.2 1.5 collective-permute-start.15
  61.3 2.2 %collective-permute-done.13.refs_11_ = bf16[576,256]{1,0:T(8,128)(2,1)S(1)} collective-permute-done((bf16[576,256]{1,0:T(8,128)(2,1)S(1)}, bf16[576,256]{1,0:T(8,128)(2,1)S(1)}, u32[]{:S(2)}, u32[]{:S(2)}) %collective-permute-start.13) | collective-permute-done | bytes 294944 | tf_op jit(solution)/shard_map/ppermute | solution.py:471
  63.6 2.5 %collective-permute-done.15.refs_12_ = bf16[576,256]{1,0:T(8,128)(2,1)S(1)} collective-permute-done((bf16[576,256]{1,0:T(8,128)(2,1)S(1)}, bf16[576,256]{1,0:T(8,128)(2,1)S(1)}, u32[]{:S(2)}, u32[]{:S(2)}) %collective-permute-start.15) | collective-permute-done | bytes 294944 | tf_op jit(solution)/shard_map/ppermute | solution.py:471
  66.1 3.5 %shard_map.105 = (f32[128,1280]{1,0:T(8,128)S(1)}, f32[128,1280]{1,0:T(8,128)S(1)}, f32[264,768]{1,0:T(8,128)S(1)}) custom-call(s32[8]{0:T(128)S(1)} %pad_add_fusion.blocks.refs_0_, bf16[2,128,4608]{2,1,0:T(8,128)(2,1)S(1)} %get-tuple-element.69.refs_1_.own, bf16[2,128,5760]{2,1,0:T(8,128)(2,1)S(1)} %collective-permute-done.3.refs_2_.refs_4_.sib.stats_sib, ...), custom_call_target="tpu_custom_call" | custom-call | tf_op jit(solution)/shard_map/pallas_call | solution.py:165
  69.6 3.0 %collective-permute-done.8.refs_8_ = bf16[1152,256]{1,0:T(8,128)(2,1)S(1)} collective-permute-done((bf16[1152,256]{1,0:T(8,128)(2,1)S(1)}, bf16[1152,256]{1,0:T(8,128)(2,1)S(1)}, u32[]{:S(2)}, u32[]{:S(2)}) %collective-permute-start.8) | collective-permute-done | bytes 589856 | tf_op jit(solution)/shard_map/ppermute | solution.py:468
  73.8 1.4 collective-permute-start.18
  75.2 7.5 %collective-permute-done.5.refs_7_.refs_12_ = bf16[1152,256]{1,0:T(8,128)(2,1)S(1)} collective-permute-done((bf16[1152,256]{1,0:T(8,128)(2,1)S(1)}, bf16[1152,256]{1,0:T(8,128)(2,1)S(1)}, u32[]{:S(2)}, u32[]{:S(2)}) %collective-permute-start.5) | collective-permute-done | bytes 589856 | tf_op jit(solution)/shard_map/ppermute | solution.py:468
  84.1 1.5 collective-permute-start.22
  87.1 3.7 %shard_map.106 = (f32[128,1280]{1,0:T(8,128)S(1)}, f32[128,1280]{1,0:T(8,128)S(1)}, f32[264,768]{1,0:T(8,128)S(1)}) custom-call(s32[8]{0:T(128)S(1)} %pad_add_fusion.blocks.refs_0_, bf16[2,128,4608]{2,1,0:T(8,128)(2,1)S(1)} %get-tuple-element.69.refs_1_.own, ...), custom_call_target="tpu_custom_call", output_to_operand_aliasing={{0}: (13, {}), {1}: (14, {}), {2}: (15, {})} | custom-call | tf_op jit(solution)/shard_map/pallas_call | solution.py:165
  90.9 1.9 collective-permute-done.21.refs_11_
  93.5 2.7 %shard_map.107 = (f32[128,1280]{1,0:T(8,128)S(1)}, f32[128,1280]{1,0:T(8,128)S(1)}, f32[264,768]{1,0:T(8,128)S(1)}) custom-call(s32[8]{0:T(128)S(1)} %pad_add_fusion.blocks.refs_0_, bf16[2,128,4608]{2,1,0:T(8,128)(2,1)S(1)} %get-tuple-element.69.refs_1_.own, ...), custom_call_target="tpu_custom_call", output_to_operand_aliasing={{0}: (13, {}), {1}: (14, {}), {2}: (15, {})} | custom-call | tf_op jit(solution)/shard_map/pallas_call | solution.py:165
  97.4 2.7 %shard_map.108 = (f32[128,1280]{1,0:T(8,128)S(1)}, f32[128,1280]{1,0:T(8,128)S(1)}, f32[264,768]{1,0:T(8,128)S(1)}) custom-call(s32[8]{0:T(128)S(1)} %pad_add_fusion.blocks.refs_0_, bf16[2,128,4608]{2,1,0:T(8,128)(2,1)S(1)} %get-tuple-element.69.refs_1_.own, ...), custom_call_target="tpu_custom_call", output_to_operand_aliasing={{0}: (13, {}), {1}: (14, {}), {2}: (15, {})} | custom-call | tf_op jit(solution)/shard_map/pallas_call | solution.py:165
  101.5 3.1 %collective-permute-start.30 = (bf16[256,1152]{1,0:T(8,128)(2,1)S(1)}, bf16[256,1152]{1,0:T(8,128)(2,1)S(1)}, u32[]{:S(2)}, u32[]{:S(2)}) collective-permute-start(bf16[256,1152]{1,0:T(8,128)(2,1)S(1)} %shard_map.112), channel_id=1, source_target_pairs={{0,6},{1,7},{2,0},{3,1},{4,2},{5,3},{6,4},{7,5},{8,14},{9,15},{10,... | collective-permute-start | bytes 1769480 | tf_op jit(solution)/shard_map/ppermute | solution.py:468
  108.9 8.6 %collective-permute-done.30.normed = bf16[256,1152]{1,0:T(8,128)(2,1)S(1)} collective-permute-done((bf16[256,1152]{1,0:T(8,128)(2,1)S(1)}, bf16[256,1152]{1,0:T(8,128)(2,1)S(1)}, u32[]{:S(2)}, u32[]{:S(2)}) %collective-permute-start.30) | collective-permute-done | bytes 589856 | tf_op jit(solution)/shard_map/ppermute | solution.py:468
  117.5 4.2 %collective-permute-done.29.refs_9_ = bf16[128,256]{1,0:T(8,128)(2,1)S(1)} collective-permute-done((bf16[128,256]{1,0:T(8,128)(2,1)S(1)}, bf16[128,256]{1,0:T(8,128)(2,1)S(1)}, u32[]{:S(2)}, u32[]{:S(2)}) %collective-permute-start.29) | collective-permute-done | bytes 65568 | tf_op jit(solution)/shard_map/ppermute | solution.py:621
  123.0 2.3 %shard_map.114.refs_5_ = bf16[256,1152]{1,0:T(8,128)(2,1)} custom-call(s32[8]{0:T(128)S(1)} %pad_add_fusion.blocks.refs_0_, bf16[2,128,4608]{2,1,0:T(8,128)(2,1)S(1)} %get-tuple-element.69.refs_1_.own, bf16[2,128,5760]{2,1,0:T(8,128)(2,1)S(1)} %collective-permute-done.3.refs_2_.refs_4_.sib.stats_sib, ...), custom_call_target="tpu_custom_call" | custom-call | tf_op jit(solution)/shard_map/pallas_call | solution.py:165
  127.4 2.7 %shard_map.115 = (bf16[256,1152]{1,0:T(8,128)(2,1)}, bf16[1152,256]{1,0:T(8,128)(2,1)}) custom-call(s32[8]{0:T(128)S(1)} %pad_add_fusion.blocks.refs_0_, bf16[2,128,4608]{2,1,0:T(8,128)(2,1)S(1)} %get-tuple-element.69.refs_1_.own, bf16[2,128,5760]{2,1,0:T(8,128)(2,1)S(1)} %collective-permute-done.3.refs_2_.refs_4_.sib.stats_sib, ...), custom_call_target="tpu_custom_call" | custom-call | tf_op jit(solution)/shard_map/pallas_call | solution.py:165
  130.2 1.9 shard_map.116
  132.2 2.5 %add_convert_fusion.6 = bf16[256,1152]{1,0:T(8,128)(2,1)} fusion(bf16[256,1152]{1,0:T(8,128)(2,1)S(1)} %collective-permute-done.32.refs_6_, bf16[256,1152]{1,0:T(8,128)(2,1)} %shard_map.114.refs_5_), kind=kLoop, calls=%fused_computation.9 | loop fusion | flops 1179648 | bytes 1769472 | tf_op jit(solution)/shard_map/convert_element_type | solution.py:681
  138.1 1.4 collective-permute-start.37
  139.5 8.2 %collective-permute-done.34 = bf16[1152,256]{1,0:T(8,128)(2,1)} collective-permute-done((bf16[1152,256]{1,0:T(8,128)(2,1)}, bf16[1152,256]{1,0:T(8,128)(2,1)}, u32[]{:S(2)}, u32[]{:S(2)}) %collective-permute-start.34) | collective-permute-done | bytes 589856 | tf_op jit(solution)/shard_map/ppermute | solution.py:468
  149.1 7.8 %collective-permute-done.33.refs_7_ = bf16[256,1152]{1,0:T(8,128)(2,1)} collective-permute-done((bf16[256,1152]{1,0:T(8,128)(2,1)}, bf16[256,1152]{1,0:T(8,128)(2,1)}, u32[]{:S(2)}, u32[]{:S(2)}) %collective-permute-start.33) | collective-permute-done | bytes 589856 | tf_op jit(solution)/shard_map/ppermute | solution.py:684
  156.9 1.7 copy-done.1
  158.6 2.3 %shard_map.117 = (bf16[128,1152]{1,0:T(8,128)(2,1)S(1)}, bf16[128,1152]{1,0:T(8,128)(2,1)S(1)}, bf16[1152,256]{1,0:T(8,128)(2,1)S(1)}) custom-call(s32[1]{0:T(128)} %bitcast.refs_0_, bf16[2,128,4608]{2,1,0:T(8,128)(2,1)S(1)} %copy-done.1, bf16[2,128,5760]{2,1,0:T(8,128)(2,1)S(1)} %collective-permute-done.3.refs_2_.refs_4_.sib.stats_sib, ...), custom_call_target="tpu_custom_call" | custom-call | tf_op jit(solution)/shard_map/pallas_call | solution.py:165
  160.9 1.5 add_convert_fusion.4
  162.5 1.4 collective-permute-start.39
  164.0 4.9 %collective-permute-done.37.refs_6_ = bf16[256,1152]{1,0:T(8,128)(2,1)S(1)} collective-permute-done((bf16[256,1152]{1,0:T(8,128)(2,1)}, bf16[256,1152]{1,0:T(8,128)(2,1)S(1)}, u32[]{:S(2)}, u32[]{:S(2)}) %collective-permute-start.37) | collective-permute-done | bytes 589856 | tf_op jit(solution)/shard_map/ppermute | solution.py:675
  170.3 1.9 shard_map.118
  173.6 7.2 %collective-permute-done.39.refs_7_ = bf16[256,1152]{1,0:T(8,128)(2,1)S(1)} collective-permute-done((bf16[256,1152]{1,0:T(8,128)(2,1)S(1)}, bf16[256,1152]{1,0:T(8,128)(2,1)S(1)}, u32[]{:S(2)}, u32[]{:S(2)}) %collective-permute-start.39) | collective-permute-done | bytes 589856 | tf_op jit(solution)/shard_map/ppermute | solution.py:684
  180.8 2.0 shard_map.119
  182.8 4.3 %collective-permute-start.45 = (bf16[256,256]{1,0:T(8,128)(2,1)S(1)}, bf16[256,256]{1,0:T(8,128)(2,1)S(1)}, u32[]{:S(2)}, u32[]{:S(2)}) collective-permute-start(bf16[256,256]{1,0:T(8,128)(2,1)S(1)} %pad_maximum_fusion.1), channel_id=1, source_target_pairs={{0,6},{1,7},{2,0},{3,1},{4,2},{5,3},{6,4},{7,5},{8,14},{9,15},{10,... | collective-permute-start | bytes 393224 | tf_op jit(solution)/shard_map/ppermute | solution.py:468
  192.2 9.0 %collective-permute-done.43 = bf16[1152,256]{1,0:T(8,128)(2,1)S(1)} collective-permute-done((bf16[1152,256]{1,0:T(8,128)(2,1)S(1)}, bf16[1152,256]{1,0:T(8,128)(2,1)S(1)}, u32[]{:S(2)}, u32[]{:S(2)}) %collective-permute-start.43) | collective-permute-done | bytes 589856 | tf_op jit(solution)/shard_map/ppermute | solution.py:468
  202.3 3.0 %shard_map.121.refs_2_ = bf16[128,9216]{1,0:T(8,128)(2,1)} custom-call(s32[8]{0:T(128)S(1)} %copy-done.23, bf16[128,1152]{1,0:T(8,128)(2,1)S(1)} %get-tuple-element.124.refs_0_, bf16[128,1152]{1,0:T(8,128)(2,1)S(1)} %get-tuple-element.125.refs_1_, bf16[128,1152]{1,0:T(8,128)(2,1)S(1)} %get-tuple-element.126.refs_2_, ...), custom_call_target="tpu_custom_call" | custom-call | tf_op jit(solution)/shard_map/pallas_call | solution.py:165
  205.6 8.6 %collective-permute-done.46 = bf16[1152,256]{1,0:T(8,128)(2,1)S(1)} collective-permute-done((bf16[1152,256]{1,0:T(8,128)(2,1)S(1)}, bf16[1152,256]{1,0:T(8,128)(2,1)S(1)}, u32[]{:S(2)}, u32[]{:S(2)}) %collective-permute-start.46) | collective-permute-done | bytes 589856 | tf_op jit(solution)/shard_map/ppermute | solution.py:468
  215.2 1.7 maximum_bitcast_fusion
  216.9 1.4 shard_map.123
  (144 shorter events, 43.2 us)
Async XLA Ops:
  0.6 19.1 %collective-permute-start.2 = (bf16[1152,256]{1,0:T(8,128)(2,1)}, bf16[1152,256]{1,0:T(8,128)(2,1)}, u32[]{:S(2)}, u32[]{:S(2)}) collective-permute-start(bf16[1152,256]{1,0:T(8,128)(2,1)} %bitcast.17), channel_id=1, source_target_pairs={{0,2},{1,3},{2,4},{3,5},{4,6},{5,7},{6,0},{7,1},{8,10},{9,11},{10,... | collective-permute-start | bytes 1769480 | tf_op jit(solution)/shard_map/ppermute | solution.py:468
  3.7 16.0 %collective-permute-start = (bf16[1152,256]{1,0:T(8,128)(2,1)}, bf16[1152,256]{1,0:T(8,128)(2,1)S(1)}, u32[]{:S(2)}, u32[]{:S(2)}) collective-permute-start(bf16[1152,256]{1,0:T(8,128)(2,1)} %bitcast.18), channel_id=1, source_target_pairs={{0,8},{8,0},{16,24},{24,16},{1,9},{9,1},{17,25},{25,17},{2,10},{10... | collective-permute-start | bytes 1769480 | tf_op jit(solution)/shard_map/ppermute | solution.py:471
  5.2 14.8 %collective-permute-start.1 = (bf16[1152,256]{1,0:T(8,128)(2,1)}, bf16[1152,256]{1,0:T(8,128)(2,1)}, u32[]{:S(2)}, u32[]{:S(2)}) collective-permute-start(bf16[1152,256]{1,0:T(8,128)(2,1)} %bitcast.19), channel_id=1, source_target_pairs={{0,16},{8,24},{16,0},{24,8},{1,17},{9,25},{17,1},{25,9},{2,18},{10... | collective-permute-start | bytes 1769480 | tf_op jit(solution)/shard_map/ppermute | solution.py:471
  20.6 19.8 %collective-permute-start.3 = (bf16[2,128,5760]{2,1,0:T(8,128)(2,1)S(1)}, bf16[2,128,5760]{2,1,0:T(8,128)(2,1)S(1)}, u32[]{:S(2)}, u32[]{:S(2)}) collective-permute-start(bf16[2,128,5760]{2,1,0:T(8,128)(2,1)S(1)} %get-tuple-element.71), channel_id=1, source_target_pairs={{0,1},{1,0},{2,3},{3,2},{4,5},{5,4},{6,7},{7,6},{8,9},{9,8},{10,11... | collective-permute-start | bytes 8847368 | tf_op jit(solution)/shard_map/ppermute | solution.py:465
  20.6 16.0 %collective-permute-start.10 = (bf16[1152,256]{1,0:T(8,128)(2,1)}, bf16[1152,256]{1,0:T(8,128)(2,1)S(1)}, u32[]{:S(2)}, u32[]{:S(2)}) collective-permute-start(bf16[1152,256]{1,0:T(8,128)(2,1)} %collective-permute-done.2.refs_8_), channel_id=1, source_target_pairs={{0,16},{8,24},{16,0},{24,8},{1,17},{9,25},{17,1},{25,9},{2,18},{10... | collective-permute-start | bytes 1769480 | tf_op jit(solution)/shard_map/ppermute | solution.py:471
  21.8 15.7 %collective-permute-start.9 = (bf16[1152,256]{1,0:T(8,128)(2,1)}, bf16[1152,256]{1,0:T(8,128)(2,1)S(1)}, u32[]{:S(2)}, u32[]{:S(2)}) collective-permute-start(bf16[1152,256]{1,0:T(8,128)(2,1)} %collective-permute-done.2.refs_8_), channel_id=1, source_target_pairs={{0,8},{8,0},{16,24},{24,16},{1,9},{9,1},{17,25},{25,17},{2,10},{10... | collective-permute-start | bytes 1769480 | tf_op jit(solution)/shard_map/ppermute | solution.py:471
  23.2 17.2 %collective-permute-start.7 = (bf16[1152,256]{1,0:T(8,128)(2,1)}, bf16[1152,256]{1,0:T(8,128)(2,1)S(1)}, u32[]{:S(2)}, u32[]{:S(2)}) collective-permute-start(bf16[1152,256]{1,0:T(8,128)(2,1)} %collective-permute-done.2.refs_8_), channel_id=1, source_target_pairs={{0,2},{1,3},{2,4},{3,5},{4,6},{5,7},{6,0},{7,1},{8,10},{9,11},{10,... | collective-permute-start | bytes 1769480 | tf_op jit(solution)/shard_map/ppermute | solution.py:468
  40.4 14.3 %collective-permute-start.11 = (bf16[1152,256]{1,0:T(8,128)(2,1)S(1)}, bf16[1152,256]{1,0:T(8,128)(2,1)S(1)}, u32[]{:S(2)}, u32[]{:S(2)}) collective-permute-start(bf16[1152,256]{1,0:T(8,128)(2,1)S(1)} %collective-permute-done.7.refs_8_), channel_id=1, source_target_pairs={{0,8},{8,0},{16,24},{24,16},{1,9},{9,1},{17,25},{25,17},{2,10},{10... | collective-permute-start | bytes 1769480 | tf_op jit(solution)/shard_map/ppermute | solution.py:471
  41.0 16.3 %collective-permute-start.12 = (bf16[1152,256]{1,0:T(8,128)(2,1)S(1)}, bf16[1152,256]{1,0:T(8,128)(2,1)S(1)}, u32[]{:S(2)}, u32[]{:S(2)}) collective-permute-start(bf16[1152,256]{1,0:T(8,128)(2,1)S(1)} %collective-permute-done.7.refs_8_), channel_id=1, source_target_pairs={{0,16},{8,24},{16,0},{24,8},{1,17},{9,25},{17,1},{25,9},{2,18},{10... | collective-permute-start | bytes 1769480 | tf_op jit(solution)/shard_map/ppermute | solution.py:471
  41.8 18.6 %collective-permute-start.4 = (bf16[1152,256]{1,0:T(8,128)(2,1)S(1)}, bf16[1152,256]{1,0:T(8,128)(2,1)S(1)}, u32[]{:S(2)}, u32[]{:S(2)}) collective-permute-start(bf16[1152,256]{1,0:T(8,128)(2,1)S(1)} %bitcast.14), channel_id=1, source_target_pairs={{0,2},{1,3},{2,4},{3,5},{4,6},{5,7},{6,0},{7,1},{8,10},{9,11},{10,... | collective-permute-start | bytes 1769480 | tf_op jit(solution)/shard_map/ppermute | solution.py:468
  41.9 30.7 %collective-permute-start.8 = (bf16[1152,256]{1,0:T(8,128)(2,1)S(1)}, bf16[1152,256]{1,0:T(8,128)(2,1)S(1)}, u32[]{:S(2)}, u32[]{:S(2)}) collective-permute-start(bf16[1152,256]{1,0:T(8,128)(2,1)S(1)} %collective-permute-done.7.refs_8_), channel_id=1, source_target_pairs={{0,2},{1,3},{2,4},{3,5},{4,6},{5,7},{6,0},{7,1},{8,10},{9,11},{10,... | collective-permute-start | bytes 1769480 | tf_op jit(solution)/shard_map/ppermute | solution.py:468
  44.2 19.3 %collective-permute-start.13 = (bf16[576,256]{1,0:T(8,128)(2,1)S(1)}, bf16[576,256]{1,0:T(8,128)(2,1)S(1)}, u32[]{:S(2)}, u32[]{:S(2)}) collective-permute-start(bf16[576,256]{1,0:T(8,128)(2,1)S(1)} %slice.24), channel_id=1, source_target_pairs={{0,16},{8,24},{16,0},{24,8},{1,17},{9,25},{17,1},{25,9},{2,18},{10... | collective-permute-start | bytes 884744 | tf_op jit(solution)/shard_map/ppermute | solution.py:471
  58.2 7.8 %collective-permute-start.15 = (bf16[576,256]{1,0:T(8,128)(2,1)S(1)}, bf16[576,256]{1,0:T(8,128)(2,1)S(1)}, u32[]{:S(2)}, u32[]{:S(2)}) collective-permute-start(bf16[576,256]{1,0:T(8,128)(2,1)S(1)} %slice.26), channel_id=1, source_target_pairs={{0,8},{8,0},{16,24},{24,16},{1,9},{9,1},{17,25},{25,17},{2,10},{10... | collective-permute-start | bytes 884744 | tf_op jit(solution)/shard_map/ppermute | solution.py:471
  59.8 12.8 %collective-permute-start.16 = (bf16[576,256]{1,0:T(8,128)(2,1)S(1)}, bf16[576,256]{1,0:T(8,128)(2,1)S(1)}, u32[]{:S(2)}, u32[]{:S(2)}) collective-permute-start(bf16[576,256]{1,0:T(8,128)(2,1)S(1)} %slice.27), channel_id=1, source_target_pairs={{0,8},{8,0},{16,24},{24,16},{1,9},{9,1},{17,25},{25,17},{2,10},{10... | collective-permute-start | bytes 884744 | tf_op jit(solution)/shard_map/ppermute | solution.py:471
  60.5 12.1 %collective-permute-start.14 = (bf16[576,256]{1,0:T(8,128)(2,1)S(1)}, bf16[576,256]{1,0:T(8,128)(2,1)S(1)}, u32[]{:S(2)}, u32[]{:S(2)}) collective-permute-start(bf16[576,256]{1,0:T(8,128)(2,1)S(1)} %slice.25), channel_id=1, source_target_pairs={{0,16},{8,24},{16,0},{24,8},{1,17},{9,25},{17,1},{25,9},{2,18},{10... | collective-permute-start | bytes 884744 | tf_op jit(solution)/shard_map/ppermute | solution.py:471
  63.6 19.2 %collective-permute-start.5 = (bf16[1152,256]{1,0:T(8,128)(2,1)S(1)}, bf16[1152,256]{1,0:T(8,128)(2,1)S(1)}, u32[]{:S(2)}, u32[]{:S(2)}) collective-permute-start(bf16[1152,256]{1,0:T(8,128)(2,1)S(1)} %collective-permute-done.4.refs_7_.refs_12_), channel_id=1, source_target_pairs={{0,2},{1,3},{2,4},{3,5},{4,6},{5,7},{6,0},{7,1},{8,10},{9,11},{10,... | collective-permute-start | bytes 1769480 | tf_op jit(solution)/shard_map/ppermute | solution.py:468
  72.6 13.0 %collective-permute-start.17 = (bf16[1152,256]{1,0:T(8,128)(2,1)S(1)}, bf16[1152,256]{1,0:T(8,128)(2,1)S(1)}, u32[]{:S(2)}, u32[]{:S(2)}) collective-permute-start(bf16[1152,256]{1,0:T(8,128)(2,1)S(1)} %collective-permute-done.8.refs_8_), channel_id=1, source_target_pairs={{0,8},{8,0},{16,24},{24,16},{1,9},{9,1},{17,25},{25,17},{2,10},{10... | collective-permute-start | bytes 1769480 | tf_op jit(solution)/shard_map/ppermute | solution.py:471
  73.8 12.4 %collective-permute-start.18 = (bf16[1152,256]{1,0:T(8,128)(2,1)S(1)}, bf16[1152,256]{1,0:T(8,128)(2,1)S(1)}, u32[]{:S(2)}, u32[]{:S(2)}) collective-permute-start(bf16[1152,256]{1,0:T(8,128)(2,1)S(1)} %collective-permute-done.8.refs_8_), channel_id=1, source_target_pairs={{0,16},{8,24},{16,0},{24,8},{1,17},{9,25},{17,1},{25,9},{2,18},{10... | collective-permute-start | bytes 1769480 | tf_op jit(solution)/shard_map/ppermute | solution.py:471
  82.7 14.6 %collective-permute-start.6 = (bf16[1152,256]{1,0:T(8,128)(2,1)S(1)}, bf16[1152,256]{1,0:T(8,128)(2,1)S(1)}, u32[]{:S(2)}, u32[]{:S(2)}) collective-permute-start(bf16[1152,256]{1,0:T(8,128)(2,1)S(1)} %collective-permute-done.5.refs_7_.refs_12_), channel_id=1, source_target_pairs={{0,2},{1,3},{2,4},{3,5},{4,6},{5,7},{6,0},{7,1},{8,10},{9,11},{10,... | collective-permute-start | bytes 1769480 | tf_op jit(solution)/shard_map/ppermute | solution.py:468
  82.8 10.0 %collective-permute-start.21 = (bf16[576,256]{1,0:T(8,128)(2,1)S(1)}, bf16[576,256]{1,0:T(8,128)(2,1)S(1)}, u32[]{:S(2)}, u32[]{:S(2)}) collective-permute-start(bf16[576,256]{1,0:T(8,128)(2,1)S(1)} %slice.34), channel_id=1, source_target_pairs={{0,16},{8,24},{16,0},{24,8},{1,17},{9,25},{17,1},{25,9},{2,18},{10... | collective-permute-start | bytes 884744 | tf_op jit(solution)/shard_map/ppermute | solution.py:471
  84.1 9.5 %collective-permute-start.22 = (bf16[576,256]{1,0:T(8,128)(2,1)S(1)}, bf16[576,256]{1,0:T(8,128)(2,1)S(1)}, u32[]{:S(2)}, u32[]{:S(2)}) collective-permute-start(bf16[576,256]{1,0:T(8,128)(2,1)S(1)} %slice.35), channel_id=1, source_target_pairs={{0,8},{8,0},{16,24},{24,16},{1,9},{9,1},{17,25},{25,17},{2,10},{10... | collective-permute-start | bytes 884744 | tf_op jit(solution)/shard_map/ppermute | solution.py:471
  85.6 11.8 %collective-permute-start.19 = (bf16[576,256]{1,0:T(8,128)(2,1)S(1)}, bf16[576,256]{1,0:T(8,128)(2,1)S(1)}, u32[]{:S(2)}, u32[]{:S(2)}) collective-permute-start(bf16[576,256]{1,0:T(8,128)(2,1)S(1)} %slice.32), channel_id=1, source_target_pairs={{0,16},{8,24},{16,0},{24,8},{1,17},{9,25},{17,1},{25,9},{2,18},{10... | collective-permute-start | bytes 884744 | tf_op jit(solution)/shard_map/ppermute | solution.py:471
  86.3 11.1 %collective-permute-start.20 = (bf16[576,256]{1,0:T(8,128)(2,1)S(1)}, bf16[576,256]{1,0:T(8,128)(2,1)S(1)}, u32[]{:S(2)}, u32[]{:S(2)}) collective-permute-start(bf16[576,256]{1,0:T(8,128)(2,1)S(1)} %slice.33), channel_id=1, source_target_pairs={{0,8},{8,0},{16,24},{24,16},{1,9},{9,1},{17,25},{25,17},{2,10},{10... | collective-permute-start | bytes 884744 | tf_op jit(solution)/shard_map/ppermute | solution.py:471
  100.1 4.6 %collective-permute-start.24 = (f32[264,768]{1,0:T(8,128)S(1)}, f32[264,768]{1,0:T(8,128)S(1)}, u32[]{:S(2)}, u32[]{:S(2)}) collective-permute-start(f32[264,768]{1,0:T(8,128)S(1)} %get-tuple-element.91.cross), channel_id=1, source_target_pairs={{0,1},{1,0},{2,3},{3,2},{4,5},{5,4},{6,7},{7,6},{8,9},{9,8},{10,11... | collective-permute-start | bytes 2433032 | tf_op jit(solution)/shard_map/ppermute | solution.py:465
  100.1 4.5 %collective-permute-start.23 = (f32[128,1280]{1,0:T(8,128)S(1)}, f32[128,1280]{1,0:T(8,128)S(1)}, u32[]{:S(2)}, u32[]{:S(2)}) collective-permute-start(f32[128,1280]{1,0:T(8,128)S(1)} %get-tuple-element.90), channel_id=1, source_target_pairs={{0,1},{1,0},{2,3},{3,2},{4,5},{5,4},{6,7},{7,6},{8,9},{9,8},{10,11... | collective-permute-start | bytes 1966088 | tf_op jit(solution)/shard_map/ppermute | solution.py:465
  101.5 15.9 %collective-permute-start.30 = (bf16[256,1152]{1,0:T(8,128)(2,1)S(1)}, bf16[256,1152]{1,0:T(8,128)(2,1)S(1)}, u32[]{:S(2)}, u32[]{:S(2)}) collective-permute-start(bf16[256,1152]{1,0:T(8,128)(2,1)S(1)} %shard_map.112), channel_id=1, source_target_pairs={{0,6},{1,7},{2,0},{3,1},{4,2},{5,3},{6,4},{7,5},{8,14},{9,15},{10,... | collective-permute-start | bytes 1769480 | tf_op jit(solution)/shard_map/ppermute | solution.py:468
  105.0 1.4 collective-permute-start.26
  105.7 1.7 collective-permute-start.27
  107.3 14.5 %collective-permute-start.25 = (f32[128,512]{1,0:T(8,128)S(1)}, f32[128,512]{1,0:T(8,128)S(1)}, u32[]{:S(2)}, u32[]{:S(2)}) collective-permute-start(f32[128,512]{1,0:T(8,128)S(1)} %get-tuple-element.92.refs_1_.refs_7_.refs_3_), channel_id=1, source_target_pairs={{0,1},{1,0},{2,3},{3,2},{4,5},{5,4},{6,7},{7,6},{8,9},{9,8},{10,11... | collective-permute-start | bytes 786440 | tf_op jit(solution)/shard_map/ppermute | solution.py:465
  107.6 14.0 %collective-permute-start.29 = (bf16[128,256]{1,0:T(8,128)(2,1)S(1)}, bf16[128,256]{1,0:T(8,128)(2,1)S(1)}, u32[]{:S(2)}, u32[]{:S(2)}) collective-permute-start(bf16[128,256]{1,0:T(8,128)(2,1)S(1)} %shard_map.111), channel_id=1, source_target_pairs={{8,0},{9,1},{10,2},{11,3},{12,4},{13,5},{14,6},{15,7}} | collective-permute-start | bytes 196616 | tf_op jit(solution)/shard_map/ppermute | solution.py:621
  121.7 1.3 collective-permute-start.31
  125.4 6.8 %collective-permute-start.32 = (bf16[256,1152]{1,0:T(8,128)(2,1)}, bf16[256,1152]{1,0:T(8,128)(2,1)S(1)}, u32[]{:S(2)}, u32[]{:S(2)}) collective-permute-start(bf16[256,1152]{1,0:T(8,128)(2,1)} %shard_map.114.refs_5_), channel_id=1, source_target_pairs={{24,16},{16,24},{25,17},{17,25},{26,18},{18,26},{27,19},{19,27},{2... | collective-permute-start | bytes 1769480 | tf_op jit(solution)/shard_map/ppermute | solution.py:678
  126.1 21.6 %collective-permute-start.35 = (bf16[256,1152]{1,0:T(8,128)(2,1)}, bf16[256,1152]{1,0:T(8,128)(2,1)}, u32[]{:S(2)}, u32[]{:S(2)}) collective-permute-start(bf16[256,1152]{1,0:T(8,128)(2,1)} %shard_map.114.refs_5_), channel_id=1, source_target_pairs={{8,0},{9,1},{10,2},{11,3},{12,4},{13,5},{14,6},{15,7}} | collective-permute-start | bytes 1769480 | tf_op jit(solution)/shard_map/ppermute | solution.py:678
  130.1 17.6 %collective-permute-start.34 = (bf16[1152,256]{1,0:T(8,128)(2,1)}, bf16[1152,256]{1,0:T(8,128)(2,1)}, u32[]{:S(2)}, u32[]{:S(2)}) collective-permute-start(bf16[1152,256]{1,0:T(8,128)(2,1)} %get-tuple-element.108), channel_id=1, source_target_pairs={{0,2},{1,3},{2,4},{3,5},{4,6},{5,7},{6,0},{7,1},{8,10},{9,11},{10,... | collective-permute-start | bytes 1769480 | tf_op jit(solution)/shard_map/ppermute | solution.py:468
  135.5 21.5 %collective-permute-start.33 = (bf16[256,1152]{1,0:T(8,128)(2,1)}, bf16[256,1152]{1,0:T(8,128)(2,1)}, u32[]{:S(2)}, u32[]{:S(2)}) collective-permute-start(bf16[256,1152]{1,0:T(8,128)(2,1)} %add_convert_fusion.6), channel_id=1, source_target_pairs={{24,8},{16,0},{25,9},{17,1},{26,10},{18,2},{27,11},{19,3},{28,12},... | collective-permute-start | bytes 1769480 | tf_op jit(solution)/shard_map/ppermute | solution.py:684
  136.8 24.1 %collective-permute-start.38 = (bf16[256,1152]{1,0:T(8,128)(2,1)}, bf16[256,1152]{1,0:T(8,128)(2,1)}, u32[]{:S(2)}, u32[]{:S(2)}) collective-permute-start(bf16[256,1152]{1,0:T(8,128)(2,1)} %get-tuple-element.105.refs_5_), channel_id=1, source_target_pairs={{24,16},{8,0},{16,24},{25,17},{9,1},{17,25},{26,18},{10,2},{18,26}... | collective-permute-start | bytes 1769480 | tf_op jit(solution)/shard_map/ppermute | solution.py:675
  138.1 30.8 %collective-permute-start.37 = (bf16[256,1152]{1,0:T(8,128)(2,1)}, bf16[256,1152]{1,0:T(8,128)(2,1)S(1)}, u32[]{:S(2)}, u32[]{:S(2)}) collective-permute-start(bf16[256,1152]{1,0:T(8,128)(2,1)} %copy-done.14), channel_id=1, source_target_pairs={{24,16},{8,0},{16,24},{25,17},{9,1},{17,25},{26,18},{10,2},{18,26}... | collective-permute-start | bytes 1769480 | tf_op jit(solution)/shard_map/ppermute | solution.py:675
  149.1 24.5 %collective-permute-start.40 = (bf16[1152,256]{1,0:T(8,128)(2,1)S(1)}, bf16[1152,256]{1,0:T(8,128)(2,1)S(1)}, u32[]{:S(2)}, u32[]{:S(2)}) collective-permute-start(bf16[1152,256]{1,0:T(8,128)(2,1)S(1)} %add_convert_fusion.5), channel_id=1, source_target_pairs={{0,2},{1,3},{2,4},{3,5},{4,6},{5,7},{6,0},{7,1},{8,10},{9,11},{10,... | collective-permute-start | bytes 1769480 | tf_op jit(solution)/shard_map/ppermute | solution.py:468
  162.5 18.3 %collective-permute-start.39 = (bf16[256,1152]{1,0:T(8,128)(2,1)S(1)}, bf16[256,1152]{1,0:T(8,128)(2,1)S(1)}, u32[]{:S(2)}, u32[]{:S(2)}) collective-permute-start(bf16[256,1152]{1,0:T(8,128)(2,1)S(1)} %add_convert_fusion.4), channel_id=1, source_target_pairs={{24,8},{16,0},{25,9},{17,1},{26,10},{18,2},{27,11},{19,3},{28,12},... | collective-permute-start | bytes 1769480 | tf_op jit(solution)/shard_map/ppermute | solution.py:684
  163.9 23.2 %collective-permute-start.42 = (bf16[1152,256]{1,0:T(8,128)(2,1)S(1)}, bf16[1152,256]{1,0:T(8,128)(2,1)S(1)}, u32[]{:S(2)}, u32[]{:S(2)}) collective-permute-start(bf16[1152,256]{1,0:T(8,128)(2,1)S(1)} %get-tuple-element.112), channel_id=1, source_target_pairs={{0,2},{1,3},{2,4},{3,5},{4,6},{5,7},{6,0},{7,1},{8,10},{9,11},{10,... | collective-permute-start | bytes 1769480 | tf_op jit(solution)/shard_map/ppermute | solution.py:468
  169.0 22.2 %collective-permute-start.44 = (bf16[256,1152]{1,0:T(8,128)(2,1)S(1)}, bf16[256,1152]{1,0:T(8,128)(2,1)S(1)}, u32[]{:S(2)}, u32[]{:S(2)}) collective-permute-start(bf16[256,1152]{1,0:T(8,128)(2,1)S(1)} %add_convert_fusion.3), channel_id=1, source_target_pairs={{24,8},{16,0},{25,9},{17,1},{26,10},{18,2},{27,11},{19,3},{28,12},... | collective-permute-start | bytes 1769480 | tf_op jit(solution)/shard_map/ppermute | solution.py:684
  172.3 16.5 %collective-permute-start.36 = (bf16[256,1152]{1,0:T(8,128)(2,1)S(1)}, bf16[256,1152]{1,0:T(8,128)(2,1)S(1)}, u32[]{:S(2)}, u32[]{:S(2)}) collective-permute-start(bf16[256,1152]{1,0:T(8,128)(2,1)S(1)} %get-tuple-element.114.refs_5_), channel_id=1, source_target_pairs={{24,16},{8,0},{16,24},{25,17},{9,1},{17,25},{26,18},{10,2},{18,26}... | collective-permute-start | bytes 1769480 | tf_op jit(solution)/shard_map/ppermute | solution.py:675
  182.8 8.4 %collective-permute-start.45 = (bf16[256,256]{1,0:T(8,128)(2,1)S(1)}, bf16[256,256]{1,0:T(8,128)(2,1)S(1)}, u32[]{:S(2)}, u32[]{:S(2)}) collective-permute-start(bf16[256,256]{1,0:T(8,128)(2,1)S(1)} %pad_maximum_fusion.1), channel_id=1, source_target_pairs={{0,6},{1,7},{2,0},{3,1},{4,2},{5,3},{6,4},{7,5},{8,14},{9,15},{10,... | collective-permute-start | bytes 393224 | tf_op jit(solution)/shard_map/ppermute | solution.py:468
  187.3 13.9 %collective-permute-start.43 = (bf16[1152,256]{1,0:T(8,128)(2,1)S(1)}, bf16[1152,256]{1,0:T(8,128)(2,1)S(1)}, u32[]{:S(2)}, u32[]{:S(2)}) collective-permute-start(bf16[1152,256]{1,0:T(8,128)(2,1)S(1)} %add_convert_fusion.1), channel_id=1, source_target_pairs={{0,2},{1,3},{2,4},{3,5},{4,6},{5,7},{6,0},{7,1},{8,10},{9,11},{10,... | collective-permute-start | bytes 1769480 | tf_op jit(solution)/shard_map/ppermute | solution.py:468
  188.9 16.7 %collective-permute-start.41 = (bf16[256,1152]{1,0:T(8,128)(2,1)S(1)}, bf16[256,1152]{1,0:T(8,128)(2,1)S(1)}, u32[]{:S(2)}, u32[]{:S(2)}) collective-permute-start(bf16[256,1152]{1,0:T(8,128)(2,1)S(1)} %add_convert_fusion.2), channel_id=1, source_target_pairs={{24,8},{16,0},{25,9},{17,1},{26,10},{18,2},{27,11},{19,3},{28,12},... | collective-permute-start | bytes 1769480 | tf_op jit(solution)/shard_map/ppermute | solution.py:684
  192.1 10.2 %collective-permute-start.47 = (bf16[128,3456]{1,0:T(8,128)(2,1)S(1)}, bf16[128,3456]{1,0:T(8,128)(2,1)S(1)}, u32[]{:S(2)}, u32[]{:S(2)}) collective-permute-start(bf16[128,3456]{1,0:T(8,128)(2,1)S(1)} %pad_maximum_fusion), channel_id=1, source_target_pairs={{0,1},{1,0},{2,3},{3,2},{4,5},{5,4},{6,7},{7,6},{8,9},{9,8},{10,11... | collective-permute-start | bytes 2654216 | tf_op jit(solution)/shard_map/ppermute | solution.py:465
  201.3 12.9 %collective-permute-start.46 = (bf16[1152,256]{1,0:T(8,128)(2,1)S(1)}, bf16[1152,256]{1,0:T(8,128)(2,1)S(1)}, u32[]{:S(2)}, u32[]{:S(2)}) collective-permute-start(bf16[1152,256]{1,0:T(8,128)(2,1)S(1)} %add_convert_fusion), channel_id=1, source_target_pairs={{0,2},{1,3},{2,4},{3,5},{4,6},{5,7},{6,0},{7,1},{8,10},{9,11},{10,... | collective-permute-start | bytes 1769480 | tf_op jit(solution)/shard_map/ppermute | solution.py:468
  215.0 1.9 collective-permute-start.48
  (26 other events, 472.3 us)

commit v2 on v1

--- a/solution.py
+++ b/solution.py
@@ -571,10 +571,6 @@
     for index in range(2, line):
         firsts.append(first_half(nears[index][0]))
         seconds.append(second_half(nears[index][1]))
-    downs.append(along(downs[2]))
-    for index in range(1, line):
-        sums = add_step(sums, index, nears[index] + (firsts[index], seconds[index]))
-    mine, other, cross = sums
     (normed,) = run_kernel(
         norm_body,
         [((2 * tokens, rows), BF16)],
@@ -588,6 +584,10 @@
         ],
         scalars=(blocks,),
     )
+    downs.append(along(downs[2]))
+    for index in range(1, line):
+        sums = add_step(after(sums, normed), index, nears[index] + (firsts[index], seconds[index]))
+    mine, other, cross = sums
     normed_ahead = along(after(normed, mine), -1)
 
     got, cross_got = sibling(other), sibling(cross)
@@ -613,7 +613,7 @@
         (passed,) = run_kernel(
             functools.partial(chain_body, width=width, turn=turn),
             [((tokens, 2 * rank if turn == 1 else rank), BF16)],
-            state + (after(arrivals, normed_ahead) if turn == 3 else arrivals),
+            state + arrivals,
         )
         if turn == 1:
             arrivals += [late, lax.ppermute(passed, "section", [(2, 1)])]
@@ -660,6 +660,7 @@
         )
 
     terms, down_grads, up_grads, mines, theirs = {}, {}, {}, {}, {}
+    act_sib = after(act_sib, normed_ahead)
     (terms[1],) = grad_block(1, act)
     act = after(act, terms[1])
     for index in (2, 3):
@@ -691,12 +692,12 @@
     more = {1: scan_more(sums[1])}
     down_sum = add(after(down_ring, beside), down_grads[3][0]).astype(BF16)
     down_ring = along(down_sum)
+    sums[2] = scan_sum(2, after(opened[2], more[1]))
+    more[2] = scan_more(sums[2])
     mines[1], theirs[1], up_grads[1] = close_block(
-        1, (opened[1], after(more[1], down_sum), beside)
+        1, (opened[1], after(more[1], down_sum, sums[2]), beside)
     )
     up_ring = along(up_grads[1])
-    sums[2] = scan_sum(2, after(opened[2], up_grads[1]))
-    more[2] = scan_more(sums[2])
     terms[0], *down_grads[0] = grad_block(0, after(act, up_grads[1]))
     opened[0] = scan_open(0)
     sums[3] = scan_sum(3, after(opened[3], sums[2]))
@@ -705,9 +706,10 @@
         2, (opened[2], after(more[2], sums[3], down_ring))
     )
     more[0] = scan_more(scan_sum(0, after(opened[0], sums[3], up_grads[2])))
-    act_ahead = along(jnp.concatenate(after([act, act_sib], up_grads[2]), axis=0), -1)
+    up_sum = add(up_ring, up_grads[2]).astype(BF16)
+    up_ring = along(up_sum)
+    act_ahead = along(jnp.concatenate(after([act, act_sib], up_sum), axis=0), -1)
     mines[3], theirs[3], up_grads[3] = close_block(3, (opened[3], after(more[3], act_ahead)))
-    up_ring = pass_on(up_ring, up_grads[2])
     up_sum = add(up_ring, up_grads[3]).astype(BF16)
     up_ring = along(up_sum)
     def place(first, count, produced):

time: 220 us -> 218 us (level)
    ppermute x13, waiting for transfers between devices: 49 us -> 34.5 us  [along(): lax.ppermute(value, 'rep', [(r, (r + 2 * steps) % reps) for r in range(re...]
    ppermute x3, waiting for transfers between devices: 6.29 us -> 20.7 us  [scan_open(): return lax.ppermute(terms[index], 'section', [(3, 2), (1, 0), (2, 3)])]
    ppermute x4, waiting for transfers between devices: 16.3 us -> 6.34 us  [scan_more(): return lax.ppermute(value, 'section', [(3, 1), (2, 0)])]
    ppermute x1, waiting for transfers between devices: 4.17 us -> 13 us  [per_device(): arrivals += [lax.ppermute(passed, 'section', [(1, 0)])]]
    unnamed x50 -> x44, local copies, waits for them, and re-layouts: 9.45 us -> 7.35 us
  transfers between devices with their start and end apart: 49 -> 49, of which waited for: 25 -> 26; matrix products, arithmetic and copies ran while one was open for 5% -> 5% of each run, Pallas kernels for 15% -> 15%
where the time goes in v2:
time: 218 us; the launch traced here: 215 us
  waiting for transfers between devices  109 us (50%)
  starting transfers between devices  46.4 us (21%)
  Pallas kernels  39.9 us (18%)
  local copies, waits for them, and re-layouts  10.2 us (5%)
  other arithmetic  8.28 us (4%)
    pallas_call x21, Pallas kernels, run_kernel(): pl.pallas_call(body, out_shape=out_shapes, grid_spec=pltpu.PrefetchScalar...  39.9 us
    ppermute x13, waiting for transfers between devices, along(): lax.ppermute(value, 'rep', [(r, (r + 2 * steps) % reps) for r in range(re...  34.5 us
    ppermute x16, waiting for transfers between devices, flip(): lax.ppermute(value, 'section', [(s, s ^ mask) for s in range(sections)])  32.5 us
    ppermute x3, waiting for transfers between devices, scan_open(): return lax.ppermute(terms[index], 'section', [(3, 2), (1, 0), (2, 3)])  20.7 us
    ppermute x16, starting transfers between devices, flip(): lax.ppermute(value, 'section', [(s, s ^ mask) for s in range(sections)])  18.3 us
    ppermute x1, waiting for transfers between devices, per_device(): arrivals += [lax.ppermute(passed, 'section', [(1, 0)])]  13 us
    ppermute x13, starting transfers between devices, along(): lax.ppermute(value, 'rep', [(r, (r + 2 * steps) % reps) for r in range(re...  13 us
    unnamed x44, local copies, waits for them, and re-layouts  7.35 us
  transfers between devices with their start and end apart: 49, of which 26 were waited for; matrix products, arithmetic and copies ran while one was open for 5% of the time, Pallas kernels for 15%

profile of v2, /device:TPU:0, one launch (start us, length us, event | category | flops | bytes accessed | tf_op | source)
XLA Modules:
  0.0 215.3 jit_solution(9092370251750460280)
XLA Ops:
  0.6 3.1 %collective-permute-start.2 = (bf16[1152,256]{1,0:T(8,128)(2,1)}, bf16[1152,256]{1,0:T(8,128)(2,1)}, u32[]{:S(2)}, u32[]{:S(2)}) collective-permute-start(bf16[1152,256]{1,0:T(8,128)(2,1)} %bitcast.17), channel_id=1, source_target_pairs={{0,2},{1,3},{2,4},{3,5},{4,6},{5,7},{6,0},{7,1},{8,10},{9,11},{10,... | collective-permute-start | bytes 1769480 | tf_op jit(solution)/shard_map/ppermute | solution.py:468
  3.7 1.5 collective-permute-start
  5.2 1.5 collective-permute-start.1
  7.6 2.3 %copy-done.2 = s32[1,2,64,9216]{3,2,1,0:T(8,128)S(1)} copy-done((s32[1,2,64,9216]{3,2,1,0:T(8,128)S(1)}, s32[1,2,64,9216]{3,2,1,0:T(8,128)}, u32[]{:S(2)}) %copy-start.2) | copy-done | bytes 4718616
  9.9 1.7 copy-done.5
  11.6 1.7 copy-done.6
  13.9 5.8 %shard_map.104 = (bf16[2,128,4608]{2,1,0:T(8,128)(2,1)S(1)}, bf16[2,128,5760]{2,1,0:T(8,128)(2,1)S(1)}, f32[128,256]{1,0:T(8,128)S(1)}) custom-call(s32[8]{0:T(128)S(1)} %pad_add_fusion.blocks.refs_0_, s32[2]{0:T(128)S(1)} %bitcast.21, bf16[2,64,9216]{2,1,0:T(8,128)(2,1)S(1)} %bitcast.12, bf16[2,64,9216]{2,1,0:T(8,128)(2,1)S(1)} %bitcast.13, ...), custom_call_target="tpu_custom_call" | custom-call | tf_op jit(solution)/shard_map/pallas_call | solution.py:165
  20.0 1.5 collective-permute-start.10
  23.7 12.3 %collective-permute-done.10.refs_10_ = bf16[1152,256]{1,0:T(8,128)(2,1)S(1)} collective-permute-done((bf16[1152,256]{1,0:T(8,128)(2,1)}, bf16[1152,256]{1,0:T(8,128)(2,1)S(1)}, u32[]{:S(2)}, u32[]{:S(2)}) %collective-permute-start.10) | collective-permute-done | bytes 589856 | tf_op jit(solution)/shard_map/ppermute | solution.py:471
  37.2 2.4 %collective-permute-done.7.refs_8_ = bf16[1152,256]{1,0:T(8,128)(2,1)S(1)} collective-permute-done((bf16[1152,256]{1,0:T(8,128)(2,1)}, bf16[1152,256]{1,0:T(8,128)(2,1)S(1)}, u32[]{:S(2)}, u32[]{:S(2)}) %collective-permute-start.7) | collective-permute-done | bytes 589856 | tf_op jit(solution)/shard_map/ppermute | solution.py:468
  41.4 1.3 collective-permute-start.8
  43.7 1.6 collective-permute-start.13
  45.3 8.6 %collective-permute-done.11.refs_9_ = bf16[1152,256]{1,0:T(8,128)(2,1)S(1)} collective-permute-done((bf16[1152,256]{1,0:T(8,128)(2,1)S(1)}, bf16[1152,256]{1,0:T(8,128)(2,1)S(1)}, u32[]{:S(2)}, u32[]{:S(2)}) %collective-permute-start.11) | collective-permute-done | bytes 589856 | tf_op jit(solution)/shard_map/ppermute | solution.py:471
  53.8 3.2 %collective-permute-done.12.refs_10_ = bf16[1152,256]{1,0:T(8,128)(2,1)S(1)} collective-permute-done((bf16[1152,256]{1,0:T(8,128)(2,1)S(1)}, bf16[1152,256]{1,0:T(8,128)(2,1)S(1)}, u32[]{:S(2)}, u32[]{:S(2)}) %collective-permute-start.12) | collective-permute-done | bytes 589856 | tf_op jit(solution)/shard_map/ppermute | solution.py:471
  60.9 2.4 %collective-permute-done.13.refs_11_ = bf16[576,256]{1,0:T(8,128)(2,1)S(1)} collective-permute-done((bf16[576,256]{1,0:T(8,128)(2,1)S(1)}, bf16[576,256]{1,0:T(8,128)(2,1)S(1)}, u32[]{:S(2)}, u32[]{:S(2)}) %collective-permute-start.13) | collective-permute-done | bytes 294944 | tf_op jit(solution)/shard_map/ppermute | solution.py:471
  63.4 2.5 %collective-permute-done.15.refs_12_ = bf16[576,256]{1,0:T(8,128)(2,1)S(1)} collective-permute-done((bf16[576,256]{1,0:T(8,128)(2,1)S(1)}, bf16[576,256]{1,0:T(8,128)(2,1)S(1)}, u32[]{:S(2)}, u32[]{:S(2)}) %collective-permute-start.15) | collective-permute-done | bytes 294944 | tf_op jit(solution)/shard_map/ppermute | solution.py:471
  65.8 3.6 %shard_map.105 = (f32[128,1280]{1,0:T(8,128)S(1)}, f32[128,1280]{1,0:T(8,128)S(1)}, f32[264,768]{1,0:T(8,128)S(1)}) custom-call(s32[8]{0:T(128)S(1)} %pad_add_fusion.blocks.refs_0_, bf16[2,128,4608]{2,1,0:T(8,128)(2,1)S(1)} %get-tuple-element.75.refs_1_.own, bf16[2,128,5760]{2,1,0:T(8,128)(2,1)S(1)} %collective-permute-done.3.refs_2_.refs_4_.sib.stats_sib, ...), custom_call_target="tpu_custom_call" | custom-call | tf_op jit(solution)/shard_map/pallas_call | solution.py:165
  69.5 2.6 %collective-permute-done.8.refs_8_ = bf16[1152,256]{1,0:T(8,128)(2,1)S(1)} collective-permute-done((bf16[1152,256]{1,0:T(8,128)(2,1)S(1)}, bf16[1152,256]{1,0:T(8,128)(2,1)S(1)}, u32[]{:S(2)}, u32[]{:S(2)}) %collective-permute-start.8) | collective-permute-done | bytes 589856 | tf_op jit(solution)/shard_map/ppermute | solution.py:468
  72.9 1.5 collective-permute-start.18
  74.4 7.8 %collective-permute-done.5.refs_7_.refs_12_ = bf16[1152,256]{1,0:T(8,128)(2,1)S(1)} collective-permute-done((bf16[1152,256]{1,0:T(8,128)(2,1)S(1)}, bf16[1152,256]{1,0:T(8,128)(2,1)S(1)}, u32[]{:S(2)}, u32[]{:S(2)}) %collective-permute-start.5) | collective-permute-done | bytes 589856 | tf_op jit(solution)/shard_map/ppermute | solution.py:468
  82.2 1.6 collective-permute-start.21
  85.3 1.3 collective-permute-start.20
  87.5 3.8 %shard_map.107 = (f32[128,1280]{1,0:T(8,128)S(1)}, f32[128,1280]{1,0:T(8,128)S(1)}, f32[264,768]{1,0:T(8,128)S(1)}) custom-call(s32[8]{0:T(128)S(1)} %pad_add_fusion.blocks.refs_0_, bf16[2,128,4608]{2,1,0:T(8,128)(2,1)S(1)} %get-tuple-element.75.refs_1_.own, ...), custom_call_target="tpu_custom_call", output_to_operand_aliasing={{0}: (13, {}), {1}: (14, {}), {2}: (15, {})} | custom-call | tf_op jit(solution)/shard_map/pallas_call | solution.py:165
  93.3 2.7 %shard_map.108 = (f32[128,1280]{1,0:T(8,128)S(1)}, f32[128,1280]{1,0:T(8,128)S(1)}, f32[264,768]{1,0:T(8,128)S(1)}) custom-call(s32[8]{0:T(128)S(1)} %pad_add_fusion.blocks.refs_0_, bf16[2,128,4608]{2,1,0:T(8,128)(2,1)S(1)} %get-tuple-element.75.refs_1_.own, ...), custom_call_target="tpu_custom_call", output_to_operand_aliasing={{0}: (13, {}), {1}: (14, {}), {2}: (15, {})} | custom-call | tf_op jit(solution)/shard_map/pallas_call | solution.py:165
  96.8 2.7 %shard_map.109 = (f32[128,1280]{1,0:T(8,128)S(1)}, f32[128,1280]{1,0:T(8,128)S(1)}, f32[264,768]{1,0:T(8,128)S(1)}) custom-call(s32[8]{0:T(128)S(1)} %pad_add_fusion.blocks.refs_0_, bf16[2,128,4608]{2,1,0:T(8,128)(2,1)S(1)} %get-tuple-element.75.refs_1_.own, ...), custom_call_target="tpu_custom_call", output_to_operand_aliasing={{0}: (13, {}), {1}: (14, {}), {2}: (15, {})} | custom-call | tf_op jit(solution)/shard_map/pallas_call | solution.py:165
  100.1 3.2 %collective-permute-start.31 = (bf16[256,1152]{1,0:T(8,128)(2,1)S(1)}, bf16[256,1152]{1,0:T(8,128)(2,1)S(1)}, u32[]{:S(2)}, u32[]{:S(2)}) collective-permute-start(bf16[256,1152]{1,0:T(8,128)(2,1)S(1)} %shard_map.106), channel_id=1, source_target_pairs={{0,6},{1,7},{2,0},{3,1},{4,2},{5,3},{6,4},{7,5},{8,14},{9,15},{10,... | collective-permute-start | bytes 1769480 | tf_op jit(solution)/shard_map/ppermute | solution.py:468
  107.5 13.0 %collective-permute-done.29.refs_9_ = bf16[128,256]{1,0:T(8,128)(2,1)S(1)} collective-permute-done((bf16[128,256]{1,0:T(8,128)(2,1)S(1)}, bf16[128,256]{1,0:T(8,128)(2,1)S(1)}, u32[]{:S(2)}, u32[]{:S(2)}) %collective-permute-start.29) | collective-permute-done | bytes 65568 | tf_op jit(solution)/shard_map/ppermute | solution.py:621
  121.9 2.3 %shard_map.114.refs_5_ = bf16[256,1152]{1,0:T(8,128)(2,1)} custom-call(s32[8]{0:T(128)S(1)} %pad_add_fusion.blocks.refs_0_, bf16[2,128,4608]{2,1,0:T(8,128)(2,1)S(1)} %get-tuple-element.75.refs_1_.own, bf16[2,128,5760]{2,1,0:T(8,128)(2,1)S(1)} %collective-permute-done.3.refs_2_.refs_4_.sib.stats_sib, ...), custom_call_target="tpu_custom_call" | custom-call | tf_op jit(solution)/shard_map/pallas_call | solution.py:165
  126.3 2.7 %shard_map.115 = (bf16[256,1152]{1,0:T(8,128)(2,1)}, bf16[1152,256]{1,0:T(8,128)(2,1)}) custom-call(s32[8]{0:T(128)S(1)} %pad_add_fusion.blocks.refs_0_, bf16[2,128,4608]{2,1,0:T(8,128)(2,1)S(1)} %get-tuple-element.75.refs_1_.own, bf16[2,128,5760]{2,1,0:T(8,128)(2,1)S(1)} %collective-permute-done.3.refs_2_.refs_4_.sib.stats_sib, ...), custom_call_target="tpu_custom_call" | custom-call | tf_op jit(solution)/shard_map/pallas_call | solution.py:165
  130.4 1.9 shard_map.116
  132.3 2.5 %add_convert_fusion.6 = bf16[256,1152]{1,0:T(8,128)(2,1)} fusion(bf16[256,1152]{1,0:T(8,128)(2,1)S(1)} %collective-permute-done.32.refs_6_, bf16[256,1152]{1,0:T(8,128)(2,1)} %shard_map.114.refs_5_), kind=kLoop, calls=%fused_computation.9 | loop fusion | flops 1179648 | bytes 1769472 | tf_op jit(solution)/shard_map/convert_element_type | solution.py:682
  138.3 8.3 %collective-permute-done.34 = bf16[1152,256]{1,0:T(8,128)(2,1)} collective-permute-done((bf16[1152,256]{1,0:T(8,128)(2,1)}, bf16[1152,256]{1,0:T(8,128)(2,1)}, u32[]{:S(2)}, u32[]{:S(2)}) %collective-permute-start.34) | collective-permute-done | bytes 589856 | tf_op jit(solution)/shard_map/ppermute | solution.py:468
  146.5 1.5 add_convert_fusion.5
  148.2 7.8 %collective-permute-done.36.refs_6_ = bf16[256,1152]{1,0:T(8,128)(2,1)} collective-permute-done((bf16[256,1152]{1,0:T(8,128)(2,1)}, bf16[256,1152]{1,0:T(8,128)(2,1)}, u32[]{:S(2)}, u32[]{:S(2)}) %collective-permute-start.36) | collective-permute-done | bytes 589856 | tf_op jit(solution)/shard_map/ppermute | solution.py:676
  156.0 1.4 add_convert_fusion.4
  158.7 2.3 %shard_map.117 = (bf16[128,1152]{1,0:T(8,128)(2,1)S(1)}, bf16[128,1152]{1,0:T(8,128)(2,1)S(1)}, bf16[1152,256]{1,0:T(8,128)(2,1)S(1)}) custom-call(s32[1]{0:T(128)} %bitcast.refs_0_, bf16[2,128,4608]{2,1,0:T(8,128)(2,1)S(1)} %copy-done.1, bf16[2,128,5760]{2,1,0:T(8,128)(2,1)S(1)} %collective-permute-done.3.refs_2_.refs_4_.sib.stats_sib, ...), custom_call_target="tpu_custom_call" | custom-call | tf_op jit(solution)/shard_map/pallas_call | solution.py:165
  161.1 6.6 %collective-permute-done.38.refs_6_ = bf16[256,1152]{1,0:T(8,128)(2,1)S(1)} collective-permute-done((bf16[256,1152]{1,0:T(8,128)(2,1)}, bf16[256,1152]{1,0:T(8,128)(2,1)S(1)}, u32[]{:S(2)}, u32[]{:S(2)}) %collective-permute-start.38) | collective-permute-done | bytes 589856 | tf_op jit(solution)/shard_map/ppermute | solution.py:676
  169.2 1.9 shard_map.118
  172.4 1.8 collective-permute-done.39.refs_7_
  174.3 2.0 shard_map.119
  177.4 3.9 %collective-permute-start.45 = (bf16[256,256]{1,0:T(8,128)(2,1)S(1)}, bf16[256,256]{1,0:T(8,128)(2,1)S(1)}, u32[]{:S(2)}, u32[]{:S(2)}) collective-permute-start(bf16[256,256]{1,0:T(8,128)(2,1)S(1)} %pad_maximum_fusion.1), channel_id=1, source_target_pairs={{0,6},{1,7},{2,0},{3,1},{4,2},{5,3},{6,4},{7,5},{8,14},{9,15},{10,... | collective-permute-start | bytes 393224 | tf_op jit(solution)/shard_map/ppermute | solution.py:468
  181.3 6.3 %collective-permute-done.37.refs_6_ = bf16[256,1152]{1,0:T(8,128)(2,1)S(1)} collective-permute-done((bf16[256,1152]{1,0:T(8,128)(2,1)S(1)}, bf16[256,1152]{1,0:T(8,128)(2,1)S(1)}, u32[]{:S(2)}, u32[]{:S(2)}) %collective-permute-start.37) | collective-permute-done | bytes 589856 | tf_op jit(solution)/shard_map/ppermute | solution.py:676
  189.0 3.3 %collective-permute-done.45.act = bf16[256,256]{1,0:T(8,128)(2,1)S(1)} collective-permute-done((bf16[256,256]{1,0:T(8,128)(2,1)S(1)}, bf16[256,256]{1,0:T(8,128)(2,1)S(1)}, u32[]{:S(2)}, u32[]{:S(2)}) %collective-permute-start.45) | collective-permute-done | bytes 131104 | tf_op jit(solution)/shard_map/ppermute | solution.py:468
  195.8 3.0 %shard_map.121.refs_2_ = bf16[128,9216]{1,0:T(8,128)(2,1)} custom-call(s32[8]{0:T(128)S(1)} %copy-done.20, bf16[128,1152]{1,0:T(8,128)(2,1)S(1)} %get-tuple-element.136.refs_0_, bf16[128,1152]{1,0:T(8,128)(2,1)S(1)} %get-tuple-element.137.refs_1_, bf16[128,1152]{1,0:T(8,128)(2,1)S(1)} %get-tuple-element.138.refs_2_, ...), custom_call_target="tpu_custom_call" | custom-call | tf_op jit(solution)/shard_map/pallas_call | solution.py:165
  198.7 4.5 %collective-permute-done.41.refs_7_ = bf16[256,1152]{1,0:T(8,128)(2,1)S(1)} collective-permute-done((bf16[256,1152]{1,0:T(8,128)(2,1)S(1)}, bf16[256,1152]{1,0:T(8,128)(2,1)S(1)}, u32[]{:S(2)}, u32[]{:S(2)}) %collective-permute-start.41) | collective-permute-done | bytes 589856 | tf_op jit(solution)/shard_map/ppermute | solution.py:685
  203.2 7.9 %collective-permute-done.46 = bf16[1152,256]{1,0:T(8,128)(2,1)S(1)} collective-permute-done((bf16[1152,256]{1,0:T(8,128)(2,1)S(1)}, bf16[1152,256]{1,0:T(8,128)(2,1)S(1)}, u32[]{:S(2)}, u32[]{:S(2)}) %collective-permute-start.46) | collective-permute-done | bytes 589856 | tf_op jit(solution)/shard_map/ppermute | solution.py:468
  212.1 1.7 maximum_bitcast_fusion
  213.9 1.4 shard_map.123
  (138 shorter events, 41.8 us)
Async XLA Ops:
  0.6 19.1 %collective-permute-start.2 = (bf16[1152,256]{1,0:T(8,128)(2,1)}, bf16[1152,256]{1,0:T(8,128)(2,1)}, u32[]{:S(2)}, u32[]{:S(2)}) collective-permute-start(bf16[1152,256]{1,0:T(8,128)(2,1)} %bitcast.17), channel_id=1, source_target_pairs={{0,2},{1,3},{2,4},{3,5},{4,6},{5,7},{6,0},{7,1},{8,10},{9,11},{10,... | collective-permute-start | bytes 1769480 | tf_op jit(solution)/shard_map/ppermute | solution.py:468
  3.7 16.1 %collective-permute-start = (bf16[1152,256]{1,0:T(8,128)(2,1)}, bf16[1152,256]{1,0:T(8,128)(2,1)}, u32[]{:S(2)}, u32[]{:S(2)}) collective-permute-start(bf16[1152,256]{1,0:T(8,128)(2,1)} %bitcast.18), channel_id=1, source_target_pairs={{0,8},{8,0},{16,24},{24,16},{1,9},{9,1},{17,25},{25,17},{2,10},{10... | collective-permute-start | bytes 1769480 | tf_op jit(solution)/shard_map/ppermute | solution.py:471
  5.2 14.8 %collective-permute-start.1 = (bf16[1152,256]{1,0:T(8,128)(2,1)}, bf16[1152,256]{1,0:T(8,128)(2,1)}, u32[]{:S(2)}, u32[]{:S(2)}) collective-permute-start(bf16[1152,256]{1,0:T(8,128)(2,1)} %bitcast.19), channel_id=1, source_target_pairs={{0,16},{8,24},{16,0},{24,8},{1,17},{9,25},{17,1},{25,9},{2,18},{10... | collective-permute-start | bytes 1769480 | tf_op jit(solution)/shard_map/ppermute | solution.py:471
  20.0 19.6 %collective-permute-start.3 = (bf16[2,128,5760]{2,1,0:T(8,128)(2,1)S(1)}, bf16[2,128,5760]{2,1,0:T(8,128)(2,1)S(1)}, u32[]{:S(2)}, u32[]{:S(2)}) collective-permute-start(bf16[2,128,5760]{2,1,0:T(8,128)(2,1)S(1)} %get-tuple-element.77), channel_id=1, source_target_pairs={{0,1},{1,0},{2,3},{3,2},{4,5},{5,4},{6,7},{7,6},{8,9},{9,8},{10,11... | collective-permute-start | bytes 8847368 | tf_op jit(solution)/shard_map/ppermute | solution.py:465
  20.0 16.0 %collective-permute-start.10 = (bf16[1152,256]{1,0:T(8,128)(2,1)}, bf16[1152,256]{1,0:T(8,128)(2,1)S(1)}, u32[]{:S(2)}, u32[]{:S(2)}) collective-permute-start(bf16[1152,256]{1,0:T(8,128)(2,1)} %collective-permute-done.2.refs_8_), channel_id=1, source_target_pairs={{0,16},{8,24},{16,0},{24,8},{1,17},{9,25},{17,1},{25,9},{2,18},{10... | collective-permute-start | bytes 1769480 | tf_op jit(solution)/shard_map/ppermute | solution.py:471
  21.5 15.7 %collective-permute-start.9 = (bf16[1152,256]{1,0:T(8,128)(2,1)}, bf16[1152,256]{1,0:T(8,128)(2,1)S(1)}, u32[]{:S(2)}, u32[]{:S(2)}) collective-permute-start(bf16[1152,256]{1,0:T(8,128)(2,1)} %collective-permute-done.2.refs_8_), channel_id=1, source_target_pairs={{0,8},{8,0},{16,24},{24,16},{1,9},{9,1},{17,25},{25,17},{2,10},{10... | collective-permute-start | bytes 1769480 | tf_op jit(solution)/shard_map/ppermute | solution.py:471
  22.5 17.1 %collective-permute-start.7 = (bf16[1152,256]{1,0:T(8,128)(2,1)}, bf16[1152,256]{1,0:T(8,128)(2,1)S(1)}, u32[]{:S(2)}, u32[]{:S(2)}) collective-permute-start(bf16[1152,256]{1,0:T(8,128)(2,1)} %collective-permute-done.2.refs_8_), channel_id=1, source_target_pairs={{0,2},{1,3},{2,4},{3,5},{4,6},{5,7},{6,0},{7,1},{8,10},{9,11},{10,... | collective-permute-start | bytes 1769480 | tf_op jit(solution)/shard_map/ppermute | solution.py:468
  39.6 14.2 %collective-permute-start.11 = (bf16[1152,256]{1,0:T(8,128)(2,1)S(1)}, bf16[1152,256]{1,0:T(8,128)(2,1)S(1)}, u32[]{:S(2)}, u32[]{:S(2)}) collective-permute-start(bf16[1152,256]{1,0:T(8,128)(2,1)S(1)} %collective-permute-done.7.refs_8_), channel_id=1, source_target_pairs={{0,8},{8,0},{16,24},{24,16},{1,9},{9,1},{17,25},{25,17},{2,10},{10... | collective-permute-start | bytes 1769480 | tf_op jit(solution)/shard_map/ppermute | solution.py:471
  40.8 16.3 %collective-permute-start.12 = (bf16[1152,256]{1,0:T(8,128)(2,1)S(1)}, bf16[1152,256]{1,0:T(8,128)(2,1)S(1)}, u32[]{:S(2)}, u32[]{:S(2)}) collective-permute-start(bf16[1152,256]{1,0:T(8,128)(2,1)S(1)} %collective-permute-done.7.refs_8_), channel_id=1, source_target_pairs={{0,16},{8,24},{16,0},{24,8},{1,17},{9,25},{17,1},{25,9},{2,18},{10... | collective-permute-start | bytes 1769480 | tf_op jit(solution)/shard_map/ppermute | solution.py:471
  41.3 18.9 %collective-permute-start.4 = (bf16[1152,256]{1,0:T(8,128)(2,1)S(1)}, bf16[1152,256]{1,0:T(8,128)(2,1)S(1)}, u32[]{:S(2)}, u32[]{:S(2)}) collective-permute-start(bf16[1152,256]{1,0:T(8,128)(2,1)S(1)} %bitcast.14), channel_id=1, source_target_pairs={{0,2},{1,3},{2,4},{3,5},{4,6},{5,7},{6,0},{7,1},{8,10},{9,11},{10,... | collective-permute-start | bytes 1769480 | tf_op jit(solution)/shard_map/ppermute | solution.py:468
  41.4 30.7 %collective-permute-start.8 = (bf16[1152,256]{1,0:T(8,128)(2,1)S(1)}, bf16[1152,256]{1,0:T(8,128)(2,1)S(1)}, u32[]{:S(2)}, u32[]{:S(2)}) collective-permute-start(bf16[1152,256]{1,0:T(8,128)(2,1)S(1)} %collective-permute-done.7.refs_8_), channel_id=1, source_target_pairs={{0,2},{1,3},{2,4},{3,5},{4,6},{5,7},{6,0},{7,1},{8,10},{9,11},{10,... | collective-permute-start | bytes 1769480 | tf_op jit(solution)/shard_map/ppermute | solution.py:468
  43.7 19.7 %collective-permute-start.13 = (bf16[576,256]{1,0:T(8,128)(2,1)S(1)}, bf16[576,256]{1,0:T(8,128)(2,1)S(1)}, u32[]{:S(2)}, u32[]{:S(2)}) collective-permute-start(bf16[576,256]{1,0:T(8,128)(2,1)S(1)} %slice.24), channel_id=1, source_target_pairs={{0,16},{8,24},{16,0},{24,8},{1,17},{9,25},{17,1},{25,9},{2,18},{10... | collective-permute-start | bytes 884744 | tf_op jit(solution)/shard_map/ppermute | solution.py:471
  58.0 7.8 %collective-permute-start.15 = (bf16[576,256]{1,0:T(8,128)(2,1)S(1)}, bf16[576,256]{1,0:T(8,128)(2,1)S(1)}, u32[]{:S(2)}, u32[]{:S(2)}) collective-permute-start(bf16[576,256]{1,0:T(8,128)(2,1)S(1)} %slice.26), channel_id=1, source_target_pairs={{0,8},{8,0},{16,24},{24,16},{1,9},{9,1},{17,25},{25,17},{2,10},{10... | collective-permute-start | bytes 884744 | tf_op jit(solution)/shard_map/ppermute | solution.py:471
  59.0 13.1 %collective-permute-start.16 = (bf16[576,256]{1,0:T(8,128)(2,1)S(1)}, bf16[576,256]{1,0:T(8,128)(2,1)S(1)}, u32[]{:S(2)}, u32[]{:S(2)}) collective-permute-start(bf16[576,256]{1,0:T(8,128)(2,1)S(1)} %slice.27), channel_id=1, source_target_pairs={{0,8},{8,0},{16,24},{24,16},{1,9},{9,1},{17,25},{25,17},{2,10},{10... | collective-permute-start | bytes 884744 | tf_op jit(solution)/shard_map/ppermute | solution.py:471
  60.2 11.8 %collective-permute-start.14 = (bf16[576,256]{1,0:T(8,128)(2,1)S(1)}, bf16[576,256]{1,0:T(8,128)(2,1)S(1)}, u32[]{:S(2)}, u32[]{:S(2)}) collective-permute-start(bf16[576,256]{1,0:T(8,128)(2,1)S(1)} %slice.25), channel_id=1, source_target_pairs={{0,16},{8,24},{16,0},{24,8},{1,17},{9,25},{17,1},{25,9},{2,18},{10... | collective-permute-start | bytes 884744 | tf_op jit(solution)/shard_map/ppermute | solution.py:471
  63.4 18.8 %collective-permute-start.5 = (bf16[1152,256]{1,0:T(8,128)(2,1)S(1)}, bf16[1152,256]{1,0:T(8,128)(2,1)S(1)}, u32[]{:S(2)}, u32[]{:S(2)}) collective-permute-start(bf16[1152,256]{1,0:T(8,128)(2,1)S(1)} %collective-permute-done.4.refs_7_.refs_12_), channel_id=1, source_target_pairs={{0,2},{1,3},{2,4},{3,5},{4,6},{5,7},{6,0},{7,1},{8,10},{9,11},{10,... | collective-permute-start | bytes 1769480 | tf_op jit(solution)/shard_map/ppermute | solution.py:468
  72.0 12.6 %collective-permute-start.17 = (bf16[1152,256]{1,0:T(8,128)(2,1)S(1)}, bf16[1152,256]{1,0:T(8,128)(2,1)S(1)}, u32[]{:S(2)}, u32[]{:S(2)}) collective-permute-start(bf16[1152,256]{1,0:T(8,128)(2,1)S(1)} %collective-permute-done.8.refs_8_), channel_id=1, source_target_pairs={{0,8},{8,0},{16,24},{24,16},{1,9},{9,1},{17,25},{25,17},{2,10},{10... | collective-permute-start | bytes 1769480 | tf_op jit(solution)/shard_map/ppermute | solution.py:471
  72.9 12.4 %collective-permute-start.18 = (bf16[1152,256]{1,0:T(8,128)(2,1)S(1)}, bf16[1152,256]{1,0:T(8,128)(2,1)S(1)}, u32[]{:S(2)}, u32[]{:S(2)}) collective-permute-start(bf16[1152,256]{1,0:T(8,128)(2,1)S(1)} %collective-permute-done.8.refs_8_), channel_id=1, source_target_pairs={{0,16},{8,24},{16,0},{24,8},{1,17},{9,25},{17,1},{25,9},{2,18},{10... | collective-permute-start | bytes 1769480 | tf_op jit(solution)/shard_map/ppermute | solution.py:471
  82.2 14.6 %collective-permute-start.6 = (bf16[1152,256]{1,0:T(8,128)(2,1)S(1)}, bf16[1152,256]{1,0:T(8,128)(2,1)S(1)}, u32[]{:S(2)}, u32[]{:S(2)}) collective-permute-start(bf16[1152,256]{1,0:T(8,128)(2,1)S(1)} %collective-permute-done.5.refs_7_.refs_12_), channel_id=1, source_target_pairs={{0,2},{1,3},{2,4},{3,5},{4,6},{5,7},{6,0},{7,1},{8,10},{9,11},{10,... | collective-permute-start | bytes 1769480 | tf_op jit(solution)/shard_map/ppermute | solution.py:468
  82.2 10.0 %collective-permute-start.21 = (bf16[576,256]{1,0:T(8,128)(2,1)S(1)}, bf16[576,256]{1,0:T(8,128)(2,1)S(1)}, u32[]{:S(2)}, u32[]{:S(2)}) collective-permute-start(bf16[576,256]{1,0:T(8,128)(2,1)S(1)} %slice.34), channel_id=1, source_target_pairs={{0,16},{8,24},{16,0},{24,8},{1,17},{9,25},{17,1},{25,9},{2,18},{10... | collective-permute-start | bytes 884744 | tf_op jit(solution)/shard_map/ppermute | solution.py:471
  83.8 9.5 %collective-permute-start.22 = (bf16[576,256]{1,0:T(8,128)(2,1)S(1)}, bf16[576,256]{1,0:T(8,128)(2,1)S(1)}, u32[]{:S(2)}, u32[]{:S(2)}) collective-permute-start(bf16[576,256]{1,0:T(8,128)(2,1)S(1)} %slice.35), channel_id=1, source_target_pairs={{0,8},{8,0},{16,24},{24,16},{1,9},{9,1},{17,25},{25,17},{2,10},{10... | collective-permute-start | bytes 884744 | tf_op jit(solution)/shard_map/ppermute | solution.py:471
  84.7 12.1 %collective-permute-start.19 = (bf16[576,256]{1,0:T(8,128)(2,1)S(1)}, bf16[576,256]{1,0:T(8,128)(2,1)S(1)}, u32[]{:S(2)}, u32[]{:S(2)}) collective-permute-start(bf16[576,256]{1,0:T(8,128)(2,1)S(1)} %slice.32), channel_id=1, source_target_pairs={{0,16},{8,24},{16,0},{24,8},{1,17},{9,25},{17,1},{25,9},{2,18},{10... | collective-permute-start | bytes 884744 | tf_op jit(solution)/shard_map/ppermute | solution.py:471
  85.3 11.5 %collective-permute-start.20 = (bf16[576,256]{1,0:T(8,128)(2,1)S(1)}, bf16[576,256]{1,0:T(8,128)(2,1)S(1)}, u32[]{:S(2)}, u32[]{:S(2)}) collective-permute-start(bf16[576,256]{1,0:T(8,128)(2,1)S(1)} %slice.33), channel_id=1, source_target_pairs={{0,8},{8,0},{16,24},{24,16},{1,9},{9,1},{17,25},{25,17},{2,10},{10... | collective-permute-start | bytes 884744 | tf_op jit(solution)/shard_map/ppermute | solution.py:471
  99.5 3.7 %collective-permute-start.24 = (f32[264,768]{1,0:T(8,128)S(1)}, f32[264,768]{1,0:T(8,128)S(1)}, u32[]{:S(2)}, u32[]{:S(2)}) collective-permute-start(f32[264,768]{1,0:T(8,128)S(1)} %get-tuple-element.106.cross), channel_id=1, source_target_pairs={{0,1},{1,0},{2,3},{3,2},{4,5},{5,4},{6,7},{7,6},{8,9},{9,8},{10,11... | collective-permute-start | bytes 2433032 | tf_op jit(solution)/shard_map/ppermute | solution.py:465
  99.6 3.7 %collective-permute-start.23 = (f32[128,1280]{1,0:T(8,128)S(1)}, f32[128,1280]{1,0:T(8,128)S(1)}, u32[]{:S(2)}, u32[]{:S(2)}) collective-permute-start(f32[128,1280]{1,0:T(8,128)S(1)} %get-tuple-element.105), channel_id=1, source_target_pairs={{0,1},{1,0},{2,3},{3,2},{4,5},{5,4},{6,7},{7,6},{8,9},{9,8},{10,11... | collective-permute-start | bytes 1966088 | tf_op jit(solution)/shard_map/ppermute | solution.py:465
  100.1 20.6 %collective-permute-start.31 = (bf16[256,1152]{1,0:T(8,128)(2,1)S(1)}, bf16[256,1152]{1,0:T(8,128)(2,1)S(1)}, u32[]{:S(2)}, u32[]{:S(2)}) collective-permute-start(bf16[256,1152]{1,0:T(8,128)(2,1)S(1)} %shard_map.106), channel_id=1, source_target_pairs={{0,6},{1,7},{2,0},{3,1},{4,2},{5,3},{6,4},{7,5},{8,14},{9,15},{10,... | collective-permute-start | bytes 1769480 | tf_op jit(solution)/shard_map/ppermute | solution.py:468
  103.7 1.4 collective-permute-start.26
  104.3 1.6 collective-permute-start.27
  105.9 16.0 %collective-permute-start.25 = (f32[128,512]{1,0:T(8,128)S(1)}, f32[128,512]{1,0:T(8,128)S(1)}, u32[]{:S(2)}, u32[]{:S(2)}) collective-permute-start(f32[128,512]{1,0:T(8,128)S(1)} %get-tuple-element.107.refs_1_.refs_7_.refs_3_), channel_id=1, source_target_pairs={{0,1},{1,0},{2,3},{3,2},{4,5},{5,4},{6,7},{7,6},{8,9},{9,8},{10,11... | collective-permute-start | bytes 786440 | tf_op jit(solution)/shard_map/ppermute | solution.py:465
  106.2 14.3 %collective-permute-start.29 = (bf16[128,256]{1,0:T(8,128)(2,1)S(1)}, bf16[128,256]{1,0:T(8,128)(2,1)S(1)}, u32[]{:S(2)}, u32[]{:S(2)}) collective-permute-start(bf16[128,256]{1,0:T(8,128)(2,1)S(1)} %shard_map.112), channel_id=1, source_target_pairs={{8,0},{9,1},{10,2},{11,3},{12,4},{13,5},{14,6},{15,7}} | collective-permute-start | bytes 196616 | tf_op jit(solution)/shard_map/ppermute | solution.py:621
  120.6 1.3 collective-permute-start.30
  124.2 8.1 %collective-permute-start.32 = (bf16[256,1152]{1,0:T(8,128)(2,1)}, bf16[256,1152]{1,0:T(8,128)(2,1)S(1)}, u32[]{:S(2)}, u32[]{:S(2)}) collective-permute-start(bf16[256,1152]{1,0:T(8,128)(2,1)} %shard_map.114.refs_5_), channel_id=1, source_target_pairs={{24,16},{16,24},{25,17},{17,25},{26,18},{18,26},{27,19},{19,27},{2... | collective-permute-start | bytes 1769480 | tf_op jit(solution)/shard_map/ppermute | solution.py:679
  125.0 21.6 %collective-permute-start.35 = (bf16[256,1152]{1,0:T(8,128)(2,1)}, bf16[256,1152]{1,0:T(8,128)(2,1)}, u32[]{:S(2)}, u32[]{:S(2)}) collective-permute-start(bf16[256,1152]{1,0:T(8,128)(2,1)} %shard_map.114.refs_5_), channel_id=1, source_target_pairs={{8,0},{9,1},{10,2},{11,3},{12,4},{13,5},{14,6},{15,7}} | collective-permute-start | bytes 1769480 | tf_op jit(solution)/shard_map/ppermute | solution.py:679
  129.0 17.6 %collective-permute-start.34 = (bf16[1152,256]{1,0:T(8,128)(2,1)}, bf16[1152,256]{1,0:T(8,128)(2,1)}, u32[]{:S(2)}, u32[]{:S(2)}) collective-permute-start(bf16[1152,256]{1,0:T(8,128)(2,1)} %get-tuple-element.120), channel_id=1, source_target_pairs={{0,2},{1,3},{2,4},{3,5},{4,6},{5,7},{6,0},{7,1},{8,10},{9,11},{10,... | collective-permute-start | bytes 1769480 | tf_op jit(solution)/shard_map/ppermute | solution.py:468
  129.1 26.9 %collective-permute-start.36 = (bf16[256,1152]{1,0:T(8,128)(2,1)}, bf16[256,1152]{1,0:T(8,128)(2,1)}, u32[]{:S(2)}, u32[]{:S(2)}) collective-permute-start(bf16[256,1152]{1,0:T(8,128)(2,1)} %get-tuple-element.117.refs_5_), channel_id=1, source_target_pairs={{24,16},{8,0},{16,24},{25,17},{9,1},{17,25},{26,18},{10,2},{18,26}... | collective-permute-start | bytes 1769480 | tf_op jit(solution)/shard_map/ppermute | solution.py:676
  135.7 20.3 %collective-permute-start.33 = (bf16[256,1152]{1,0:T(8,128)(2,1)}, bf16[256,1152]{1,0:T(8,128)(2,1)}, u32[]{:S(2)}, u32[]{:S(2)}) collective-permute-start(bf16[256,1152]{1,0:T(8,128)(2,1)} %add_convert_fusion.6), channel_id=1, source_target_pairs={{24,8},{16,0},{25,9},{17,1},{26,10},{18,2},{27,11},{19,3},{28,12},... | collective-permute-start | bytes 1769480 | tf_op jit(solution)/shard_map/ppermute | solution.py:685
  137.0 30.8 %collective-permute-start.38 = (bf16[256,1152]{1,0:T(8,128)(2,1)}, bf16[256,1152]{1,0:T(8,128)(2,1)S(1)}, u32[]{:S(2)}, u32[]{:S(2)}) collective-permute-start(bf16[256,1152]{1,0:T(8,128)(2,1)} %copy-done.13), channel_id=1, source_target_pairs={{24,16},{8,0},{16,24},{25,17},{9,1},{17,25},{26,18},{10,2},{18,26}... | collective-permute-start | bytes 1769480 | tf_op jit(solution)/shard_map/ppermute | solution.py:676
  148.1 24.3 %collective-permute-start.40 = (bf16[1152,256]{1,0:T(8,128)(2,1)S(1)}, bf16[1152,256]{1,0:T(8,128)(2,1)S(1)}, u32[]{:S(2)}, u32[]{:S(2)}) collective-permute-start(bf16[1152,256]{1,0:T(8,128)(2,1)S(1)} %add_convert_fusion.5), channel_id=1, source_target_pairs={{0,2},{1,3},{2,4},{3,5},{4,6},{5,7},{6,0},{7,1},{8,10},{9,11},{10,... | collective-permute-start | bytes 1769480 | tf_op jit(solution)/shard_map/ppermute | solution.py:468
  157.4 16.9 %collective-permute-start.39 = (bf16[256,1152]{1,0:T(8,128)(2,1)S(1)}, bf16[256,1152]{1,0:T(8,128)(2,1)S(1)}, u32[]{:S(2)}, u32[]{:S(2)}) collective-permute-start(bf16[256,1152]{1,0:T(8,128)(2,1)S(1)} %add_convert_fusion.4), channel_id=1, source_target_pairs={{24,8},{16,0},{25,9},{17,1},{26,10},{18,2},{27,11},{19,3},{28,12},... | collective-permute-start | bytes 1769480 | tf_op jit(solution)/shard_map/ppermute | solution.py:685
  161.1 16.1 %collective-permute-start.42 = (bf16[1152,256]{1,0:T(8,128)(2,1)S(1)}, bf16[1152,256]{1,0:T(8,128)(2,1)S(1)}, u32[]{:S(2)}, u32[]{:S(2)}) collective-permute-start(bf16[1152,256]{1,0:T(8,128)(2,1)S(1)} %get-tuple-element.125), channel_id=1, source_target_pairs={{0,2},{1,3},{2,4},{3,5},{4,6},{5,7},{6,0},{7,1},{8,10},{9,11},{10,... | collective-permute-start | bytes 1769480 | tf_op jit(solution)/shard_map/ppermute | solution.py:468
  167.9 21.1 %collective-permute-start.44 = (bf16[256,1152]{1,0:T(8,128)(2,1)S(1)}, bf16[256,1152]{1,0:T(8,128)(2,1)S(1)}, u32[]{:S(2)}, u32[]{:S(2)}) collective-permute-start(bf16[256,1152]{1,0:T(8,128)(2,1)S(1)} %add_convert_fusion.3), channel_id=1, source_target_pairs={{24,8},{16,0},{25,9},{17,1},{26,10},{18,2},{27,11},{19,3},{28,12},... | collective-permute-start | bytes 1769480 | tf_op jit(solution)/shard_map/ppermute | solution.py:685
  171.1 16.4 %collective-permute-start.37 = (bf16[256,1152]{1,0:T(8,128)(2,1)S(1)}, bf16[256,1152]{1,0:T(8,128)(2,1)S(1)}, u32[]{:S(2)}, u32[]{:S(2)}) collective-permute-start(bf16[256,1152]{1,0:T(8,128)(2,1)S(1)} %get-tuple-element.127.refs_5_), channel_id=1, source_target_pairs={{24,16},{8,0},{16,24},{25,17},{9,1},{17,25},{26,18},{10,2},{18,26}... | collective-permute-start | bytes 1769480 | tf_op jit(solution)/shard_map/ppermute | solution.py:676
  177.3 16.6 %collective-permute-start.43 = (bf16[1152,256]{1,0:T(8,128)(2,1)S(1)}, bf16[1152,256]{1,0:T(8,128)(2,1)S(1)}, u32[]{:S(2)}, u32[]{:S(2)}) collective-permute-start(bf16[1152,256]{1,0:T(8,128)(2,1)S(1)} %add_convert_fusion.1), channel_id=1, source_target_pairs={{0,2},{1,3},{2,4},{3,5},{4,6},{5,7},{6,0},{7,1},{8,10},{9,11},{10,... | collective-permute-start | bytes 1769480 | tf_op jit(solution)/shard_map/ppermute | solution.py:468
  177.4 14.9 %collective-permute-start.45 = (bf16[256,256]{1,0:T(8,128)(2,1)S(1)}, bf16[256,256]{1,0:T(8,128)(2,1)S(1)}, u32[]{:S(2)}, u32[]{:S(2)}) collective-permute-start(bf16[256,256]{1,0:T(8,128)(2,1)S(1)} %pad_maximum_fusion.1), channel_id=1, source_target_pairs={{0,6},{1,7},{2,0},{3,1},{4,2},{5,3},{6,4},{7,5},{8,14},{9,15},{10,... | collective-permute-start | bytes 393224 | tf_op jit(solution)/shard_map/ppermute | solution.py:468
  187.7 15.5 %collective-permute-start.41 = (bf16[256,1152]{1,0:T(8,128)(2,1)S(1)}, bf16[256,1152]{1,0:T(8,128)(2,1)S(1)}, u32[]{:S(2)}, u32[]{:S(2)}) collective-permute-start(bf16[256,1152]{1,0:T(8,128)(2,1)S(1)} %add_convert_fusion.2), channel_id=1, source_target_pairs={{24,8},{16,0},{25,9},{17,1},{26,10},{18,2},{27,11},{19,3},{28,12},... | collective-permute-start | bytes 1769480 | tf_op jit(solution)/shard_map/ppermute | solution.py:685
  193.3 2.5 %collective-permute-start.47 = (bf16[128,3456]{1,0:T(8,128)(2,1)S(1)}, bf16[128,3456]{1,0:T(8,128)(2,1)S(1)}, u32[]{:S(2)}, u32[]{:S(2)}) collective-permute-start(bf16[128,3456]{1,0:T(8,128)(2,1)S(1)} %pad_maximum_fusion), channel_id=1, source_target_pairs={{0,1},{1,0},{2,3},{3,2},{4,5},{5,4},{6,7},{7,6},{8,9},{9,8},{10,11... | collective-permute-start | bytes 2654216 | tf_op jit(solution)/shard_map/ppermute | solution.py:465
  194.1 17.0 %collective-permute-start.46 = (bf16[1152,256]{1,0:T(8,128)(2,1)S(1)}, bf16[1152,256]{1,0:T(8,128)(2,1)S(1)}, u32[]{:S(2)}, u32[]{:S(2)}) collective-permute-start(bf16[1152,256]{1,0:T(8,128)(2,1)S(1)} %add_convert_fusion), channel_id=1, source_target_pairs={{0,2},{1,3},{2,4},{3,5},{4,6},{5,7},{6,0},{7,1},{8,10},{9,11},{10,... | collective-permute-start | bytes 1769480 | tf_op jit(solution)/shard_map/ppermute | solution.py:468
  211.9 2.0 collective-permute-start.48
  (23 other events, 419.1 us)

commit v3 on v2

--- a/solution.py
+++ b/solution.py
@@ -663,8 +663,9 @@
     act_sib = after(act_sib, normed_ahead)
     (terms[1],) = grad_block(1, act)
     act = after(act, terms[1])
-    for index in (2, 3):
-        terms[index], *down_grads[index] = grad_block(index, act)
+    act_ahead = along(jnp.concatenate([act, act_sib], axis=0), -1)
+    terms[2], *down_grads[2] = grad_block(2, act)
+    terms[3], *down_grads[3] = grad_block(3, after(act, act_ahead))
 
     def add(*values):
         return sum(value.astype(F32) for value in values)
@@ -700,18 +701,21 @@
     up_ring = along(up_grads[1])
     terms[0], *down_grads[0] = grad_block(0, after(act, up_grads[1]))
     opened[0] = scan_open(0)
-    sums[3] = scan_sum(3, after(opened[3], sums[2]))
+    sums[3] = scan_sum(3, after(opened[3], sums[2], up_grads[1]))
     more[3] = scan_more(sums[3])
     mines[2], theirs[2], up_grads[2] = close_block(
         2, (opened[2], after(more[2], sums[3], down_ring))
     )
     more[0] = scan_more(scan_sum(0, after(opened[0], sums[3], up_grads[2])))
-    up_sum = add(up_ring, up_grads[2]).astype(BF16)
-    up_ring = along(up_sum)
-    act_ahead = along(jnp.concatenate(after([act, act_sib], up_sum), axis=0), -1)
-    mines[3], theirs[3], up_grads[3] = close_block(3, (opened[3], after(more[3], act_ahead)))
-    up_sum = add(up_ring, up_grads[3]).astype(BF16)
-    up_ring = along(up_sum)
+    halves = [slice(0, rows // 2), slice(rows // 2, rows)]
+    up_sums = [add(up_ring[half], up_grads[2][half]).astype(BF16) for half in halves]
+    up_ring = [along(value) for value in up_sums]
+    mines[3], theirs[3], up_grads[3] = close_block(3, (opened[3], after(more[3], *up_sums)))
+    up_sums = [add(up_ring[0], up_grads[3][halves[0]]).astype(BF16)]
+    second = after(up_ring[1], up_sums[0])
+    up_sums.append(add(second, up_grads[3][halves[1]]).astype(BF16))
+    up_ring = [along(value) for value in up_sums]
+
     def place(first, count, produced):
         sent = [theirs[index] for index in range(first, first + count)]
         arrived = sibling(jnp.concatenate(sent, axis=1) if count > 1 else sent[0])
@@ -734,7 +738,7 @@
 
     produced = place(1, line - 1, None)
     mines[0], theirs[0], up_grads[0] = close_block(
-        0, (opened[0], after(more[0], up_ring, produced))
+        0, (opened[0], after(more[0], up_ring[0], up_sums[1], produced))
     )
     produced = place(0, 1, produced)
     (down_own,) = run_kernel(
@@ -742,7 +746,7 @@
         [((rows, rank), F32)],
         [normed_ahead, act_ahead, after(down_grads[0][0], mines[3])],
     )
-    up_sum = add(up_ring, up_grads[0])
+    up_sum = add(jnp.concatenate(up_ring, axis=0), up_grads[0])
     grads = jnp.concatenate([add(down_ring, down_own), up_sum], axis=1)
     return produced.reshape(1, micro, tok, width), grads[None]
 

time: 218 us -> 213 us (0.977)
    ppermute x3, waiting for transfers between devices: 20.7 us -> 14.1 us  [scan_open(): return lax.ppermute(terms[index], 'section', [(3, 2), (1, 0), (2, 3)])]
    ppermute x4, waiting for transfers between devices: 6.34 us -> 10.6 us  [scan_more(): return lax.ppermute(value, 'section', [(3, 1), (2, 0)])]
    ppermute x13 -> x15, waiting for transfers between devices: 34.5 us -> 36.9 us  [along(): lax.ppermute(value, 'rep', [(r, (r + 2 * steps) % reps) for r in range(re...]
    ppermute x13 -> x15, starting transfers between devices: 13 us -> 11.1 us  [along(): lax.ppermute(value, 'rep', [(r, (r + 2 * steps) % reps) for r in range(re...]
    unnamed x44 -> x52, local copies, waits for them, and re-layouts: 7.35 us -> 7.79 us
  transfers between devices with their start and end apart: 49 -> 51, of which waited for: 26 -> 27; matrix products, arithmetic and copies ran while one was open for 5% -> 5% of each run, Pallas kernels for 15% -> 16%
where the time goes in v3:
time: 213 us; the launch traced here: 212 us
  waiting for transfers between devices  108 us (51%)
  starting transfers between devices  44.4 us (21%)
  Pallas kernels  39.7 us (19%)
  local copies, waits for them, and re-layouts  10.6 us (5%)
  other arithmetic  8.18 us (4%)
    pallas_call x21, Pallas kernels, run_kernel(): pl.pallas_call(body, out_shape=out_shapes, grid_spec=pltpu.PrefetchScalar...  39.7 us
    ppermute x15, waiting for transfers between devices, along(): lax.ppermute(value, 'rep', [(r, (r + 2 * steps) % reps) for r in range(re...  36.9 us
    ppermute x16, waiting for transfers between devices, flip(): lax.ppermute(value, 'section', [(s, s ^ mask) for s in range(sections)])  32.1 us
    ppermute x16, starting transfers between devices, flip(): lax.ppermute(value, 'section', [(s, s ^ mask) for s in range(sections)])  18.1 us
    ppermute x3, waiting for transfers between devices, scan_open(): return lax.ppermute(terms[index], 'section', [(3, 2), (1, 0), (2, 3)])  14.1 us
    ppermute x1, waiting for transfers between devices, per_device(): arrivals += [lax.ppermute(passed, 'section', [(1, 0)])]  13 us
    ppermute x15, starting transfers between devices, along(): lax.ppermute(value, 'rep', [(r, (r + 2 * steps) % reps) for r in range(re...  11.1 us
    ppermute x4, waiting for transfers between devices, scan_more(): return lax.ppermute(value, 'section', [(3, 1), (2, 0)])  10.6 us
  transfers between devices with their start and end apart: 51, of which 27 were waited for; matrix products, arithmetic and copies ran while one was open for 5% of the time, Pallas kernels for 16%

profile of v3, /device:TPU:0, one launch (start us, length us, event | category | flops | bytes accessed | tf_op | source)
XLA Modules:
  0.0 212.2 jit_solution(6202879876092170562)
XLA Ops:
  0.6 3.1 %collective-permute-start.2 = (bf16[1152,256]{1,0:T(8,128)(2,1)}, bf16[1152,256]{1,0:T(8,128)(2,1)}, u32[]{:S(2)}, u32[]{:S(2)}) collective-permute-start(bf16[1152,256]{1,0:T(8,128)(2,1)} %bitcast.17), channel_id=1, source_target_pairs={{0,2},{1,3},{2,4},{3,5},{4,6},{5,7},{6,0},{7,1},{8,10},{9,11},{10,... | collective-permute-start | bytes 1769480 | tf_op jit(solution)/shard_map/ppermute | solution.py:468
  3.7 1.5 collective-permute-start
  5.2 1.5 collective-permute-start.1
  7.6 2.3 %copy-done.2 = s32[1,2,64,9216]{3,2,1,0:T(8,128)S(1)} copy-done((s32[1,2,64,9216]{3,2,1,0:T(8,128)S(1)}, s32[1,2,64,9216]{3,2,1,0:T(8,128)}, u32[]{:S(2)}) %copy-start.2) | copy-done | bytes 4718616
  9.9 1.7 copy-done.5
  11.6 1.7 copy-done.6
  13.9 5.7 %shard_map.104 = (bf16[2,128,4608]{2,1,0:T(8,128)(2,1)S(1)}, bf16[2,128,5760]{2,1,0:T(8,128)(2,1)S(1)}, f32[128,256]{1,0:T(8,128)S(1)}) custom-call(s32[8]{0:T(128)S(1)} %pad_add_fusion.blocks.refs_0_, s32[2]{0:T(128)S(1)} %bitcast.21, bf16[2,64,9216]{2,1,0:T(8,128)(2,1)S(1)} %bitcast.12, bf16[2,64,9216]{2,1,0:T(8,128)(2,1)S(1)} %bitcast.13, ...), custom_call_target="tpu_custom_call" | custom-call | tf_op jit(solution)/shard_map/pallas_call | solution.py:165
  21.8 1.4 collective-permute-start.9
  24.1 12.4 %collective-permute-done.10.refs_10_ = bf16[1152,256]{1,0:T(8,128)(2,1)S(1)} collective-permute-done((bf16[1152,256]{1,0:T(8,128)(2,1)}, bf16[1152,256]{1,0:T(8,128)(2,1)S(1)}, u32[]{:S(2)}, u32[]{:S(2)}) %collective-permute-start.10) | collective-permute-done | bytes 589856 | tf_op jit(solution)/shard_map/ppermute | solution.py:471
  37.4 3.0 %collective-permute-done.7.refs_8_ = bf16[1152,256]{1,0:T(8,128)(2,1)S(1)} collective-permute-done((bf16[1152,256]{1,0:T(8,128)(2,1)}, bf16[1152,256]{1,0:T(8,128)(2,1)S(1)}, u32[]{:S(2)}, u32[]{:S(2)}) %collective-permute-start.7) | collective-permute-done | bytes 589856 | tf_op jit(solution)/shard_map/ppermute | solution.py:468
  45.3 9.5 %collective-permute-done.11.refs_9_ = bf16[1152,256]{1,0:T(8,128)(2,1)S(1)} collective-permute-done((bf16[1152,256]{1,0:T(8,128)(2,1)S(1)}, bf16[1152,256]{1,0:T(8,128)(2,1)S(1)}, u32[]{:S(2)}, u32[]{:S(2)}) %collective-permute-start.11) | collective-permute-done | bytes 589856 | tf_op jit(solution)/shard_map/ppermute | solution.py:471
  54.7 2.5 %collective-permute-done.12.refs_10_ = bf16[1152,256]{1,0:T(8,128)(2,1)S(1)} collective-permute-done((bf16[1152,256]{1,0:T(8,128)(2,1)S(1)}, bf16[1152,256]{1,0:T(8,128)(2,1)S(1)}, u32[]{:S(2)}, u32[]{:S(2)}) %collective-permute-start.12) | collective-permute-done | bytes 589856 | tf_op jit(solution)/shard_map/ppermute | solution.py:471
  58.2 1.5 collective-permute-start.15
  61.3 2.2 %collective-permute-done.13.refs_11_ = bf16[576,256]{1,0:T(8,128)(2,1)S(1)} collective-permute-done((bf16[576,256]{1,0:T(8,128)(2,1)S(1)}, bf16[576,256]{1,0:T(8,128)(2,1)S(1)}, u32[]{:S(2)}, u32[]{:S(2)}) %collective-permute-start.13) | collective-permute-done | bytes 294944 | tf_op jit(solution)/shard_map/ppermute | solution.py:471
  63.6 2.5 %collective-permute-done.15.refs_12_ = bf16[576,256]{1,0:T(8,128)(2,1)S(1)} collective-permute-done((bf16[576,256]{1,0:T(8,128)(2,1)S(1)}, bf16[576,256]{1,0:T(8,128)(2,1)S(1)}, u32[]{:S(2)}, u32[]{:S(2)}) %collective-permute-start.15) | collective-permute-done | bytes 294944 | tf_op jit(solution)/shard_map/ppermute | solution.py:471
  66.1 3.5 %shard_map.105 = (f32[128,1280]{1,0:T(8,128)S(1)}, f32[128,1280]{1,0:T(8,128)S(1)}, f32[264,768]{1,0:T(8,128)S(1)}) custom-call(s32[8]{0:T(128)S(1)} %pad_add_fusion.blocks.refs_0_, bf16[2,128,4608]{2,1,0:T(8,128)(2,1)S(1)} %get-tuple-element.75.refs_1_.own, bf16[2,128,5760]{2,1,0:T(8,128)(2,1)S(1)} %collective-permute-done.3.refs_2_.refs_4_.sib.stats_sib, ...), custom_call_target="tpu_custom_call" | custom-call | tf_op jit(solution)/shard_map/pallas_call | solution.py:165
  69.6 3.0 %collective-permute-done.8.refs_8_ = bf16[1152,256]{1,0:T(8,128)(2,1)S(1)} collective-permute-done((bf16[1152,256]{1,0:T(8,128)(2,1)S(1)}, bf16[1152,256]{1,0:T(8,128)(2,1)S(1)}, u32[]{:S(2)}, u32[]{:S(2)}) %collective-permute-start.8) | collective-permute-done | bytes 589856 | tf_op jit(solution)/shard_map/ppermute | solution.py:468
  73.8 1.4 collective-permute-start.18
  75.2 7.5 %collective-permute-done.5.refs_7_.refs_12_ = bf16[1152,256]{1,0:T(8,128)(2,1)S(1)} collective-permute-done((bf16[1152,256]{1,0:T(8,128)(2,1)S(1)}, bf16[1152,256]{1,0:T(8,128)(2,1)S(1)}, u32[]{:S(2)}, u32[]{:S(2)}) %collective-permute-start.5) | collective-permute-done | bytes 589856 | tf_op jit(solution)/shard_map/ppermute | solution.py:468
  84.1 1.5 collective-permute-start.22
  88.1 3.7 %shard_map.107 = (f32[128,1280]{1,0:T(8,128)S(1)}, f32[128,1280]{1,0:T(8,128)S(1)}, f32[264,768]{1,0:T(8,128)S(1)}) custom-call(s32[8]{0:T(128)S(1)} %pad_add_fusion.blocks.refs_0_, bf16[2,128,4608]{2,1,0:T(8,128)(2,1)S(1)} %get-tuple-element.75.refs_1_.own, ...), custom_call_target="tpu_custom_call", output_to_operand_aliasing={{0}: (13, {}), {1}: (14, {}), {2}: (15, {})} | custom-call | tf_op jit(solution)/shard_map/pallas_call | solution.py:165
  93.5 2.7 %shard_map.108 = (f32[128,1280]{1,0:T(8,128)S(1)}, f32[128,1280]{1,0:T(8,128)S(1)}, f32[264,768]{1,0:T(8,128)S(1)}) custom-call(s32[8]{0:T(128)S(1)} %pad_add_fusion.blocks.refs_0_, bf16[2,128,4608]{2,1,0:T(8,128)(2,1)S(1)} %get-tuple-element.75.refs_1_.own, ...), custom_call_target="tpu_custom_call", output_to_operand_aliasing={{0}: (13, {}), {1}: (14, {}), {2}: (15, {})} | custom-call | tf_op jit(solution)/shard_map/pallas_call | solution.py:165
  97.4 2.7 %shard_map.109 = (f32[128,1280]{1,0:T(8,128)S(1)}, f32[128,1280]{1,0:T(8,128)S(1)}, f32[264,768]{1,0:T(8,128)S(1)}) custom-call(s32[8]{0:T(128)S(1)} %pad_add_fusion.blocks.refs_0_, bf16[2,128,4608]{2,1,0:T(8,128)(2,1)S(1)} %get-tuple-element.75.refs_1_.own, ...), custom_call_target="tpu_custom_call", output_to_operand_aliasing={{0}: (13, {}), {1}: (14, {}), {2}: (15, {})} | custom-call | tf_op jit(solution)/shard_map/pallas_call | solution.py:165
  100.6 2.8 %collective-permute-start.31 = (bf16[256,1152]{1,0:T(8,128)(2,1)S(1)}, bf16[256,1152]{1,0:T(8,128)(2,1)S(1)}, u32[]{:S(2)}, u32[]{:S(2)}) collective-permute-start(bf16[256,1152]{1,0:T(8,128)(2,1)S(1)} %shard_map.106), channel_id=1, source_target_pairs={{0,6},{1,7},{2,0},{3,1},{4,2},{5,3},{6,4},{7,5},{8,14},{9,15},{10,... | collective-permute-start | bytes 1769480 | tf_op jit(solution)/shard_map/ppermute | solution.py:468
  107.7 13.0 %collective-permute-done.29.refs_9_ = bf16[128,256]{1,0:T(8,128)(2,1)S(1)} collective-permute-done((bf16[128,256]{1,0:T(8,128)(2,1)S(1)}, bf16[128,256]{1,0:T(8,128)(2,1)S(1)}, u32[]{:S(2)}, u32[]{:S(2)}) %collective-permute-start.29) | collective-permute-done | bytes 65568 | tf_op jit(solution)/shard_map/ppermute | solution.py:621
  122.1 2.4 %shard_map.114.refs_5_ = bf16[256,1152]{1,0:T(8,128)(2,1)} custom-call(s32[8]{0:T(128)S(1)} %pad_add_fusion.blocks.refs_0_, bf16[2,128,4608]{2,1,0:T(8,128)(2,1)S(1)} %get-tuple-element.75.refs_1_.own, bf16[2,128,5760]{2,1,0:T(8,128)(2,1)S(1)} %collective-permute-done.3.refs_2_.refs_4_.sib.stats_sib, ...), custom_call_target="tpu_custom_call" | custom-call | tf_op jit(solution)/shard_map/pallas_call | solution.py:165
  125.2 2.5 %collective-permute-start.33 = (bf16[256,256]{1,0:T(8,128)(2,1)S(1)}, bf16[256,256]{1,0:T(8,128)(2,1)S(1)}, u32[]{:S(2)}, u32[]{:S(2)}) collective-permute-start(bf16[256,256]{1,0:T(8,128)(2,1)S(1)} %pad_maximum_fusion.1), channel_id=1, source_target_pairs={{0,6},{1,7},{2,0},{3,1},{4,2},{5,3},{6,4},{7,5},{8,14},{9,15},{10,... | collective-permute-start | bytes 393224 | tf_op jit(solution)/shard_map/ppermute | solution.py:468
  129.0 2.7 %shard_map.115 = (bf16[256,1152]{1,0:T(8,128)(2,1)}, bf16[1152,256]{1,0:T(8,128)(2,1)}) custom-call(s32[8]{0:T(128)S(1)} %pad_add_fusion.blocks.refs_0_, bf16[2,128,4608]{2,1,0:T(8,128)(2,1)S(1)} %get-tuple-element.75.refs_1_.own, bf16[2,128,5760]{2,1,0:T(8,128)(2,1)S(1)} %collective-permute-done.3.refs_2_.refs_4_.sib.stats_sib, ...), custom_call_target="tpu_custom_call" | custom-call | tf_op jit(solution)/shard_map/pallas_call | solution.py:165
  133.2 1.9 shard_map.116
  135.1 2.5 %add_convert_fusion.4 = bf16[256,1152]{1,0:T(8,128)(2,1)} fusion(bf16[256,1152]{1,0:T(8,128)(2,1)S(1)} %collective-permute-done.32.refs_6_, bf16[256,1152]{1,0:T(8,128)(2,1)} %shard_map.114.refs_5_), kind=kLoop, calls=%fused_computation.7 | loop fusion | flops 1179648 | bytes 1769472 | tf_op jit(solution)/shard_map/convert_element_type | solution.py:683
  141.0 9.3 %collective-permute-done.35 = bf16[1152,256]{1,0:T(8,128)(2,1)} collective-permute-done((bf16[1152,256]{1,0:T(8,128)(2,1)}, bf16[1152,256]{1,0:T(8,128)(2,1)}, u32[]{:S(2)}, u32[]{:S(2)}) %collective-permute-start.35) | collective-permute-done | bytes 589856 | tf_op jit(solution)/shard_map/ppermute | solution.py:468
  150.3 1.5 add_convert_fusion.3
  152.0 6.8 %collective-permute-done.37.refs_6_ = bf16[256,1152]{1,0:T(8,128)(2,1)} collective-permute-done((bf16[256,1152]{1,0:T(8,128)(2,1)}, bf16[256,1152]{1,0:T(8,128)(2,1)}, u32[]{:S(2)}, u32[]{:S(2)}) %collective-permute-start.37) | collective-permute-done | bytes 589856 | tf_op jit(solution)/shard_map/ppermute | solution.py:677
  158.8 1.4 add_convert_fusion.2
  161.5 2.3 %shard_map.117 = (bf16[128,1152]{1,0:T(8,128)(2,1)S(1)}, bf16[128,1152]{1,0:T(8,128)(2,1)S(1)}, bf16[1152,256]{1,0:T(8,128)(2,1)S(1)}) custom-call(s32[1]{0:T(128)} %bitcast.refs_0_, bf16[2,128,4608]{2,1,0:T(8,128)(2,1)S(1)} %copy-done.1, bf16[2,128,5760]{2,1,0:T(8,128)(2,1)S(1)} %collective-permute-done.3.refs_2_.refs_4_.sib.stats_sib, ...), custom_call_target="tpu_custom_call" | custom-call | tf_op jit(solution)/shard_map/pallas_call | solution.py:165
  163.9 6.3 %collective-permute-done.39.refs_6_ = bf16[256,1152]{1,0:T(8,128)(2,1)S(1)} collective-permute-done((bf16[256,1152]{1,0:T(8,128)(2,1)}, bf16[256,1152]{1,0:T(8,128)(2,1)S(1)}, u32[]{:S(2)}, u32[]{:S(2)}) %collective-permute-start.39) | collective-permute-done | bytes 589856 | tf_op jit(solution)/shard_map/ppermute | solution.py:677
  171.7 1.9 shard_map.118
  175.0 1.5 collective-permute-done.40.refs_7_
  176.5 2.0 shard_map.119
  178.5 2.1 %collective-permute-done.43 = bf16[1152,256]{1,0:T(8,128)(2,1)S(1)} collective-permute-done((bf16[1152,256]{1,0:T(8,128)(2,1)S(1)}, bf16[1152,256]{1,0:T(8,128)(2,1)S(1)}, u32[]{:S(2)}, u32[]{:S(2)}) %collective-permute-start.43) | collective-permute-done | bytes 589856 | tf_op jit(solution)/shard_map/ppermute | solution.py:468
  180.9 6.9 %collective-permute-done.45.refs_7_ = bf16[256,1152]{1,0:T(8,128)(2,1)S(1)} collective-permute-done((bf16[256,1152]{1,0:T(8,128)(2,1)S(1)}, bf16[256,1152]{1,0:T(8,128)(2,1)S(1)}, u32[]{:S(2)}, u32[]{:S(2)}) %collective-permute-start.45) | collective-permute-done | bytes 589856 | tf_op jit(solution)/shard_map/ppermute | solution.py:686
  192.7 4.1 %collective-permute-done.47 = bf16[576,256]{1,0:T(8,128)(2,1)S(1)} collective-permute-done((bf16[576,256]{1,0:T(8,128)(2,1)S(1)}, bf16[576,256]{1,0:T(8,128)(2,1)S(1)}, u32[]{:S(2)}, u32[]{:S(2)}) %collective-permute-start.47) | collective-permute-done | bytes 294944 | tf_op jit(solution)/shard_map/ppermute | solution.py:468
  197.1 3.0 %shard_map.121.refs_2_ = bf16[128,9216]{1,0:T(8,128)(2,1)} custom-call(s32[8]{0:T(128)S(1)} %copy-done.24, bf16[128,1152]{1,0:T(8,128)(2,1)S(1)} %get-tuple-element.136.refs_0_, bf16[128,1152]{1,0:T(8,128)(2,1)S(1)} %get-tuple-element.137.refs_1_, bf16[128,1152]{1,0:T(8,128)(2,1)S(1)} %get-tuple-element.138.refs_2_, ...), custom_call_target="tpu_custom_call" | custom-call | tf_op jit(solution)/shard_map/pallas_call | solution.py:165
  200.1 4.4 %collective-permute-done.46 = bf16[576,256]{1,0:T(8,128)(2,1)S(1)} collective-permute-done((bf16[576,256]{1,0:T(8,128)(2,1)S(1)}, bf16[576,256]{1,0:T(8,128)(2,1)S(1)}, u32[]{:S(2)}, u32[]{:S(2)}) %collective-permute-start.46) | collective-permute-done | bytes 294944 | tf_op jit(solution)/shard_map/ppermute | solution.py:468
  204.5 2.1 collective-permute-done.42.refs_7_
  207.5 1.5 collective-permute-done.50
  209.1 1.7 maximum_bitcast_fusion
  210.8 1.4 shard_map.123
  (151 shorter events, 44.2 us)
Async XLA Ops:
  0.6 19.1 %collective-permute-start.2 = (bf16[1152,256]{1,0:T(8,128)(2,1)}, bf16[1152,256]{1,0:T(8,128)(2,1)}, u32[]{:S(2)}, u32[]{:S(2)}) collective-permute-start(bf16[1152,256]{1,0:T(8,128)(2,1)} %bitcast.17), channel_id=1, source_target_pairs={{0,2},{1,3},{2,4},{3,5},{4,6},{5,7},{6,0},{7,1},{8,10},{9,11},{10,... | collective-permute-start | bytes 1769480 | tf_op jit(solution)/shard_map/ppermute | solution.py:468
  3.7 16.0 %collective-permute-start = (bf16[1152,256]{1,0:T(8,128)(2,1)}, bf16[1152,256]{1,0:T(8,128)(2,1)S(1)}, u32[]{:S(2)}, u32[]{:S(2)}) collective-permute-start(bf16[1152,256]{1,0:T(8,128)(2,1)} %bitcast.18), channel_id=1, source_target_pairs={{0,8},{8,0},{16,24},{24,16},{1,9},{9,1},{17,25},{25,17},{2,10},{10... | collective-permute-start | bytes 1769480 | tf_op jit(solution)/shard_map/ppermute | solution.py:471
  5.2 14.8 %collective-permute-start.1 = (bf16[1152,256]{1,0:T(8,128)(2,1)}, bf16[1152,256]{1,0:T(8,128)(2,1)}, u32[]{:S(2)}, u32[]{:S(2)}) collective-permute-start(bf16[1152,256]{1,0:T(8,128)(2,1)} %bitcast.19), channel_id=1, source_target_pairs={{0,16},{8,24},{16,0},{24,8},{1,17},{9,25},{17,1},{25,9},{2,18},{10... | collective-permute-start | bytes 1769480 | tf_op jit(solution)/shard_map/ppermute | solution.py:471
  20.6 19.8 %collective-permute-start.3 = (bf16[2,128,5760]{2,1,0:T(8,128)(2,1)S(1)}, bf16[2,128,5760]{2,1,0:T(8,128)(2,1)S(1)}, u32[]{:S(2)}, u32[]{:S(2)}) collective-permute-start(bf16[2,128,5760]{2,1,0:T(8,128)(2,1)S(1)} %get-tuple-element.77), channel_id=1, source_target_pairs={{0,1},{1,0},{2,3},{3,2},{4,5},{5,4},{6,7},{7,6},{8,9},{9,8},{10,11... | collective-permute-start | bytes 8847368 | tf_op jit(solution)/shard_map/ppermute | solution.py:465
  20.6 16.0 %collective-permute-start.10 = (bf16[1152,256]{1,0:T(8,128)(2,1)}, bf16[1152,256]{1,0:T(8,128)(2,1)S(1)}, u32[]{:S(2)}, u32[]{:S(2)}) collective-permute-start(bf16[1152,256]{1,0:T(8,128)(2,1)} %collective-permute-done.2.refs_8_), channel_id=1, source_target_pairs={{0,16},{8,24},{16,0},{24,8},{1,17},{9,25},{17,1},{25,9},{2,18},{10... | collective-permute-start | bytes 1769480 | tf_op jit(solution)/shard_map/ppermute | solution.py:471
  21.8 15.7 %collective-permute-start.9 = (bf16[1152,256]{1,0:T(8,128)(2,1)}, bf16[1152,256]{1,0:T(8,128)(2,1)S(1)}, u32[]{:S(2)}, u32[]{:S(2)}) collective-permute-start(bf16[1152,256]{1,0:T(8,128)(2,1)} %collective-permute-done.2.refs_8_), channel_id=1, source_target_pairs={{0,8},{8,0},{16,24},{24,16},{1,9},{9,1},{17,25},{25,17},{2,10},{10... | collective-permute-start | bytes 1769480 | tf_op jit(solution)/shard_map/ppermute | solution.py:471
  23.2 17.2 %collective-permute-start.7 = (bf16[1152,256]{1,0:T(8,128)(2,1)}, bf16[1152,256]{1,0:T(8,128)(2,1)S(1)}, u32[]{:S(2)}, u32[]{:S(2)}) collective-permute-start(bf16[1152,256]{1,0:T(8,128)(2,1)} %collective-permute-done.2.refs_8_), channel_id=1, source_target_pairs={{0,2},{1,3},{2,4},{3,5},{4,6},{5,7},{6,0},{7,1},{8,10},{9,11},{10,... | collective-permute-start | bytes 1769480 | tf_op jit(solution)/shard_map/ppermute | solution.py:468
  40.4 14.3 %collective-permute-start.11 = (bf16[1152,256]{1,0:T(8,128)(2,1)S(1)}, bf16[1152,256]{1,0:T(8,128)(2,1)S(1)}, u32[]{:S(2)}, u32[]{:S(2)}) collective-permute-start(bf16[1152,256]{1,0:T(8,128)(2,1)S(1)} %collective-permute-done.7.refs_8_), channel_id=1, source_target_pairs={{0,8},{8,0},{16,24},{24,16},{1,9},{9,1},{17,25},{25,17},{2,10},{10... | collective-permute-start | bytes 1769480 | tf_op jit(solution)/shard_map/ppermute | solution.py:471
  41.0 16.3 %collective-permute-start.12 = (bf16[1152,256]{1,0:T(8,128)(2,1)S(1)}, bf16[1152,256]{1,0:T(8,128)(2,1)S(1)}, u32[]{:S(2)}, u32[]{:S(2)}) collective-permute-start(bf16[1152,256]{1,0:T(8,128)(2,1)S(1)} %collective-permute-done.7.refs_8_), channel_id=1, source_target_pairs={{0,16},{8,24},{16,0},{24,8},{1,17},{9,25},{17,1},{25,9},{2,18},{10... | collective-permute-start | bytes 1769480 | tf_op jit(solution)/shard_map/ppermute | solution.py:471
  41.8 18.6 %collective-permute-start.4 = (bf16[1152,256]{1,0:T(8,128)(2,1)S(1)}, bf16[1152,256]{1,0:T(8,128)(2,1)S(1)}, u32[]{:S(2)}, u32[]{:S(2)}) collective-permute-start(bf16[1152,256]{1,0:T(8,128)(2,1)S(1)} %bitcast.14), channel_id=1, source_target_pairs={{0,2},{1,3},{2,4},{3,5},{4,6},{5,7},{6,0},{7,1},{8,10},{9,11},{10,... | collective-permute-start | bytes 1769480 | tf_op jit(solution)/shard_map/ppermute | solution.py:468
  41.9 30.7 %collective-permute-start.8 = (bf16[1152,256]{1,0:T(8,128)(2,1)S(1)}, bf16[1152,256]{1,0:T(8,128)(2,1)S(1)}, u32[]{:S(2)}, u32[]{:S(2)}) collective-permute-start(bf16[1152,256]{1,0:T(8,128)(2,1)S(1)} %collective-permute-done.7.refs_8_), channel_id=1, source_target_pairs={{0,2},{1,3},{2,4},{3,5},{4,6},{5,7},{6,0},{7,1},{8,10},{9,11},{10,... | collective-permute-start | bytes 1769480 | tf_op jit(solution)/shard_map/ppermute | solution.py:468
  44.2 19.3 %collective-permute-start.13 = (bf16[576,256]{1,0:T(8,128)(2,1)S(1)}, bf16[576,256]{1,0:T(8,128)(2,1)S(1)}, u32[]{:S(2)}, u32[]{:S(2)}) collective-permute-start(bf16[576,256]{1,0:T(8,128)(2,1)S(1)} %slice.42), channel_id=1, source_target_pairs={{0,16},{8,24},{16,0},{24,8},{1,17},{9,25},{17,1},{25,9},{2,18},{10... | collective-permute-start | bytes 884744 | tf_op jit(solution)/shard_map/ppermute | solution.py:471
  58.2 7.8 %collective-permute-start.15 = (bf16[576,256]{1,0:T(8,128)(2,1)S(1)}, bf16[576,256]{1,0:T(8,128)(2,1)S(1)}, u32[]{:S(2)}, u32[]{:S(2)}) collective-permute-start(bf16[576,256]{1,0:T(8,128)(2,1)S(1)} %slice.44), channel_id=1, source_target_pairs={{0,8},{8,0},{16,24},{24,16},{1,9},{9,1},{17,25},{25,17},{2,10},{10... | collective-permute-start | bytes 884744 | tf_op jit(solution)/shard_map/ppermute | solution.py:471
  59.8 12.8 %collective-permute-start.16 = (bf16[576,256]{1,0:T(8,128)(2,1)S(1)}, bf16[576,256]{1,0:T(8,128)(2,1)S(1)}, u32[]{:S(2)}, u32[]{:S(2)}) collective-permute-start(bf16[576,256]{1,0:T(8,128)(2,1)S(1)} %slice.45), channel_id=1, source_target_pairs={{0,8},{8,0},{16,24},{24,16},{1,9},{9,1},{17,25},{25,17},{2,10},{10... | collective-permute-start | bytes 884744 | tf_op jit(solution)/shard_map/ppermute | solution.py:471
  60.5 12.1 %collective-permute-start.14 = (bf16[576,256]{1,0:T(8,128)(2,1)S(1)}, bf16[576,256]{1,0:T(8,128)(2,1)S(1)}, u32[]{:S(2)}, u32[]{:S(2)}) collective-permute-start(bf16[576,256]{1,0:T(8,128)(2,1)S(1)} %slice.43), channel_id=1, source_target_pairs={{0,16},{8,24},{16,0},{24,8},{1,17},{9,25},{17,1},{25,9},{2,18},{10... | collective-permute-start | bytes 884744 | tf_op jit(solution)/shard_map/ppermute | solution.py:471
  63.6 19.2 %collective-permute-start.5 = (bf16[1152,256]{1,0:T(8,128)(2,1)S(1)}, bf16[1152,256]{1,0:T(8,128)(2,1)S(1)}, u32[]{:S(2)}, u32[]{:S(2)}) collective-permute-start(bf16[1152,256]{1,0:T(8,128)(2,1)S(1)} %collective-permute-done.4.refs_7_.refs_12_), channel_id=1, source_target_pairs={{0,2},{1,3},{2,4},{3,5},{4,6},{5,7},{6,0},{7,1},{8,10},{9,11},{10,... | collective-permute-start | bytes 1769480 | tf_op jit(solution)/shard_map/ppermute | solution.py:468
  72.6 13.0 %collective-permute-start.17 = (bf16[1152,256]{1,0:T(8,128)(2,1)S(1)}, bf16[1152,256]{1,0:T(8,128)(2,1)S(1)}, u32[]{:S(2)}, u32[]{:S(2)}) collective-permute-start(bf16[1152,256]{1,0:T(8,128)(2,1)S(1)} %collective-permute-done.8.refs_8_), channel_id=1, source_target_pairs={{0,8},{8,0},{16,24},{24,16},{1,9},{9,1},{17,25},{25,17},{2,10},{10... | collective-permute-start | bytes 1769480 | tf_op jit(solution)/shard_map/ppermute | solution.py:471
  73.8 12.4 %collective-permute-start.18 = (bf16[1152,256]{1,0:T(8,128)(2,1)S(1)}, bf16[1152,256]{1,0:T(8,128)(2,1)S(1)}, u32[]{:S(2)}, u32[]{:S(2)}) collective-permute-start(bf16[1152,256]{1,0:T(8,128)(2,1)S(1)} %collective-permute-done.8.refs_8_), channel_id=1, source_target_pairs={{0,16},{8,24},{16,0},{24,8},{1,17},{9,25},{17,1},{25,9},{2,18},{10... | collective-permute-start | bytes 1769480 | tf_op jit(solution)/shard_map/ppermute | solution.py:471
  82.7 14.6 %collective-permute-start.6 = (bf16[1152,256]{1,0:T(8,128)(2,1)S(1)}, bf16[1152,256]{1,0:T(8,128)(2,1)S(1)}, u32[]{:S(2)}, u32[]{:S(2)}) collective-permute-start(bf16[1152,256]{1,0:T(8,128)(2,1)S(1)} %collective-permute-done.5.refs_7_.refs_12_), channel_id=1, source_target_pairs={{0,2},{1,3},{2,4},{3,5},{4,6},{5,7},{6,0},{7,1},{8,10},{9,11},{10,... | collective-permute-start | bytes 1769480 | tf_op jit(solution)/shard_map/ppermute | solution.py:468
  82.8 10.0 %collective-permute-start.21 = (bf16[576,256]{1,0:T(8,128)(2,1)S(1)}, bf16[576,256]{1,0:T(8,128)(2,1)S(1)}, u32[]{:S(2)}, u32[]{:S(2)}) collective-permute-start(bf16[576,256]{1,0:T(8,128)(2,1)S(1)} %slice.58), channel_id=1, source_target_pairs={{0,16},{8,24},{16,0},{24,8},{1,17},{9,25},{17,1},{25,9},{2,18},{10... | collective-permute-start | bytes 884744 | tf_op jit(solution)/shard_map/ppermute | solution.py:471
  84.1 9.5 %collective-permute-start.22 = (bf16[576,256]{1,0:T(8,128)(2,1)S(1)}, bf16[576,256]{1,0:T(8,128)(2,1)S(1)}, u32[]{:S(2)}, u32[]{:S(2)}) collective-permute-start(bf16[576,256]{1,0:T(8,128)(2,1)S(1)} %slice.59), channel_id=1, source_target_pairs={{0,8},{8,0},{16,24},{24,16},{1,9},{9,1},{17,25},{25,17},{2,10},{10... | collective-permute-start | bytes 884744 | tf_op jit(solution)/shard_map/ppermute | solution.py:471
  85.6 11.8 %collective-permute-start.19 = (bf16[576,256]{1,0:T(8,128)(2,1)S(1)}, bf16[576,256]{1,0:T(8,128)(2,1)S(1)}, u32[]{:S(2)}, u32[]{:S(2)}) collective-permute-start(bf16[576,256]{1,0:T(8,128)(2,1)S(1)} %slice.56), channel_id=1, source_target_pairs={{0,16},{8,24},{16,0},{24,8},{1,17},{9,25},{17,1},{25,9},{2,18},{10... | collective-permute-start | bytes 884744 | tf_op jit(solution)/shard_map/ppermute | solution.py:471
  86.3 11.1 %collective-permute-start.20 = (bf16[576,256]{1,0:T(8,128)(2,1)S(1)}, bf16[576,256]{1,0:T(8,128)(2,1)S(1)}, u32[]{:S(2)}, u32[]{:S(2)}) collective-permute-start(bf16[576,256]{1,0:T(8,128)(2,1)S(1)} %slice.57), channel_id=1, source_target_pairs={{0,8},{8,0},{16,24},{24,16},{1,9},{9,1},{17,25},{25,17},{2,10},{10... | collective-permute-start | bytes 884744 | tf_op jit(solution)/shard_map/ppermute | solution.py:471
  100.1 3.4 %collective-permute-start.24 = (f32[264,768]{1,0:T(8,128)S(1)}, f32[264,768]{1,0:T(8,128)S(1)}, u32[]{:S(2)}, u32[]{:S(2)}) collective-permute-start(f32[264,768]{1,0:T(8,128)S(1)} %get-tuple-element.106.cross), channel_id=1, source_target_pairs={{0,1},{1,0},{2,3},{3,2},{4,5},{5,4},{6,7},{7,6},{8,9},{9,8},{10,11... | collective-permute-start | bytes 2433032 | tf_op jit(solution)/shard_map/ppermute | solution.py:465
  100.1 3.3 %collective-permute-start.23 = (f32[128,1280]{1,0:T(8,128)S(1)}, f32[128,1280]{1,0:T(8,128)S(1)}, u32[]{:S(2)}, u32[]{:S(2)}) collective-permute-start(f32[128,1280]{1,0:T(8,128)S(1)} %get-tuple-element.105), channel_id=1, source_target_pairs={{0,1},{1,0},{2,3},{3,2},{4,5},{5,4},{6,7},{7,6},{8,9},{9,8},{10,11... | collective-permute-start | bytes 1966088 | tf_op jit(solution)/shard_map/ppermute | solution.py:465
  100.6 20.3 %collective-permute-start.31 = (bf16[256,1152]{1,0:T(8,128)(2,1)S(1)}, bf16[256,1152]{1,0:T(8,128)(2,1)S(1)}, u32[]{:S(2)}, u32[]{:S(2)}) collective-permute-start(bf16[256,1152]{1,0:T(8,128)(2,1)S(1)} %shard_map.106), channel_id=1, source_target_pairs={{0,6},{1,7},{2,0},{3,1},{4,2},{5,3},{6,4},{7,5},{8,14},{9,15},{10,... | collective-permute-start | bytes 1769480 | tf_op jit(solution)/shard_map/ppermute | solution.py:468
  104.6 1.7 collective-permute-start.27
  106.1 16.0 %collective-permute-start.25 = (f32[128,512]{1,0:T(8,128)S(1)}, f32[128,512]{1,0:T(8,128)S(1)}, u32[]{:S(2)}, u32[]{:S(2)}) collective-permute-start(f32[128,512]{1,0:T(8,128)S(1)} %get-tuple-element.107.refs_1_.refs_7_.refs_3_), channel_id=1, source_target_pairs={{0,1},{1,0},{2,3},{3,2},{4,5},{5,4},{6,7},{7,6},{8,9},{9,8},{10,11... | collective-permute-start | bytes 786440 | tf_op jit(solution)/shard_map/ppermute | solution.py:465
  106.4 14.3 %collective-permute-start.29 = (bf16[128,256]{1,0:T(8,128)(2,1)S(1)}, bf16[128,256]{1,0:T(8,128)(2,1)S(1)}, u32[]{:S(2)}, u32[]{:S(2)}) collective-permute-start(bf16[128,256]{1,0:T(8,128)(2,1)S(1)} %shard_map.112), channel_id=1, source_target_pairs={{8,0},{9,1},{10,2},{11,3},{12,4},{13,5},{14,6},{15,7}} | collective-permute-start | bytes 196616 | tf_op jit(solution)/shard_map/ppermute | solution.py:621
  124.5 10.6 %collective-permute-start.32 = (bf16[256,1152]{1,0:T(8,128)(2,1)}, bf16[256,1152]{1,0:T(8,128)(2,1)S(1)}, u32[]{:S(2)}, u32[]{:S(2)}) collective-permute-start(bf16[256,1152]{1,0:T(8,128)(2,1)} %shard_map.114.refs_5_), channel_id=1, source_target_pairs={{24,16},{16,24},{25,17},{17,25},{26,18},{18,26},{27,19},{19,27},{2... | collective-permute-start | bytes 1769480 | tf_op jit(solution)/shard_map/ppermute | solution.py:680
  125.2 7.9 %collective-permute-start.33 = (bf16[256,256]{1,0:T(8,128)(2,1)S(1)}, bf16[256,256]{1,0:T(8,128)(2,1)S(1)}, u32[]{:S(2)}, u32[]{:S(2)}) collective-permute-start(bf16[256,256]{1,0:T(8,128)(2,1)S(1)} %pad_maximum_fusion.1), channel_id=1, source_target_pairs={{0,6},{1,7},{2,0},{3,1},{4,2},{5,3},{6,4},{7,5},{8,14},{9,15},{10,... | collective-permute-start | bytes 393224 | tf_op jit(solution)/shard_map/ppermute | solution.py:468
  127.7 22.6 %collective-permute-start.36 = (bf16[256,1152]{1,0:T(8,128)(2,1)}, bf16[256,1152]{1,0:T(8,128)(2,1)}, u32[]{:S(2)}, u32[]{:S(2)}) collective-permute-start(bf16[256,1152]{1,0:T(8,128)(2,1)} %shard_map.114.refs_5_), channel_id=1, source_target_pairs={{8,0},{9,1},{10,2},{11,3},{12,4},{13,5},{14,6},{15,7}} | collective-permute-start | bytes 1769480 | tf_op jit(solution)/shard_map/ppermute | solution.py:680
  131.8 27.0 %collective-permute-start.37 = (bf16[256,1152]{1,0:T(8,128)(2,1)}, bf16[256,1152]{1,0:T(8,128)(2,1)}, u32[]{:S(2)}, u32[]{:S(2)}) collective-permute-start(bf16[256,1152]{1,0:T(8,128)(2,1)} %get-tuple-element.117.refs_5_), channel_id=1, source_target_pairs={{24,16},{8,0},{16,24},{25,17},{9,1},{17,25},{26,18},{10,2},{18,26}... | collective-permute-start | bytes 1769480 | tf_op jit(solution)/shard_map/ppermute | solution.py:677
  133.1 17.3 %collective-permute-start.35 = (bf16[1152,256]{1,0:T(8,128)(2,1)}, bf16[1152,256]{1,0:T(8,128)(2,1)}, u32[]{:S(2)}, u32[]{:S(2)}) collective-permute-start(bf16[1152,256]{1,0:T(8,128)(2,1)} %get-tuple-element.121), channel_id=1, source_target_pairs={{0,2},{1,3},{2,4},{3,5},{4,6},{5,7},{6,0},{7,1},{8,10},{9,11},{10,... | collective-permute-start | bytes 1769480 | tf_op jit(solution)/shard_map/ppermute | solution.py:468
  138.4 20.3 %collective-permute-start.34 = (bf16[256,1152]{1,0:T(8,128)(2,1)}, bf16[256,1152]{1,0:T(8,128)(2,1)}, u32[]{:S(2)}, u32[]{:S(2)}) collective-permute-start(bf16[256,1152]{1,0:T(8,128)(2,1)} %add_convert_fusion.4), channel_id=1, source_target_pairs={{24,8},{16,0},{25,9},{17,1},{26,10},{18,2},{27,11},{19,3},{28,12},... | collective-permute-start | bytes 1769480 | tf_op jit(solution)/shard_map/ppermute | solution.py:686
  139.7 30.5 %collective-permute-start.39 = (bf16[256,1152]{1,0:T(8,128)(2,1)}, bf16[256,1152]{1,0:T(8,128)(2,1)S(1)}, u32[]{:S(2)}, u32[]{:S(2)}) collective-permute-start(bf16[256,1152]{1,0:T(8,128)(2,1)} %copy-done.13), channel_id=1, source_target_pairs={{24,16},{8,0},{16,24},{25,17},{9,1},{17,25},{26,18},{10,2},{18,26}... | collective-permute-start | bytes 1769480 | tf_op jit(solution)/shard_map/ppermute | solution.py:677
  151.9 23.0 %collective-permute-start.41 = (bf16[1152,256]{1,0:T(8,128)(2,1)S(1)}, bf16[1152,256]{1,0:T(8,128)(2,1)S(1)}, u32[]{:S(2)}, u32[]{:S(2)}) collective-permute-start(bf16[1152,256]{1,0:T(8,128)(2,1)S(1)} %add_convert_fusion.3), channel_id=1, source_target_pairs={{0,2},{1,3},{2,4},{3,5},{4,6},{5,7},{6,0},{7,1},{8,10},{9,11},{10,... | collective-permute-start | bytes 1769480 | tf_op jit(solution)/shard_map/ppermute | solution.py:468
  160.2 16.3 %collective-permute-start.40 = (bf16[256,1152]{1,0:T(8,128)(2,1)S(1)}, bf16[256,1152]{1,0:T(8,128)(2,1)S(1)}, u32[]{:S(2)}, u32[]{:S(2)}) collective-permute-start(bf16[256,1152]{1,0:T(8,128)(2,1)S(1)} %add_convert_fusion.2), channel_id=1, source_target_pairs={{24,8},{16,0},{25,9},{17,1},{26,10},{18,2},{27,11},{19,3},{28,12},... | collective-permute-start | bytes 1769480 | tf_op jit(solution)/shard_map/ppermute | solution.py:686
  163.9 16.8 %collective-permute-start.43 = (bf16[1152,256]{1,0:T(8,128)(2,1)S(1)}, bf16[1152,256]{1,0:T(8,128)(2,1)S(1)}, u32[]{:S(2)}, u32[]{:S(2)}) collective-permute-start(bf16[1152,256]{1,0:T(8,128)(2,1)S(1)} %get-tuple-element.126), channel_id=1, source_target_pairs={{0,2},{1,3},{2,4},{3,5},{4,6},{5,7},{6,0},{7,1},{8,10},{9,11},{10,... | collective-permute-start | bytes 1769480 | tf_op jit(solution)/shard_map/ppermute | solution.py:468
  170.4 17.5 %collective-permute-start.45 = (bf16[256,1152]{1,0:T(8,128)(2,1)S(1)}, bf16[256,1152]{1,0:T(8,128)(2,1)S(1)}, u32[]{:S(2)}, u32[]{:S(2)}) collective-permute-start(bf16[256,1152]{1,0:T(8,128)(2,1)S(1)} %add_convert_fusion.1), channel_id=1, source_target_pairs={{24,8},{16,0},{25,9},{17,1},{26,10},{18,2},{27,11},{19,3},{28,12},... | collective-permute-start | bytes 1769480 | tf_op jit(solution)/shard_map/ppermute | solution.py:686
  173.6 16.1 %collective-permute-start.38 = (bf16[256,1152]{1,0:T(8,128)(2,1)S(1)}, bf16[256,1152]{1,0:T(8,128)(2,1)S(1)}, u32[]{:S(2)}, u32[]{:S(2)}) collective-permute-start(bf16[256,1152]{1,0:T(8,128)(2,1)S(1)} %get-tuple-element.128.refs_5_), channel_id=1, source_target_pairs={{24,16},{8,0},{16,24},{25,17},{9,1},{17,25},{26,18},{10,2},{18,26}... | collective-permute-start | bytes 1769480 | tf_op jit(solution)/shard_map/ppermute | solution.py:677
  180.8 11.8 %collective-permute-start.44 = (bf16[576,256]{1,0:T(8,128)(2,1)S(1)}, bf16[576,256]{1,0:T(8,128)(2,1)S(1)}, u32[]{:S(2)}, u32[]{:S(2)}) collective-permute-start(bf16[576,256]{1,0:T(8,128)(2,1)S(1)} %get-tuple-element.149), channel_id=1, source_target_pairs={{0,2},{1,3},{2,4},{3,5},{4,6},{5,7},{6,0},{7,1},{8,10},{9,11},{10,... | collective-permute-start | bytes 884744 | tf_op jit(solution)/shard_map/ppermute | solution.py:468
  180.9 15.9 %collective-permute-start.47 = (bf16[576,256]{1,0:T(8,128)(2,1)S(1)}, bf16[576,256]{1,0:T(8,128)(2,1)S(1)}, u32[]{:S(2)}, u32[]{:S(2)}) collective-permute-start(bf16[576,256]{1,0:T(8,128)(2,1)S(1)} %get-tuple-element.148), channel_id=1, source_target_pairs={{0,2},{1,3},{2,4},{3,5},{4,6},{5,7},{6,0},{7,1},{8,10},{9,11},{10,... | collective-permute-start | bytes 884744 | tf_op jit(solution)/shard_map/ppermute | solution.py:468
  188.7 8.4 %collective-permute-start.48 = (bf16[128,3456]{1,0:T(8,128)(2,1)S(1)}, bf16[128,3456]{1,0:T(8,128)(2,1)S(1)}, u32[]{:S(2)}, u32[]{:S(2)}) collective-permute-start(bf16[128,3456]{1,0:T(8,128)(2,1)S(1)} %pad_maximum_fusion), channel_id=1, source_target_pairs={{0,1},{1,0},{2,3},{3,2},{4,5},{5,4},{6,7},{7,6},{8,9},{9,8},{10,11... | collective-permute-start | bytes 2654216 | tf_op jit(solution)/shard_map/ppermute | solution.py:465
  189.9 16.7 %collective-permute-start.42 = (bf16[256,1152]{1,0:T(8,128)(2,1)S(1)}, bf16[256,1152]{1,0:T(8,128)(2,1)S(1)}, u32[]{:S(2)}, u32[]{:S(2)}) collective-permute-start(bf16[256,1152]{1,0:T(8,128)(2,1)S(1)} %add_convert_fusion), channel_id=1, source_target_pairs={{24,8},{16,0},{25,9},{17,1},{26,10},{18,2},{27,11},{19,3},{28,12},... | collective-permute-start | bytes 1769480 | tf_op jit(solution)/shard_map/ppermute | solution.py:686
  192.7 11.8 %collective-permute-start.46 = (bf16[576,256]{1,0:T(8,128)(2,1)S(1)}, bf16[576,256]{1,0:T(8,128)(2,1)S(1)}, u32[]{:S(2)}, u32[]{:S(2)}) collective-permute-start(bf16[576,256]{1,0:T(8,128)(2,1)S(1)} %add_convert_fusion.6), channel_id=1, source_target_pairs={{0,2},{1,3},{2,4},{3,5},{4,6},{5,7},{6,0},{7,1},{8,10},{9,11},{10,... | collective-permute-start | bytes 884744 | tf_op jit(solution)/shard_map/ppermute | solution.py:468
  196.9 12.0 %collective-permute-start.50 = (bf16[576,256]{1,0:T(8,128)(2,1)S(1)}, bf16[576,256]{1,0:T(8,128)(2,1)S(1)}, u32[]{:S(2)}, u32[]{:S(2)}) collective-permute-start(bf16[576,256]{1,0:T(8,128)(2,1)S(1)} %add_convert_fusion.5), channel_id=1, source_target_pairs={{0,2},{1,3},{2,4},{3,5},{4,6},{5,7},{6,0},{7,1},{8,10},{9,11},{10,... | collective-permute-start | bytes 884744 | tf_op jit(solution)/shard_map/ppermute | solution.py:468
  207.4 3.4 %collective-permute-start.49 = (bf16[128,1152]{1,0:T(8,128)(2,1)S(1)}, bf16[128,1152]{1,0:T(8,128)(2,1)S(1)}, u32[]{:S(2)}, u32[]{:S(2)}) collective-permute-start(bf16[128,1152]{1,0:T(8,128)(2,1)S(1)} %get-tuple-element.144), channel_id=1, source_target_pairs={{0,1},{1,0},{2,3},{3,2},{4,5},{5,4},{6,7},{7,6},{8,9},{9,8},{10,11... | collective-permute-start | bytes 884744 | tf_op jit(solution)/shard_map/ppermute | solution.py:465
  (29 other events, 456.6 us)

commit v4 on v3

--- a/solution.py
+++ b/solution.py
@@ -663,9 +663,9 @@
     act_sib = after(act_sib, normed_ahead)
     (terms[1],) = grad_block(1, act)
     act = after(act, terms[1])
-    act_ahead = along(jnp.concatenate([act, act_sib], axis=0), -1)
     terms[2], *down_grads[2] = grad_block(2, act)
-    terms[3], *down_grads[3] = grad_block(3, after(act, act_ahead))
+    terms[3], *down_grads[3] = grad_block(3, act)
+    act_ahead = along(jnp.concatenate(after([act, act_sib], terms[3]), axis=0), -1)
 
     def add(*values):
         return sum(value.astype(F32) for value in values)
@@ -691,7 +691,7 @@
     down_ring = along(down_grads[2][0])
     sums = {1: scan_sum(1, after(opened[1], terms[2], terms[3]))}
     more = {1: scan_more(sums[1])}
-    down_sum = add(after(down_ring, beside), down_grads[3][0]).astype(BF16)
+    down_sum = add(after(down_ring, beside, act_ahead), down_grads[3][0]).astype(BF16)
     down_ring = along(down_sum)
     sums[2] = scan_sum(2, after(opened[2], more[1]))
     more[2] = scan_more(sums[2])

time: 213 us -> 216 us (1.014)
  starting transfers between devices: 44.4 us -> 47.6 us
    ppermute x15, waiting for transfers between devices: 36.9 us -> 47.6 us  [along(): lax.ppermute(value, 'rep', [(r, (r + 2 * steps) % reps) for r in range(re...]
    ppermute x3, waiting for transfers between devices: 14.1 us -> 7.28 us  [scan_open(): return lax.ppermute(terms[index], 'section', [(3, 2), (1, 0), (2, 3)])]
    ppermute x4, waiting for transfers between devices: 10.6 us -> 5.52 us  [scan_more(): return lax.ppermute(value, 'section', [(3, 1), (2, 0)])]
    ppermute x15, starting transfers between devices: 11.1 us -> 14.3 us  [along(): lax.ppermute(value, 'rep', [(r, (r + 2 * steps) % reps) for r in range(re...]
    unnamed x52 -> x48, local copies, waits for them, and re-layouts: 7.79 us -> 7.78 us
  transfers between devices with their start and end apart: 51 -> 51, of which waited for: 27 -> 25; matrix products, arithmetic and copies ran while one was open for 5% -> 5% of each run, Pallas kernels for 16% -> 16%
where the time goes in v4:
time: 216 us; the launch traced here: 215 us
  waiting for transfers between devices  107 us (50%)
  starting transfers between devices  47.6 us (22%)
  Pallas kernels  40.6 us (19%)
  local copies, waits for them, and re-layouts  10.6 us (5%)
  other arithmetic  8.5 us (4%)
    ppermute x15, waiting for transfers between devices, along(): lax.ppermute(value, 'rep', [(r, (r + 2 * steps) % reps) for r in range(re...  47.6 us
    pallas_call x21, Pallas kernels, run_kernel(): pl.pallas_call(body, out_shape=out_shapes, grid_spec=pltpu.PrefetchScalar...  40.6 us
    ppermute x16, waiting for transfers between devices, flip(): lax.ppermute(value, 'section', [(s, s ^ mask) for s in range(sections)])  32.1 us
    ppermute x16, starting transfers between devices, flip(): lax.ppermute(value, 'section', [(s, s ^ mask) for s in range(sections)])  18.1 us
    ppermute x15, starting transfers between devices, along(): lax.ppermute(value, 'rep', [(r, (r + 2 * steps) % reps) for r in range(re...  14.3 us
    ppermute x1, waiting for transfers between devices, per_device(): arrivals += [lax.ppermute(passed, 'section', [(1, 0)])]  13 us
    unnamed x48, local copies, waits for them, and re-layouts  7.78 us
    ppermute x3, waiting for transfers between devices, scan_open(): return lax.ppermute(terms[index], 'section', [(3, 2), (1, 0), (2, 3)])  7.28 us
  transfers between devices with their start and end apart: 51, of which 25 were waited for; matrix products, arithmetic and copies ran while one was open for 5% of the time, Pallas kernels for 16%

profile of v4, /device:TPU:0, one launch (start us, length us, event | category | flops | bytes accessed | tf_op | source)
XLA Modules:
  0.0 215.4 jit_solution(2409191517999375749)
XLA Ops:
  0.6 3.1 %collective-permute-start.2 = (bf16[1152,256]{1,0:T(8,128)(2,1)}, bf16[1152,256]{1,0:T(8,128)(2,1)}, u32[]{:S(2)}, u32[]{:S(2)}) collective-permute-start(bf16[1152,256]{1,0:T(8,128)(2,1)} %bitcast.17), channel_id=1, source_target_pairs={{0,2},{1,3},{2,4},{3,5},{4,6},{5,7},{6,0},{7,1},{8,10},{9,11},{10,... | collective-permute-start | bytes 1769480 | tf_op jit(solution)/shard_map/ppermute | solution.py:468
  3.7 1.5 collective-permute-start
  5.2 1.5 collective-permute-start.1
  7.6 2.3 %copy-done.2 = s32[1,2,64,9216]{3,2,1,0:T(8,128)S(1)} copy-done((s32[1,2,64,9216]{3,2,1,0:T(8,128)S(1)}, s32[1,2,64,9216]{3,2,1,0:T(8,128)}, u32[]{:S(2)}) %copy-start.2) | copy-done | bytes 4718616
  9.9 1.7 copy-done.5
  11.6 1.7 copy-done.6
  13.9 5.7 %shard_map.104 = (bf16[2,128,4608]{2,1,0:T(8,128)(2,1)S(1)}, bf16[2,128,5760]{2,1,0:T(8,128)(2,1)S(1)}, f32[128,256]{1,0:T(8,128)S(1)}) custom-call(s32[8]{0:T(128)S(1)} %pad_add_fusion.blocks.refs_0_, s32[2]{0:T(128)S(1)} %bitcast.21, bf16[2,64,9216]{2,1,0:T(8,128)(2,1)S(1)} %bitcast.12, bf16[2,64,9216]{2,1,0:T(8,128)(2,1)S(1)} %bitcast.13, ...), custom_call_target="tpu_custom_call" | custom-call | tf_op jit(solution)/shard_map/pallas_call | solution.py:165
  21.8 1.4 collective-permute-start.9
  24.1 12.4 %collective-permute-done.10.refs_10_ = bf16[1152,256]{1,0:T(8,128)(2,1)S(1)} collective-permute-done((bf16[1152,256]{1,0:T(8,128)(2,1)}, bf16[1152,256]{1,0:T(8,128)(2,1)S(1)}, u32[]{:S(2)}, u32[]{:S(2)}) %collective-permute-start.10) | collective-permute-done | bytes 589856 | tf_op jit(solution)/shard_map/ppermute | solution.py:471
  37.4 3.0 %collective-permute-done.7.refs_8_ = bf16[1152,256]{1,0:T(8,128)(2,1)S(1)} collective-permute-done((bf16[1152,256]{1,0:T(8,128)(2,1)}, bf16[1152,256]{1,0:T(8,128)(2,1)S(1)}, u32[]{:S(2)}, u32[]{:S(2)}) %collective-permute-start.7) | collective-permute-done | bytes 589856 | tf_op jit(solution)/shard_map/ppermute | solution.py:468
  45.3 9.5 %collective-permute-done.11.refs_9_ = bf16[1152,256]{1,0:T(8,128)(2,1)S(1)} collective-permute-done((bf16[1152,256]{1,0:T(8,128)(2,1)S(1)}, bf16[1152,256]{1,0:T(8,128)(2,1)S(1)}, u32[]{:S(2)}, u32[]{:S(2)}) %collective-permute-start.11) | collective-permute-done | bytes 589856 | tf_op jit(solution)/shard_map/ppermute | solution.py:471
  54.7 2.5 %collective-permute-done.12.refs_10_ = bf16[1152,256]{1,0:T(8,128)(2,1)S(1)} collective-permute-done((bf16[1152,256]{1,0:T(8,128)(2,1)S(1)}, bf16[1152,256]{1,0:T(8,128)(2,1)S(1)}, u32[]{:S(2)}, u32[]{:S(2)}) %collective-permute-start.12) | collective-permute-done | bytes 589856 | tf_op jit(solution)/shard_map/ppermute | solution.py:471
  58.2 1.5 collective-permute-start.15
  61.3 2.2 %collective-permute-done.13.refs_11_ = bf16[576,256]{1,0:T(8,128)(2,1)S(1)} collective-permute-done((bf16[576,256]{1,0:T(8,128)(2,1)S(1)}, bf16[576,256]{1,0:T(8,128)(2,1)S(1)}, u32[]{:S(2)}, u32[]{:S(2)}) %collective-permute-start.13) | collective-permute-done | bytes 294944 | tf_op jit(solution)/shard_map/ppermute | solution.py:471
  63.6 2.5 %collective-permute-done.15.refs_12_ = bf16[576,256]{1,0:T(8,128)(2,1)S(1)} collective-permute-done((bf16[576,256]{1,0:T(8,128)(2,1)S(1)}, bf16[576,256]{1,0:T(8,128)(2,1)S(1)}, u32[]{:S(2)}, u32[]{:S(2)}) %collective-permute-start.15) | collective-permute-done | bytes 294944 | tf_op jit(solution)/shard_map/ppermute | solution.py:471
  66.1 3.5 %shard_map.105 = (f32[128,1280]{1,0:T(8,128)S(1)}, f32[128,1280]{1,0:T(8,128)S(1)}, f32[264,768]{1,0:T(8,128)S(1)}) custom-call(s32[8]{0:T(128)S(1)} %pad_add_fusion.blocks.refs_0_, bf16[2,128,4608]{2,1,0:T(8,128)(2,1)S(1)} %get-tuple-element.76.refs_1_.own, bf16[2,128,5760]{2,1,0:T(8,128)(2,1)S(1)} %collective-permute-done.3.refs_2_.refs_4_.sib.stats_sib, ...), custom_call_target="tpu_custom_call" | custom-call | tf_op jit(solution)/shard_map/pallas_call | solution.py:165
  69.6 3.0 %collective-permute-done.8.refs_8_ = bf16[1152,256]{1,0:T(8,128)(2,1)S(1)} collective-permute-done((bf16[1152,256]{1,0:T(8,128)(2,1)S(1)}, bf16[1152,256]{1,0:T(8,128)(2,1)S(1)}, u32[]{:S(2)}, u32[]{:S(2)}) %collective-permute-start.8) | collective-permute-done | bytes 589856 | tf_op jit(solution)/shard_map/ppermute | solution.py:468
  73.8 1.4 collective-permute-start.18
  75.2 7.5 %collective-permute-done.5.refs_7_.refs_12_ = bf16[1152,256]{1,0:T(8,128)(2,1)S(1)} collective-permute-done((bf16[1152,256]{1,0:T(8,128)(2,1)S(1)}, bf16[1152,256]{1,0:T(8,128)(2,1)S(1)}, u32[]{:S(2)}, u32[]{:S(2)}) %collective-permute-start.5) | collective-permute-done | bytes 589856 | tf_op jit(solution)/shard_map/ppermute | solution.py:468
  84.1 1.5 collective-permute-start.22
  88.1 3.7 %shard_map.107 = (f32[128,1280]{1,0:T(8,128)S(1)}, f32[128,1280]{1,0:T(8,128)S(1)}, f32[264,768]{1,0:T(8,128)S(1)}) custom-call(s32[8]{0:T(128)S(1)} %pad_add_fusion.blocks.refs_0_, bf16[2,128,4608]{2,1,0:T(8,128)(2,1)S(1)} %get-tuple-element.76.refs_1_.own, ...), custom_call_target="tpu_custom_call", output_to_operand_aliasing={{0}: (13, {}), {1}: (14, {}), {2}: (15, {})} | custom-call | tf_op jit(solution)/shard_map/pallas_call | solution.py:165
  93.5 2.7 %shard_map.108 = (f32[128,1280]{1,0:T(8,128)S(1)}, f32[128,1280]{1,0:T(8,128)S(1)}, f32[264,768]{1,0:T(8,128)S(1)}) custom-call(s32[8]{0:T(128)S(1)} %pad_add_fusion.blocks.refs_0_, bf16[2,128,4608]{2,1,0:T(8,128)(2,1)S(1)} %get-tuple-element.76.refs_1_.own, ...), custom_call_target="tpu_custom_call", output_to_operand_aliasing={{0}: (13, {}), {1}: (14, {}), {2}: (15, {})} | custom-call | tf_op jit(solution)/shard_map/pallas_call | solution.py:165
  97.4 2.7 %shard_map.109 = (f32[128,1280]{1,0:T(8,128)S(1)}, f32[128,1280]{1,0:T(8,128)S(1)}, f32[264,768]{1,0:T(8,128)S(1)}) custom-call(s32[8]{0:T(128)S(1)} %pad_add_fusion.blocks.refs_0_, bf16[2,128,4608]{2,1,0:T(8,128)(2,1)S(1)} %get-tuple-element.76.refs_1_.own, ...), custom_call_target="tpu_custom_call", output_to_operand_aliasing={{0}: (13, {}), {1}: (14, {}), {2}: (15, {})} | custom-call | tf_op jit(solution)/shard_map/pallas_call | solution.py:165
  100.6 2.8 %collective-permute-start.31 = (bf16[256,1152]{1,0:T(8,128)(2,1)S(1)}, bf16[256,1152]{1,0:T(8,128)(2,1)S(1)}, u32[]{:S(2)}, u32[]{:S(2)}) collective-permute-start(bf16[256,1152]{1,0:T(8,128)(2,1)S(1)} %shard_map.106), channel_id=1, source_target_pairs={{0,6},{1,7},{2,0},{3,1},{4,2},{5,3},{6,4},{7,5},{8,14},{9,15},{10,... | collective-permute-start | bytes 1769480 | tf_op jit(solution)/shard_map/ppermute | solution.py:468
  107.7 13.0 %collective-permute-done.29.refs_9_ = bf16[128,256]{1,0:T(8,128)(2,1)S(1)} collective-permute-done((bf16[128,256]{1,0:T(8,128)(2,1)S(1)}, bf16[128,256]{1,0:T(8,128)(2,1)S(1)}, u32[]{:S(2)}, u32[]{:S(2)}) %collective-permute-start.29) | collective-permute-done | bytes 65568 | tf_op jit(solution)/shard_map/ppermute | solution.py:621
  122.1 2.4 %shard_map.114.refs_5_ = bf16[256,1152]{1,0:T(8,128)(2,1)} custom-call(s32[8]{0:T(128)S(1)} %pad_add_fusion.blocks.refs_0_, bf16[2,128,4608]{2,1,0:T(8,128)(2,1)S(1)} %get-tuple-element.76.refs_1_.own, bf16[2,128,5760]{2,1,0:T(8,128)(2,1)S(1)} %collective-permute-done.3.refs_2_.refs_4_.sib.stats_sib, ...), custom_call_target="tpu_custom_call" | custom-call | tf_op jit(solution)/shard_map/pallas_call | solution.py:165
  126.5 2.7 %shard_map.115 = (bf16[256,1152]{1,0:T(8,128)(2,1)}, bf16[1152,256]{1,0:T(8,128)(2,1)}) custom-call(s32[8]{0:T(128)S(1)} %pad_add_fusion.blocks.refs_0_, bf16[2,128,4608]{2,1,0:T(8,128)(2,1)S(1)} %get-tuple-element.76.refs_1_.own, bf16[2,128,5760]{2,1,0:T(8,128)(2,1)S(1)} %collective-permute-done.3.refs_2_.refs_4_.sib.stats_sib, ...), custom_call_target="tpu_custom_call" | custom-call | tf_op jit(solution)/shard_map/pallas_call | solution.py:165
  130.6 1.9 shard_map.116
  133.4 3.7 %collective-permute-start.36 = (bf16[256,256]{1,0:T(8,128)(2,1)}, bf16[256,256]{1,0:T(8,128)(2,1)}, u32[]{:S(2)}, u32[]{:S(2)}) collective-permute-start(bf16[256,256]{1,0:T(8,128)(2,1)} %pad_maximum_fusion.1), channel_id=1, source_target_pairs={{0,6},{1,7},{2,0},{3,1},{4,2},{5,3},{6,4},{7,5},{8,14},{9,15},{10,... | collective-permute-start | bytes 393224 | tf_op jit(solution)/shard_map/ppermute | solution.py:468
  137.1 2.0 add_convert_fusion.4
  141.2 10.7 %collective-permute-done.36.act = bf16[256,256]{1,0:T(8,128)(2,1)} collective-permute-done((bf16[256,256]{1,0:T(8,128)(2,1)}, bf16[256,256]{1,0:T(8,128)(2,1)}, u32[]{:S(2)}, u32[]{:S(2)}) %collective-permute-start.36) | collective-permute-done | bytes 131104 | tf_op jit(solution)/shard_map/ppermute | solution.py:468
  153.2 1.5 add_convert_fusion.3
  154.8 1.5 collective-permute-start.41
  157.0 1.4 add_convert_fusion.2
  159.7 2.3 %shard_map.117 = (bf16[128,1152]{1,0:T(8,128)(2,1)S(1)}, bf16[128,1152]{1,0:T(8,128)(2,1)S(1)}, bf16[1152,256]{1,0:T(8,128)(2,1)S(1)}) custom-call(s32[1]{0:T(128)} %bitcast.refs_0_, bf16[2,128,4608]{2,1,0:T(8,128)(2,1)S(1)} %copy-done.1, bf16[2,128,5760]{2,1,0:T(8,128)(2,1)S(1)} %collective-permute-done.3.refs_2_.refs_4_.sib.stats_sib, ...), custom_call_target="tpu_custom_call" | custom-call | tf_op jit(solution)/shard_map/pallas_call | solution.py:165
  162.1 7.3 %collective-permute-done.39.refs_6_ = bf16[256,1152]{1,0:T(8,128)(2,1)S(1)} collective-permute-done((bf16[256,1152]{1,0:T(8,128)(2,1)}, bf16[256,1152]{1,0:T(8,128)(2,1)S(1)}, u32[]{:S(2)}, u32[]{:S(2)}) %collective-permute-start.39) | collective-permute-done | bytes 589856 | tf_op jit(solution)/shard_map/ppermute | solution.py:677
  170.9 1.9 shard_map.118
  174.2 2.3 %collective-permute-done.40.refs_7_ = bf16[256,1152]{1,0:T(8,128)(2,1)S(1)} collective-permute-done((bf16[256,1152]{1,0:T(8,128)(2,1)S(1)}, bf16[256,1152]{1,0:T(8,128)(2,1)S(1)}, u32[]{:S(2)}, u32[]{:S(2)}) %collective-permute-start.40) | collective-permute-done | bytes 589856 | tf_op jit(solution)/shard_map/ppermute | solution.py:686
  176.5 2.0 shard_map.119
  178.5 5.3 %collective-permute-done.43 = bf16[1152,256]{1,0:T(8,128)(2,1)S(1)} collective-permute-done((bf16[1152,256]{1,0:T(8,128)(2,1)S(1)}, bf16[1152,256]{1,0:T(8,128)(2,1)S(1)}, u32[]{:S(2)}, u32[]{:S(2)}) %collective-permute-start.43) | collective-permute-done | bytes 589856 | tf_op jit(solution)/shard_map/ppermute | solution.py:468
  184.6 2.5 %collective-permute-done.45.refs_7_ = bf16[256,1152]{1,0:T(8,128)(2,1)S(1)} collective-permute-done((bf16[256,1152]{1,0:T(8,128)(2,1)S(1)}, bf16[256,1152]{1,0:T(8,128)(2,1)S(1)}, u32[]{:S(2)}, u32[]{:S(2)}) %collective-permute-start.45) | collective-permute-done | bytes 589856 | tf_op jit(solution)/shard_map/ppermute | solution.py:686
  190.8 5.0 %collective-permute-done.44 = bf16[576,256]{1,0:T(8,128)(2,1)S(1)} collective-permute-done((bf16[576,256]{1,0:T(8,128)(2,1)S(1)}, bf16[576,256]{1,0:T(8,128)(2,1)S(1)}, u32[]{:S(2)}, u32[]{:S(2)}) %collective-permute-start.44) | collective-permute-done | bytes 294944 | tf_op jit(solution)/shard_map/ppermute | solution.py:468
  195.9 6.2 %collective-permute-done.47 = bf16[576,256]{1,0:T(8,128)(2,1)S(1)} collective-permute-done((bf16[576,256]{1,0:T(8,128)(2,1)S(1)}, bf16[576,256]{1,0:T(8,128)(2,1)S(1)}, u32[]{:S(2)}, u32[]{:S(2)}) %collective-permute-start.47) | collective-permute-done | bytes 294944 | tf_op jit(solution)/shard_map/ppermute | solution.py:468
  202.4 3.0 %shard_map.121.refs_2_ = bf16[128,9216]{1,0:T(8,128)(2,1)} custom-call(s32[8]{0:T(128)S(1)} %copy-done.22, bf16[128,1152]{1,0:T(8,128)(2,1)S(1)} %get-tuple-element.138.refs_0_, bf16[128,1152]{1,0:T(8,128)(2,1)S(1)} %get-tuple-element.139.refs_1_, bf16[128,1152]{1,0:T(8,128)(2,1)S(1)} %get-tuple-element.140.refs_2_, ...), custom_call_target="tpu_custom_call" | custom-call | tf_op jit(solution)/shard_map/pallas_call | solution.py:165
  205.4 3.0 %collective-permute-done.46 = bf16[576,256]{1,0:T(8,128)(2,1)S(1)} collective-permute-done((bf16[576,256]{1,0:T(8,128)(2,1)S(1)}, bf16[576,256]{1,0:T(8,128)(2,1)S(1)}, u32[]{:S(2)}, u32[]{:S(2)}) %collective-permute-start.46) | collective-permute-done | bytes 294944 | tf_op jit(solution)/shard_map/ppermute | solution.py:468
  209.3 2.8 %collective-permute-done.50 = bf16[576,256]{1,0:T(8,128)(2,1)S(1)} collective-permute-done((bf16[576,256]{1,0:T(8,128)(2,1)S(1)}, bf16[576,256]{1,0:T(8,128)(2,1)S(1)}, u32[]{:S(2)}, u32[]{:S(2)}) %collective-permute-start.50) | collective-permute-done | bytes 294944 | tf_op jit(solution)/shard_map/ppermute | solution.py:468
  212.2 1.7 maximum_bitcast_fusion
  214.0 1.4 shard_map.123
  (147 shorter events, 45.1 us)
Async XLA Ops:
  0.6 19.1 %collective-permute-start.2 = (bf16[1152,256]{1,0:T(8,128)(2,1)}, bf16[1152,256]{1,0:T(8,128)(2,1)}, u32[]{:S(2)}, u32[]{:S(2)}) collective-permute-start(bf16[1152,256]{1,0:T(8,128)(2,1)} %bitcast.17), channel_id=1, source_target_pairs={{0,2},{1,3},{2,4},{3,5},{4,6},{5,7},{6,0},{7,1},{8,10},{9,11},{10,... | collective-permute-start | bytes 1769480 | tf_op jit(solution)/shard_map/ppermute | solution.py:468
  3.7 16.0 %collective-permute-start = (bf16[1152,256]{1,0:T(8,128)(2,1)}, bf16[1152,256]{1,0:T(8,128)(2,1)S(1)}, u32[]{:S(2)}, u32[]{:S(2)}) collective-permute-start(bf16[1152,256]{1,0:T(8,128)(2,1)} %bitcast.18), channel_id=1, source_target_pairs={{0,8},{8,0},{16,24},{24,16},{1,9},{9,1},{17,25},{25,17},{2,10},{10... | collective-permute-start | bytes 1769480 | tf_op jit(solution)/shard_map/ppermute | solution.py:471
  5.2 14.8 %collective-permute-start.1 = (bf16[1152,256]{1,0:T(8,128)(2,1)}, bf16[1152,256]{1,0:T(8,128)(2,1)}, u32[]{:S(2)}, u32[]{:S(2)}) collective-permute-start(bf16[1152,256]{1,0:T(8,128)(2,1)} %bitcast.19), channel_id=1, source_target_pairs={{0,16},{8,24},{16,0},{24,8},{1,17},{9,25},{17,1},{25,9},{2,18},{10... | collective-permute-start | bytes 1769480 | tf_op jit(solution)/shard_map/ppermute | solution.py:471
  20.6 19.8 %collective-permute-start.3 = (bf16[2,128,5760]{2,1,0:T(8,128)(2,1)S(1)}, bf16[2,128,5760]{2,1,0:T(8,128)(2,1)S(1)}, u32[]{:S(2)}, u32[]{:S(2)}) collective-permute-start(bf16[2,128,5760]{2,1,0:T(8,128)(2,1)S(1)} %get-tuple-element.78), channel_id=1, source_target_pairs={{0,1},{1,0},{2,3},{3,2},{4,5},{5,4},{6,7},{7,6},{8,9},{9,8},{10,11... | collective-permute-start | bytes 8847368 | tf_op jit(solution)/shard_map/ppermute | solution.py:465
  20.6 16.0 %collective-permute-start.10 = (bf16[1152,256]{1,0:T(8,128)(2,1)}, bf16[1152,256]{1,0:T(8,128)(2,1)S(1)}, u32[]{:S(2)}, u32[]{:S(2)}) collective-permute-start(bf16[1152,256]{1,0:T(8,128)(2,1)} %collective-permute-done.2.refs_8_), channel_id=1, source_target_pairs={{0,16},{8,24},{16,0},{24,8},{1,17},{9,25},{17,1},{25,9},{2,18},{10... | collective-permute-start | bytes 1769480 | tf_op jit(solution)/shard_map/ppermute | solution.py:471
  21.8 15.7 %collective-permute-start.9 = (bf16[1152,256]{1,0:T(8,128)(2,1)}, bf16[1152,256]{1,0:T(8,128)(2,1)S(1)}, u32[]{:S(2)}, u32[]{:S(2)}) collective-permute-start(bf16[1152,256]{1,0:T(8,128)(2,1)} %collective-permute-done.2.refs_8_), channel_id=1, source_target_pairs={{0,8},{8,0},{16,24},{24,16},{1,9},{9,1},{17,25},{25,17},{2,10},{10... | collective-permute-start | bytes 1769480 | tf_op jit(solution)/shard_map/ppermute | solution.py:471
  23.2 17.2 %collective-permute-start.7 = (bf16[1152,256]{1,0:T(8,128)(2,1)}, bf16[1152,256]{1,0:T(8,128)(2,1)S(1)}, u32[]{:S(2)}, u32[]{:S(2)}) collective-permute-start(bf16[1152,256]{1,0:T(8,128)(2,1)} %collective-permute-done.2.refs_8_), channel_id=1, source_target_pairs={{0,2},{1,3},{2,4},{3,5},{4,6},{5,7},{6,0},{7,1},{8,10},{9,11},{10,... | collective-permute-start | bytes 1769480 | tf_op jit(solution)/shard_map/ppermute | solution.py:468
  40.4 14.3 %collective-permute-start.11 = (bf16[1152,256]{1,0:T(8,128)(2,1)S(1)}, bf16[1152,256]{1,0:T(8,128)(2,1)S(1)}, u32[]{:S(2)}, u32[]{:S(2)}) collective-permute-start(bf16[1152,256]{1,0:T(8,128)(2,1)S(1)} %collective-permute-done.7.refs_8_), channel_id=1, source_target_pairs={{0,8},{8,0},{16,24},{24,16},{1,9},{9,1},{17,25},{25,17},{2,10},{10... | collective-permute-start | bytes 1769480 | tf_op jit(solution)/shard_map/ppermute | solution.py:471
  41.0 16.3 %collective-permute-start.12 = (bf16[1152,256]{1,0:T(8,128)(2,1)S(1)}, bf16[1152,256]{1,0:T(8,128)(2,1)S(1)}, u32[]{:S(2)}, u32[]{:S(2)}) collective-permute-start(bf16[1152,256]{1,0:T(8,128)(2,1)S(1)} %collective-permute-done.7.refs_8_), channel_id=1, source_target_pairs={{0,16},{8,24},{16,0},{24,8},{1,17},{9,25},{17,1},{25,9},{2,18},{10... | collective-permute-start | bytes 1769480 | tf_op jit(solution)/shard_map/ppermute | solution.py:471
  41.8 18.6 %collective-permute-start.4 = (bf16[1152,256]{1,0:T(8,128)(2,1)S(1)}, bf16[1152,256]{1,0:T(8,128)(2,1)S(1)}, u32[]{:S(2)}, u32[]{:S(2)}) collective-permute-start(bf16[1152,256]{1,0:T(8,128)(2,1)S(1)} %bitcast.14), channel_id=1, source_target_pairs={{0,2},{1,3},{2,4},{3,5},{4,6},{5,7},{6,0},{7,1},{8,10},{9,11},{10,... | collective-permute-start | bytes 1769480 | tf_op jit(solution)/shard_map/ppermute | solution.py:468
  41.9 30.7 %collective-permute-start.8 = (bf16[1152,256]{1,0:T(8,128)(2,1)S(1)}, bf16[1152,256]{1,0:T(8,128)(2,1)S(1)}, u32[]{:S(2)}, u32[]{:S(2)}) collective-permute-start(bf16[1152,256]{1,0:T(8,128)(2,1)S(1)} %collective-permute-done.7.refs_8_), channel_id=1, source_target_pairs={{0,2},{1,3},{2,4},{3,5},{4,6},{5,7},{6,0},{7,1},{8,10},{9,11},{10,... | collective-permute-start | bytes 1769480 | tf_op jit(solution)/shard_map/ppermute | solution.py:468
  44.2 19.3 %collective-permute-start.13 = (bf16[576,256]{1,0:T(8,128)(2,1)S(1)}, bf16[576,256]{1,0:T(8,128)(2,1)S(1)}, u32[]{:S(2)}, u32[]{:S(2)}) collective-permute-start(bf16[576,256]{1,0:T(8,128)(2,1)S(1)} %slice.42), channel_id=1, source_target_pairs={{0,16},{8,24},{16,0},{24,8},{1,17},{9,25},{17,1},{25,9},{2,18},{10... | collective-permute-start | bytes 884744 | tf_op jit(solution)/shard_map/ppermute | solution.py:471
  58.2 7.8 %collective-permute-start.15 = (bf16[576,256]{1,0:T(8,128)(2,1)S(1)}, bf16[576,256]{1,0:T(8,128)(2,1)S(1)}, u32[]{:S(2)}, u32[]{:S(2)}) collective-permute-start(bf16[576,256]{1,0:T(8,128)(2,1)S(1)} %slice.44), channel_id=1, source_target_pairs={{0,8},{8,0},{16,24},{24,16},{1,9},{9,1},{17,25},{25,17},{2,10},{10... | collective-permute-start | bytes 884744 | tf_op jit(solution)/shard_map/ppermute | solution.py:471
  59.8 12.8 %collective-permute-start.16 = (bf16[576,256]{1,0:T(8,128)(2,1)S(1)}, bf16[576,256]{1,0:T(8,128)(2,1)S(1)}, u32[]{:S(2)}, u32[]{:S(2)}) collective-permute-start(bf16[576,256]{1,0:T(8,128)(2,1)S(1)} %slice.45), channel_id=1, source_target_pairs={{0,8},{8,0},{16,24},{24,16},{1,9},{9,1},{17,25},{25,17},{2,10},{10... | collective-permute-start | bytes 884744 | tf_op jit(solution)/shard_map/ppermute | solution.py:471
  60.5 12.1 %collective-permute-start.14 = (bf16[576,256]{1,0:T(8,128)(2,1)S(1)}, bf16[576,256]{1,0:T(8,128)(2,1)S(1)}, u32[]{:S(2)}, u32[]{:S(2)}) collective-permute-start(bf16[576,256]{1,0:T(8,128)(2,1)S(1)} %slice.43), channel_id=1, source_target_pairs={{0,16},{8,24},{16,0},{24,8},{1,17},{9,25},{17,1},{25,9},{2,18},{10... | collective-permute-start | bytes 884744 | tf_op jit(solution)/shard_map/ppermute | solution.py:471
  63.6 19.2 %collective-permute-start.5 = (bf16[1152,256]{1,0:T(8,128)(2,1)S(1)}, bf16[1152,256]{1,0:T(8,128)(2,1)S(1)}, u32[]{:S(2)}, u32[]{:S(2)}) collective-permute-start(bf16[1152,256]{1,0:T(8,128)(2,1)S(1)} %collective-permute-done.4.refs_7_.refs_12_), channel_id=1, source_target_pairs={{0,2},{1,3},{2,4},{3,5},{4,6},{5,7},{6,0},{7,1},{8,10},{9,11},{10,... | collective-permute-start | bytes 1769480 | tf_op jit(solution)/shard_map/ppermute | solution.py:468
  72.6 13.0 %collective-permute-start.17 = (bf16[1152,256]{1,0:T(8,128)(2,1)S(1)}, bf16[1152,256]{1,0:T(8,128)(2,1)S(1)}, u32[]{:S(2)}, u32[]{:S(2)}) collective-permute-start(bf16[1152,256]{1,0:T(8,128)(2,1)S(1)} %collective-permute-done.8.refs_8_), channel_id=1, source_target_pairs={{0,8},{8,0},{16,24},{24,16},{1,9},{9,1},{17,25},{25,17},{2,10},{10... | collective-permute-start | bytes 1769480 | tf_op jit(solution)/shard_map/ppermute | solution.py:471
  73.8 12.4 %collective-permute-start.18 = (bf16[1152,256]{1,0:T(8,128)(2,1)S(1)}, bf16[1152,256]{1,0:T(8,128)(2,1)S(1)}, u32[]{:S(2)}, u32[]{:S(2)}) collective-permute-start(bf16[1152,256]{1,0:T(8,128)(2,1)S(1)} %collective-permute-done.8.refs_8_), channel_id=1, source_target_pairs={{0,16},{8,24},{16,0},{24,8},{1,17},{9,25},{17,1},{25,9},{2,18},{10... | collective-permute-start | bytes 1769480 | tf_op jit(solution)/shard_map/ppermute | solution.py:471
  82.7 14.6 %collective-permute-start.6 = (bf16[1152,256]{1,0:T(8,128)(2,1)S(1)}, bf16[1152,256]{1,0:T(8,128)(2,1)S(1)}, u32[]{:S(2)}, u32[]{:S(2)}) collective-permute-start(bf16[1152,256]{1,0:T(8,128)(2,1)S(1)} %collective-permute-done.5.refs_7_.refs_12_), channel_id=1, source_target_pairs={{0,2},{1,3},{2,4},{3,5},{4,6},{5,7},{6,0},{7,1},{8,10},{9,11},{10,... | collective-permute-start | bytes 1769480 | tf_op jit(solution)/shard_map/ppermute | solution.py:468
  82.8 10.0 %collective-permute-start.21 = (bf16[576,256]{1,0:T(8,128)(2,1)S(1)}, bf16[576,256]{1,0:T(8,128)(2,1)S(1)}, u32[]{:S(2)}, u32[]{:S(2)}) collective-permute-start(bf16[576,256]{1,0:T(8,128)(2,1)S(1)} %slice.58), channel_id=1, source_target_pairs={{0,16},{8,24},{16,0},{24,8},{1,17},{9,25},{17,1},{25,9},{2,18},{10... | collective-permute-start | bytes 884744 | tf_op jit(solution)/shard_map/ppermute | solution.py:471
  84.1 9.5 %collective-permute-start.22 = (bf16[576,256]{1,0:T(8,128)(2,1)S(1)}, bf16[576,256]{1,0:T(8,128)(2,1)S(1)}, u32[]{:S(2)}, u32[]{:S(2)}) collective-permute-start(bf16[576,256]{1,0:T(8,128)(2,1)S(1)} %slice.59), channel_id=1, source_target_pairs={{0,8},{8,0},{16,24},{24,16},{1,9},{9,1},{17,25},{25,17},{2,10},{10... | collective-permute-start | bytes 884744 | tf_op jit(solution)/shard_map/ppermute | solution.py:471
  85.6 11.8 %collective-permute-start.19 = (bf16[576,256]{1,0:T(8,128)(2,1)S(1)}, bf16[576,256]{1,0:T(8,128)(2,1)S(1)}, u32[]{:S(2)}, u32[]{:S(2)}) collective-permute-start(bf16[576,256]{1,0:T(8,128)(2,1)S(1)} %slice.56), channel_id=1, source_target_pairs={{0,16},{8,24},{16,0},{24,8},{1,17},{9,25},{17,1},{25,9},{2,18},{10... | collective-permute-start | bytes 884744 | tf_op jit(solution)/shard_map/ppermute | solution.py:471
  86.3 11.1 %collective-permute-start.20 = (bf16[576,256]{1,0:T(8,128)(2,1)S(1)}, bf16[576,256]{1,0:T(8,128)(2,1)S(1)}, u32[]{:S(2)}, u32[]{:S(2)}) collective-permute-start(bf16[576,256]{1,0:T(8,128)(2,1)S(1)} %slice.57), channel_id=1, source_target_pairs={{0,8},{8,0},{16,24},{24,16},{1,9},{9,1},{17,25},{25,17},{2,10},{10... | collective-permute-start | bytes 884744 | tf_op jit(solution)/shard_map/ppermute | solution.py:471
  100.1 3.4 %collective-permute-start.24 = (f32[264,768]{1,0:T(8,128)S(1)}, f32[264,768]{1,0:T(8,128)S(1)}, u32[]{:S(2)}, u32[]{:S(2)}) collective-permute-start(f32[264,768]{1,0:T(8,128)S(1)} %get-tuple-element.107.cross), channel_id=1, source_target_pairs={{0,1},{1,0},{2,3},{3,2},{4,5},{5,4},{6,7},{7,6},{8,9},{9,8},{10,11... | collective-permute-start | bytes 2433032 | tf_op jit(solution)/shard_map/ppermute | solution.py:465
  100.1 3.3 %collective-permute-start.23 = (f32[128,1280]{1,0:T(8,128)S(1)}, f32[128,1280]{1,0:T(8,128)S(1)}, u32[]{:S(2)}, u32[]{:S(2)}) collective-permute-start(f32[128,1280]{1,0:T(8,128)S(1)} %get-tuple-element.106), channel_id=1, source_target_pairs={{0,1},{1,0},{2,3},{3,2},{4,5},{5,4},{6,7},{7,6},{8,9},{9,8},{10,11... | collective-permute-start | bytes 1966088 | tf_op jit(solution)/shard_map/ppermute | solution.py:465
  100.6 20.3 %collective-permute-start.31 = (bf16[256,1152]{1,0:T(8,128)(2,1)S(1)}, bf16[256,1152]{1,0:T(8,128)(2,1)S(1)}, u32[]{:S(2)}, u32[]{:S(2)}) collective-permute-start(bf16[256,1152]{1,0:T(8,128)(2,1)S(1)} %shard_map.106), channel_id=1, source_target_pairs={{0,6},{1,7},{2,0},{3,1},{4,2},{5,3},{6,4},{7,5},{8,14},{9,15},{10,... | collective-permute-start | bytes 1769480 | tf_op jit(solution)/shard_map/ppermute | solution.py:468
  104.6 1.7 collective-permute-start.27
  106.1 16.0 %collective-permute-start.25 = (f32[128,512]{1,0:T(8,128)S(1)}, f32[128,512]{1,0:T(8,128)S(1)}, u32[]{:S(2)}, u32[]{:S(2)}) collective-permute-start(f32[128,512]{1,0:T(8,128)S(1)} %get-tuple-element.108.refs_1_.refs_7_.refs_3_), channel_id=1, source_target_pairs={{0,1},{1,0},{2,3},{3,2},{4,5},{5,4},{6,7},{7,6},{8,9},{9,8},{10,11... | collective-permute-start | bytes 786440 | tf_op jit(solution)/shard_map/ppermute | solution.py:465
  106.4 14.3 %collective-permute-start.29 = (bf16[128,256]{1,0:T(8,128)(2,1)S(1)}, bf16[128,256]{1,0:T(8,128)(2,1)S(1)}, u32[]{:S(2)}, u32[]{:S(2)}) collective-permute-start(bf16[128,256]{1,0:T(8,128)(2,1)S(1)} %shard_map.112), channel_id=1, source_target_pairs={{8,0},{9,1},{10,2},{11,3},{12,4},{13,5},{14,6},{15,7}} | collective-permute-start | bytes 196616 | tf_op jit(solution)/shard_map/ppermute | solution.py:621
  124.5 12.6 %collective-permute-start.32 = (bf16[256,1152]{1,0:T(8,128)(2,1)}, bf16[256,1152]{1,0:T(8,128)(2,1)S(1)}, u32[]{:S(2)}, u32[]{:S(2)}) collective-permute-start(bf16[256,1152]{1,0:T(8,128)(2,1)} %shard_map.114.refs_5_), channel_id=1, source_target_pairs={{24,16},{16,24},{25,17},{17,25},{26,18},{18,26},{27,19},{19,27},{2... | collective-permute-start | bytes 1769480 | tf_op jit(solution)/shard_map/ppermute | solution.py:680
  125.2 28.0 %collective-permute-start.35 = (bf16[256,1152]{1,0:T(8,128)(2,1)}, bf16[256,1152]{1,0:T(8,128)(2,1)}, u32[]{:S(2)}, u32[]{:S(2)}) collective-permute-start(bf16[256,1152]{1,0:T(8,128)(2,1)} %shard_map.114.refs_5_), channel_id=1, source_target_pairs={{8,0},{9,1},{10,2},{11,3},{12,4},{13,5},{14,6},{15,7}} | collective-permute-start | bytes 1769480 | tf_op jit(solution)/shard_map/ppermute | solution.py:680
  129.3 27.0 %collective-permute-start.37 = (bf16[256,1152]{1,0:T(8,128)(2,1)}, bf16[256,1152]{1,0:T(8,128)(2,1)}, u32[]{:S(2)}, u32[]{:S(2)}) collective-permute-start(bf16[256,1152]{1,0:T(8,128)(2,1)} %get-tuple-element.118.refs_5_), channel_id=1, source_target_pairs={{24,16},{8,0},{16,24},{25,17},{9,1},{17,25},{26,18},{10,2},{18,26}... | collective-permute-start | bytes 1769480 | tf_op jit(solution)/shard_map/ppermute | solution.py:677
  132.5 20.7 %collective-permute-start.34 = (bf16[1152,256]{1,0:T(8,128)(2,1)}, bf16[1152,256]{1,0:T(8,128)(2,1)}, u32[]{:S(2)}, u32[]{:S(2)}) collective-permute-start(bf16[1152,256]{1,0:T(8,128)(2,1)} %get-tuple-element.121), channel_id=1, source_target_pairs={{0,2},{1,3},{2,4},{3,5},{4,6},{5,7},{6,0},{7,1},{8,10},{9,11},{10,... | collective-permute-start | bytes 1769480 | tf_op jit(solution)/shard_map/ppermute | solution.py:468
  133.4 18.5 %collective-permute-start.36 = (bf16[256,256]{1,0:T(8,128)(2,1)}, bf16[256,256]{1,0:T(8,128)(2,1)}, u32[]{:S(2)}, u32[]{:S(2)}) collective-permute-start(bf16[256,256]{1,0:T(8,128)(2,1)} %pad_maximum_fusion.1), channel_id=1, source_target_pairs={{0,6},{1,7},{2,0},{3,1},{4,2},{5,3},{6,4},{7,5},{8,14},{9,15},{10,... | collective-permute-start | bytes 393224 | tf_op jit(solution)/shard_map/ppermute | solution.py:468
  139.9 17.0 %collective-permute-start.33 = (bf16[256,1152]{1,0:T(8,128)(2,1)}, bf16[256,1152]{1,0:T(8,128)(2,1)}, u32[]{:S(2)}, u32[]{:S(2)}) collective-permute-start(bf16[256,1152]{1,0:T(8,128)(2,1)} %add_convert_fusion.4), channel_id=1, source_target_pairs={{24,8},{16,0},{25,9},{17,1},{26,10},{18,2},{27,11},{19,3},{28,12},... | collective-permute-start | bytes 1769480 | tf_op jit(solution)/shard_map/ppermute | solution.py:686
  151.9 17.5 %collective-permute-start.39 = (bf16[256,1152]{1,0:T(8,128)(2,1)}, bf16[256,1152]{1,0:T(8,128)(2,1)S(1)}, u32[]{:S(2)}, u32[]{:S(2)}) collective-permute-start(bf16[256,1152]{1,0:T(8,128)(2,1)} %copy-done.13), channel_id=1, source_target_pairs={{24,16},{8,0},{16,24},{25,17},{9,1},{17,25},{26,18},{10,2},{18,26}... | collective-permute-start | bytes 1769480 | tf_op jit(solution)/shard_map/ppermute | solution.py:677
  154.8 19.4 %collective-permute-start.41 = (bf16[1152,256]{1,0:T(8,128)(2,1)S(1)}, bf16[1152,256]{1,0:T(8,128)(2,1)S(1)}, u32[]{:S(2)}, u32[]{:S(2)}) collective-permute-start(bf16[1152,256]{1,0:T(8,128)(2,1)S(1)} %add_convert_fusion.3), channel_id=1, source_target_pairs={{0,2},{1,3},{2,4},{3,5},{4,6},{5,7},{6,0},{7,1},{8,10},{9,11},{10,... | collective-permute-start | bytes 1769480 | tf_op jit(solution)/shard_map/ppermute | solution.py:468
  158.3 18.2 %collective-permute-start.40 = (bf16[256,1152]{1,0:T(8,128)(2,1)S(1)}, bf16[256,1152]{1,0:T(8,128)(2,1)S(1)}, u32[]{:S(2)}, u32[]{:S(2)}) collective-permute-start(bf16[256,1152]{1,0:T(8,128)(2,1)S(1)} %add_convert_fusion.2), channel_id=1, source_target_pairs={{24,8},{16,0},{25,9},{17,1},{26,10},{18,2},{27,11},{19,3},{28,12},... | collective-permute-start | bytes 1769480 | tf_op jit(solution)/shard_map/ppermute | solution.py:686
  162.0 21.8 %collective-permute-start.43 = (bf16[1152,256]{1,0:T(8,128)(2,1)S(1)}, bf16[1152,256]{1,0:T(8,128)(2,1)S(1)}, u32[]{:S(2)}, u32[]{:S(2)}) collective-permute-start(bf16[1152,256]{1,0:T(8,128)(2,1)S(1)} %get-tuple-element.128), channel_id=1, source_target_pairs={{0,2},{1,3},{2,4},{3,5},{4,6},{5,7},{6,0},{7,1},{8,10},{9,11},{10,... | collective-permute-start | bytes 1769480 | tf_op jit(solution)/shard_map/ppermute | solution.py:468
  169.6 17.5 %collective-permute-start.45 = (bf16[256,1152]{1,0:T(8,128)(2,1)S(1)}, bf16[256,1152]{1,0:T(8,128)(2,1)S(1)}, u32[]{:S(2)}, u32[]{:S(2)}) collective-permute-start(bf16[256,1152]{1,0:T(8,128)(2,1)S(1)} %add_convert_fusion.1), channel_id=1, source_target_pairs={{24,8},{16,0},{25,9},{17,1},{26,10},{18,2},{27,11},{19,3},{28,12},... | collective-permute-start | bytes 1769480 | tf_op jit(solution)/shard_map/ppermute | solution.py:686
  172.8 15.2 %collective-permute-start.38 = (bf16[256,1152]{1,0:T(8,128)(2,1)S(1)}, bf16[256,1152]{1,0:T(8,128)(2,1)S(1)}, u32[]{:S(2)}, u32[]{:S(2)}) collective-permute-start(bf16[256,1152]{1,0:T(8,128)(2,1)S(1)} %get-tuple-element.130.refs_5_), channel_id=1, source_target_pairs={{24,16},{8,0},{16,24},{25,17},{9,1},{17,25},{26,18},{10,2},{18,26}... | collective-permute-start | bytes 1769480 | tf_op jit(solution)/shard_map/ppermute | solution.py:677
  184.0 11.8 %collective-permute-start.44 = (bf16[576,256]{1,0:T(8,128)(2,1)S(1)}, bf16[576,256]{1,0:T(8,128)(2,1)S(1)}, u32[]{:S(2)}, u32[]{:S(2)}) collective-permute-start(bf16[576,256]{1,0:T(8,128)(2,1)S(1)} %get-tuple-element.151), channel_id=1, source_target_pairs={{0,2},{1,3},{2,4},{3,5},{4,6},{5,7},{6,0},{7,1},{8,10},{9,11},{10,... | collective-permute-start | bytes 884744 | tf_op jit(solution)/shard_map/ppermute | solution.py:468
  184.3 17.8 %collective-permute-start.47 = (bf16[576,256]{1,0:T(8,128)(2,1)S(1)}, bf16[576,256]{1,0:T(8,128)(2,1)S(1)}, u32[]{:S(2)}, u32[]{:S(2)}) collective-permute-start(bf16[576,256]{1,0:T(8,128)(2,1)S(1)} %get-tuple-element.150), channel_id=1, source_target_pairs={{0,2},{1,3},{2,4},{3,5},{4,6},{5,7},{6,0},{7,1},{8,10},{9,11},{10,... | collective-permute-start | bytes 884744 | tf_op jit(solution)/shard_map/ppermute | solution.py:468
  187.9 14.5 %collective-permute-start.48 = (bf16[128,3456]{1,0:T(8,128)(2,1)S(1)}, bf16[128,3456]{1,0:T(8,128)(2,1)S(1)}, u32[]{:S(2)}, u32[]{:S(2)}) collective-permute-start(bf16[128,3456]{1,0:T(8,128)(2,1)S(1)} %pad_maximum_fusion), channel_id=1, source_target_pairs={{0,1},{1,0},{2,3},{3,2},{4,5},{5,4},{6,7},{7,6},{8,9},{9,8},{10,11... | collective-permute-start | bytes 2654216 | tf_op jit(solution)/shard_map/ppermute | solution.py:465
  188.2 20.2 %collective-permute-start.42 = (bf16[256,1152]{1,0:T(8,128)(2,1)S(1)}, bf16[256,1152]{1,0:T(8,128)(2,1)S(1)}, u32[]{:S(2)}, u32[]{:S(2)}) collective-permute-start(bf16[256,1152]{1,0:T(8,128)(2,1)S(1)} %add_convert_fusion), channel_id=1, source_target_pairs={{24,8},{16,0},{25,9},{17,1},{26,10},{18,2},{27,11},{19,3},{28,12},... | collective-permute-start | bytes 1769480 | tf_op jit(solution)/shard_map/ppermute | solution.py:686
  195.9 12.6 %collective-permute-start.46 = (bf16[576,256]{1,0:T(8,128)(2,1)S(1)}, bf16[576,256]{1,0:T(8,128)(2,1)S(1)}, u32[]{:S(2)}, u32[]{:S(2)}) collective-permute-start(bf16[576,256]{1,0:T(8,128)(2,1)S(1)} %add_convert_fusion.6), channel_id=1, source_target_pairs={{0,2},{1,3},{2,4},{3,5},{4,6},{5,7},{6,0},{7,1},{8,10},{9,11},{10,... | collective-permute-start | bytes 884744 | tf_op jit(solution)/shard_map/ppermute | solution.py:468
  202.2 9.9 %collective-permute-start.50 = (bf16[576,256]{1,0:T(8,128)(2,1)S(1)}, bf16[576,256]{1,0:T(8,128)(2,1)S(1)}, u32[]{:S(2)}, u32[]{:S(2)}) collective-permute-start(bf16[576,256]{1,0:T(8,128)(2,1)S(1)} %add_convert_fusion.5), channel_id=1, source_target_pairs={{0,2},{1,3},{2,4},{3,5},{4,6},{5,7},{6,0},{7,1},{8,10},{9,11},{10,... | collective-permute-start | bytes 884744 | tf_op jit(solution)/shard_map/ppermute | solution.py:468
  209.2 4.7 %collective-permute-start.49 = (bf16[128,1152]{1,0:T(8,128)(2,1)S(1)}, bf16[128,1152]{1,0:T(8,128)(2,1)S(1)}, u32[]{:S(2)}, u32[]{:S(2)}) collective-permute-start(bf16[128,1152]{1,0:T(8,128)(2,1)S(1)} %get-tuple-element.146), channel_id=1, source_target_pairs={{0,1},{1,0},{2,3},{3,2},{4,5},{5,4},{6,7},{7,6},{8,9},{9,8},{10,11... | collective-permute-start | bytes 884744 | tf_op jit(solution)/shard_map/ppermute | solution.py:465
  (27 other events, 440.6 us)

commit v5 on v4

--- a/solution.py
+++ b/solution.py
@@ -665,7 +665,6 @@
     act = after(act, terms[1])
     terms[2], *down_grads[2] = grad_block(2, act)
     terms[3], *down_grads[3] = grad_block(3, act)
-    act_ahead = along(jnp.concatenate(after([act, act_sib], terms[3]), axis=0), -1)
 
     def add(*values):
         return sum(value.astype(F32) for value in values)
@@ -691,9 +690,10 @@
     down_ring = along(down_grads[2][0])
     sums = {1: scan_sum(1, after(opened[1], terms[2], terms[3]))}
     more = {1: scan_more(sums[1])}
-    down_sum = add(after(down_ring, beside, act_ahead), down_grads[3][0]).astype(BF16)
+    act_ahead = along(jnp.concatenate(after([act, act_sib], sums[1]), axis=0), -1)
+    down_sum = add(after(down_ring, beside), down_grads[3][0]).astype(BF16)
     down_ring = along(down_sum)
-    sums[2] = scan_sum(2, after(opened[2], more[1]))
+    sums[2] = scan_sum(2, after(opened[2], more[1], act_ahead))
     more[2] = scan_more(sums[2])
     mines[1], theirs[1], up_grads[1] = close_block(
         1, (opened[1], after(more[1], down_sum, sums[2]), beside)

time: 216 us -> 224 us (1.037)
  waiting for transfers between devices: 107 us -> 121 us
  other arithmetic: 8.5 us -> 4.42 us
  local copies, waits for them, and re-layouts: 10.6 us -> 14.1 us
  Pallas kernels: 40.6 us -> 37.5 us
  starting transfers between devices: 47.6 us -> 45 us
    ppermute x15, waiting for transfers between devices: 47.6 us -> 68.1 us  [along(): lax.ppermute(value, 'rep', [(r, (r + 2 * steps) % reps) for r in range(re...]
    ppermute x3, waiting for transfers between devices: 7.28 us -> 2.58 us  [scan_open(): return lax.ppermute(terms[index], 'section', [(3, 2), (1, 0), (2, 3)])]
    unnamed x48 -> x52, local copies, waits for them, and re-layouts: 7.78 us -> 11.3 us
    ppermute x15, starting transfers between devices: 14.3 us -> 10.8 us  [along(): lax.ppermute(value, 'rep', [(r, (r + 2 * steps) % reps) for r in range(re...]
    pallas_call x21, Pallas kernels: 40.6 us -> 37.5 us  [run_kernel(): pl.pallas_call(body, out_shape=out_shapes, grid_spec=pltpu.PrefetchScalar...]
  transfers between devices with their start and end apart: 51 -> 51, of which waited for: 25 -> 24; matrix products, arithmetic and copies ran while one was open for 5% -> 3% of each run, Pallas kernels for 16% -> 14%
where the time goes in v5:
time: 224 us; the launch traced here: 223 us
  waiting for transfers between devices  121 us (54%)
  starting transfers between devices  45 us (20%)
  Pallas kernels  37.5 us (17%)
  local copies, waits for them, and re-layouts  14.1 us (6%)
  other arithmetic  4.42 us (2%)
    ppermute x15, waiting for transfers between devices, along(): lax.ppermute(value, 'rep', [(r, (r + 2 * steps) % reps) for r in range(re...  68.1 us
    pallas_call x21, Pallas kernels, run_kernel(): pl.pallas_call(body, out_shape=out_shapes, grid_spec=pltpu.PrefetchScalar...  37.5 us
    ppermute x16, waiting for transfers between devices, flip(): lax.ppermute(value, 'section', [(s, s ^ mask) for s in range(sections)])  32.1 us
    ppermute x16, starting transfers between devices, flip(): lax.ppermute(value, 'section', [(s, s ^ mask) for s in range(sections)])  18.1 us
    ppermute x1, waiting for transfers between devices, per_device(): arrivals += [lax.ppermute(passed, 'section', [(1, 0)])]  13 us
    unnamed x52, local copies, waits for them, and re-layouts  11.3 us
    ppermute x15, starting transfers between devices, along(): lax.ppermute(value, 'rep', [(r, (r + 2 * steps) % reps) for r in range(re...  10.8 us
    ppermute x4, starting transfers between devices, scan_more(): return lax.ppermute(value, 'section', [(3, 1), (2, 0)])  5.17 us
  transfers between devices with their start and end apart: 51, of which 24 were waited for; matrix products, arithmetic and copies ran while one was open for 3% of the time, Pallas kernels for 14%

profile of v5, /device:TPU:0, one launch (start us, length us, event | category | flops | bytes accessed | tf_op | source)
XLA Modules:
  0.0 223.0 jit_solution(17708980013043141675)
XLA Ops:
  0.6 3.1 %collective-permute-start.2 = (bf16[1152,256]{1,0:T(8,128)(2,1)}, bf16[1152,256]{1,0:T(8,128)(2,1)}, u32[]{:S(2)}, u32[]{:S(2)}) collective-permute-start(bf16[1152,256]{1,0:T(8,128)(2,1)} %bitcast.17), channel_id=1, source_target_pairs={{0,2},{1,3},{2,4},{3,5},{4,6},{5,7},{6,0},{7,1},{8,10},{9,11},{10,... | collective-permute-start | bytes 1769480 | tf_op jit(solution)/shard_map/ppermute | solution.py:468
  3.7 1.5 collective-permute-start
  5.2 1.5 collective-permute-start.1
  7.6 2.3 %copy-done.3 = s32[1,2,64,9216]{3,2,1,0:T(8,128)S(1)} copy-done((s32[1,2,64,9216]{3,2,1,0:T(8,128)S(1)}, s32[1,2,64,9216]{3,2,1,0:T(8,128)}, u32[]{:S(2)}) %copy-start.3) | copy-done | bytes 4718616
  9.9 1.7 copy-done.7
  11.6 1.7 copy-done.8
  13.9 5.7 %shard_map.104 = (bf16[2,128,4608]{2,1,0:T(8,128)(2,1)S(1)}, bf16[2,128,5760]{2,1,0:T(8,128)(2,1)S(1)}, f32[128,256]{1,0:T(8,128)S(1)}) custom-call(s32[8]{0:T(128)S(1)} %pad_add_fusion.blocks.refs_0_, s32[2]{0:T(128)S(1)} %bitcast.21, bf16[2,64,9216]{2,1,0:T(8,128)(2,1)S(1)} %bitcast.12, bf16[2,64,9216]{2,1,0:T(8,128)(2,1)S(1)} %bitcast.13, ...), custom_call_target="tpu_custom_call" | custom-call | tf_op jit(solution)/shard_map/pallas_call | solution.py:165
  21.8 1.4 collective-permute-start.9
  24.1 12.4 %collective-permute-done.10.refs_10_ = bf16[1152,256]{1,0:T(8,128)(2,1)S(1)} collective-permute-done((bf16[1152,256]{1,0:T(8,128)(2,1)}, bf16[1152,256]{1,0:T(8,128)(2,1)S(1)}, u32[]{:S(2)}, u32[]{:S(2)}) %collective-permute-start.10) | collective-permute-done | bytes 589856 | tf_op jit(solution)/shard_map/ppermute | solution.py:471
  37.4 3.0 %collective-permute-done.7.refs_8_ = bf16[1152,256]{1,0:T(8,128)(2,1)S(1)} collective-permute-done((bf16[1152,256]{1,0:T(8,128)(2,1)}, bf16[1152,256]{1,0:T(8,128)(2,1)S(1)}, u32[]{:S(2)}, u32[]{:S(2)}) %collective-permute-start.7) | collective-permute-done | bytes 589856 | tf_op jit(solution)/shard_map/ppermute | solution.py:468
  41.9 1.3 collective-permute-start.8
  45.3 9.5 %collective-permute-done.11.refs_9_ = bf16[1152,256]{1,0:T(8,128)(2,1)S(1)} collective-permute-done((bf16[1152,256]{1,0:T(8,128)(2,1)S(1)}, bf16[1152,256]{1,0:T(8,128)(2,1)S(1)}, u32[]{:S(2)}, u32[]{:S(2)}) %collective-permute-start.11) | collective-permute-done | bytes 589856 | tf_op jit(solution)/shard_map/ppermute | solution.py:471
  54.7 2.5 %collective-permute-done.12.refs_10_ = bf16[1152,256]{1,0:T(8,128)(2,1)S(1)} collective-permute-done((bf16[1152,256]{1,0:T(8,128)(2,1)S(1)}, bf16[1152,256]{1,0:T(8,128)(2,1)S(1)}, u32[]{:S(2)}, u32[]{:S(2)}) %collective-permute-start.12) | collective-permute-done | bytes 589856 | tf_op jit(solution)/shard_map/ppermute | solution.py:471
  58.2 1.5 collective-permute-start.15
  61.3 2.2 %collective-permute-done.13.refs_11_ = bf16[576,256]{1,0:T(8,128)(2,1)S(1)} collective-permute-done((bf16[576,256]{1,0:T(8,128)(2,1)S(1)}, bf16[576,256]{1,0:T(8,128)(2,1)S(1)}, u32[]{:S(2)}, u32[]{:S(2)}) %collective-permute-start.13) | collective-permute-done | bytes 294944 | tf_op jit(solution)/shard_map/ppermute | solution.py:471
  63.6 2.5 %collective-permute-done.15.refs_12_ = bf16[576,256]{1,0:T(8,128)(2,1)S(1)} collective-permute-done((bf16[576,256]{1,0:T(8,128)(2,1)S(1)}, bf16[576,256]{1,0:T(8,128)(2,1)S(1)}, u32[]{:S(2)}, u32[]{:S(2)}) %collective-permute-start.15) | collective-permute-done | bytes 294944 | tf_op jit(solution)/shard_map/ppermute | solution.py:471
  66.1 3.5 %shard_map.105 = (f32[128,1280]{1,0:T(8,128)S(1)}, f32[128,1280]{1,0:T(8,128)S(1)}, f32[264,768]{1,0:T(8,128)S(1)}) custom-call(s32[8]{0:T(128)S(1)} %pad_add_fusion.blocks.refs_0_, bf16[2,128,4608]{2,1,0:T(8,128)(2,1)S(1)} %get-tuple-element.76.refs_1_.own, bf16[2,128,5760]{2,1,0:T(8,128)(2,1)S(1)} %collective-permute-done.3.refs_2_.refs_4_.sib.stats_sib, ...), custom_call_target="tpu_custom_call" | custom-call | tf_op jit(solution)/shard_map/pallas_call | solution.py:165
  69.6 3.0 %collective-permute-done.8.refs_8_ = bf16[1152,256]{1,0:T(8,128)(2,1)S(1)} collective-permute-done((bf16[1152,256]{1,0:T(8,128)(2,1)S(1)}, bf16[1152,256]{1,0:T(8,128)(2,1)S(1)}, u32[]{:S(2)}, u32[]{:S(2)}) %collective-permute-start.8) | collective-permute-done | bytes 589856 | tf_op jit(solution)/shard_map/ppermute | solution.py:468
  73.8 1.4 collective-permute-start.18
  75.2 7.5 %collective-permute-done.5.refs_7_.refs_12_ = bf16[1152,256]{1,0:T(8,128)(2,1)S(1)} collective-permute-done((bf16[1152,256]{1,0:T(8,128)(2,1)S(1)}, bf16[1152,256]{1,0:T(8,128)(2,1)S(1)}, u32[]{:S(2)}, u32[]{:S(2)}) %collective-permute-start.5) | collective-permute-done | bytes 589856 | tf_op jit(solution)/shard_map/ppermute | solution.py:468
  84.1 1.5 collective-permute-start.22
  88.1 3.8 %shard_map.107 = (f32[128,1280]{1,0:T(8,128)S(1)}, f32[128,1280]{1,0:T(8,128)S(1)}, f32[264,768]{1,0:T(8,128)S(1)}) custom-call(s32[8]{0:T(128)S(1)} %pad_add_fusion.blocks.refs_0_, bf16[2,128,4608]{2,1,0:T(8,128)(2,1)S(1)} %get-tuple-element.76.refs_1_.own, ...), custom_call_target="tpu_custom_call", output_to_operand_aliasing={{0}: (13, {}), {1}: (14, {}), {2}: (15, {})} | custom-call | tf_op jit(solution)/shard_map/pallas_call | solution.py:165
  93.5 2.7 %shard_map.108 = (f32[128,1280]{1,0:T(8,128)S(1)}, f32[128,1280]{1,0:T(8,128)S(1)}, f32[264,768]{1,0:T(8,128)S(1)}) custom-call(s32[8]{0:T(128)S(1)} %pad_add_fusion.blocks.refs_0_, bf16[2,128,4608]{2,1,0:T(8,128)(2,1)S(1)} %get-tuple-element.76.refs_1_.own, ...), custom_call_target="tpu_custom_call", output_to_operand_aliasing={{0}: (13, {}), {1}: (14, {}), {2}: (15, {})} | custom-call | tf_op jit(solution)/shard_map/pallas_call | solution.py:165
  97.4 2.7 %shard_map.109 = (f32[128,1280]{1,0:T(8,128)S(1)}, f32[128,1280]{1,0:T(8,128)S(1)}, f32[264,768]{1,0:T(8,128)S(1)}) custom-call(s32[8]{0:T(128)S(1)} %pad_add_fusion.blocks.refs_0_, bf16[2,128,4608]{2,1,0:T(8,128)(2,1)S(1)} %get-tuple-element.76.refs_1_.own, ...), custom_call_target="tpu_custom_call", output_to_operand_aliasing={{0}: (13, {}), {1}: (14, {}), {2}: (15, {})} | custom-call | tf_op jit(solution)/shard_map/pallas_call | solution.py:165
  100.7 2.8 %collective-permute-start.31 = (bf16[256,1152]{1,0:T(8,128)(2,1)S(1)}, bf16[256,1152]{1,0:T(8,128)(2,1)S(1)}, u32[]{:S(2)}, u32[]{:S(2)}) collective-permute-start(bf16[256,1152]{1,0:T(8,128)(2,1)S(1)} %shard_map.106), channel_id=1, source_target_pairs={{0,6},{1,7},{2,0},{3,1},{4,2},{5,3},{6,4},{7,5},{8,14},{9,15},{10,... | collective-permute-start | bytes 1769480 | tf_op jit(solution)/shard_map/ppermute | solution.py:468
  107.8 13.0 %collective-permute-done.29.refs_9_ = bf16[128,256]{1,0:T(8,128)(2,1)S(1)} collective-permute-done((bf16[128,256]{1,0:T(8,128)(2,1)S(1)}, bf16[128,256]{1,0:T(8,128)(2,1)S(1)}, u32[]{:S(2)}, u32[]{:S(2)}) %collective-permute-start.29) | collective-permute-done | bytes 65568 | tf_op jit(solution)/shard_map/ppermute | solution.py:621
  122.2 2.3 %shard_map.114.refs_5_ = bf16[256,1152]{1,0:T(8,128)(2,1)} custom-call(s32[8]{0:T(128)S(1)} %pad_add_fusion.blocks.refs_0_, bf16[2,128,4608]{2,1,0:T(8,128)(2,1)S(1)} %get-tuple-element.76.refs_1_.own, bf16[2,128,5760]{2,1,0:T(8,128)(2,1)S(1)} %collective-permute-done.3.refs_2_.refs_4_.sib.stats_sib, ...), custom_call_target="tpu_custom_call" | custom-call | tf_op jit(solution)/shard_map/pallas_call | solution.py:165
  124.6 1.5 collective-permute-start.32
  127.4 1.7 copy-done.1
  131.7 1.9 shard_map.115
  133.6 1.3 collective-permute-start.36
  135.0 1.9 shard_map.116
  138.2 1.4 add_convert_fusion.4
  141.0 11.2 %collective-permute-done.34 = bf16[1152,256]{1,0:T(8,128)(2,1)S(1)} collective-permute-done((bf16[1152,256]{1,0:T(8,128)(2,1)S(1)}, bf16[1152,256]{1,0:T(8,128)(2,1)S(1)}, u32[]{:S(2)}, u32[]{:S(2)}) %collective-permute-start.34) | collective-permute-done | bytes 589856 | tf_op jit(solution)/shard_map/ppermute | solution.py:468
  153.0 1.4 collective-permute-start.41
  154.4 2.6 %collective-permute-done.36.refs_6_ = bf16[256,1152]{1,0:T(8,128)(2,1)S(1)} collective-permute-done((bf16[256,1152]{1,0:T(8,128)(2,1)S(1)}, bf16[256,1152]{1,0:T(8,128)(2,1)S(1)}, u32[]{:S(2)}, u32[]{:S(2)}) %collective-permute-start.36) | collective-permute-done | bytes 589856 | tf_op jit(solution)/shard_map/ppermute | solution.py:676
  157.0 19.1 %collective-permute-done.37.act = bf16[256,256]{1,0:T(8,128)(2,1)S(1)} collective-permute-done((bf16[256,256]{1,0:T(8,128)(2,1)S(1)}, bf16[256,256]{1,0:T(8,128)(2,1)S(1)}, u32[]{:S(2)}, u32[]{:S(2)}) %collective-permute-start.37) | collective-permute-done | bytes 131104 | tf_op jit(solution)/shard_map/ppermute | solution.py:468
  177.6 2.1 shard_map.117
  181.2 1.9 shard_map.118
  184.4 3.6 %collective-permute-done.40.refs_7_ = bf16[256,1152]{1,0:T(8,128)(2,1)S(1)} collective-permute-done((bf16[256,1152]{1,0:T(8,128)(2,1)S(1)}, bf16[256,1152]{1,0:T(8,128)(2,1)S(1)}, u32[]{:S(2)}, u32[]{:S(2)}) %collective-permute-start.40) | collective-permute-done | bytes 589856 | tf_op jit(solution)/shard_map/ppermute | solution.py:685
  188.8 6.4 %collective-permute-done.43 = bf16[1152,256]{1,0:T(8,128)(2,1)S(1)} collective-permute-done((bf16[1152,256]{1,0:T(8,128)(2,1)S(1)}, bf16[1152,256]{1,0:T(8,128)(2,1)S(1)}, u32[]{:S(2)}, u32[]{:S(2)}) %collective-permute-start.43) | collective-permute-done | bytes 589856 | tf_op jit(solution)/shard_map/ppermute | solution.py:468
  198.5 5.7 %collective-permute-done.44 = bf16[576,256]{1,0:T(8,128)(2,1)S(1)} collective-permute-done((bf16[576,256]{1,0:T(8,128)(2,1)S(1)}, bf16[576,256]{1,0:T(8,128)(2,1)S(1)}, u32[]{:S(2)}, u32[]{:S(2)}) %collective-permute-start.44) | collective-permute-done | bytes 294944 | tf_op jit(solution)/shard_map/ppermute | solution.py:468
  204.3 6.2 %collective-permute-done.47 = bf16[576,256]{1,0:T(8,128)(2,1)S(1)} collective-permute-done((bf16[576,256]{1,0:T(8,128)(2,1)S(1)}, bf16[576,256]{1,0:T(8,128)(2,1)S(1)}, u32[]{:S(2)}, u32[]{:S(2)}) %collective-permute-start.47) | collective-permute-done | bytes 294944 | tf_op jit(solution)/shard_map/ppermute | solution.py:468
  210.8 3.0 %shard_map.121.refs_2_ = bf16[128,9216]{1,0:T(8,128)(2,1)} custom-call(s32[8]{0:T(128)S(1)} %copy-done.24, bf16[128,1152]{1,0:T(8,128)(2,1)S(1)} %get-tuple-element.138.refs_0_, bf16[128,1152]{1,0:T(8,128)(2,1)S(1)} %get-tuple-element.139.refs_1_, bf16[128,1152]{1,0:T(8,128)(2,1)S(1)} %get-tuple-element.140.refs_2_, ...), custom_call_target="tpu_custom_call" | custom-call | tf_op jit(solution)/shard_map/pallas_call | solution.py:165
  213.8 2.8 %collective-permute-done.46 = bf16[576,256]{1,0:T(8,128)(2,1)S(1)} collective-permute-done((bf16[576,256]{1,0:T(8,128)(2,1)S(1)}, bf16[576,256]{1,0:T(8,128)(2,1)S(1)}, u32[]{:S(2)}, u32[]{:S(2)}) %collective-permute-start.46) | collective-permute-done | bytes 294944 | tf_op jit(solution)/shard_map/ppermute | solution.py:468
  217.4 2.3 %collective-permute-done.50 = bf16[576,256]{1,0:T(8,128)(2,1)S(1)} collective-permute-done((bf16[576,256]{1,0:T(8,128)(2,1)S(1)}, bf16[576,256]{1,0:T(8,128)(2,1)S(1)}, u32[]{:S(2)}, u32[]{:S(2)}) %collective-permute-start.50) | collective-permute-done | bytes 294944 | tf_op jit(solution)/shard_map/ppermute | solution.py:468
  219.8 1.7 maximum_bitcast_fusion
  221.6 1.4 shard_map.123
  (151 shorter events, 42.6 us)
Async XLA Ops:
  0.6 19.1 %collective-permute-start.2 = (bf16[1152,256]{1,0:T(8,128)(2,1)}, bf16[1152,256]{1,0:T(8,128)(2,1)}, u32[]{:S(2)}, u32[]{:S(2)}) collective-permute-start(bf16[1152,256]{1,0:T(8,128)(2,1)} %bitcast.17), channel_id=1, source_target_pairs={{0,2},{1,3},{2,4},{3,5},{4,6},{5,7},{6,0},{7,1},{8,10},{9,11},{10,... | collective-permute-start | bytes 1769480 | tf_op jit(solution)/shard_map/ppermute | solution.py:468
  3.7 16.0 %collective-permute-start = (bf16[1152,256]{1,0:T(8,128)(2,1)}, bf16[1152,256]{1,0:T(8,128)(2,1)S(1)}, u32[]{:S(2)}, u32[]{:S(2)}) collective-permute-start(bf16[1152,256]{1,0:T(8,128)(2,1)} %bitcast.18), channel_id=1, source_target_pairs={{0,8},{8,0},{16,24},{24,16},{1,9},{9,1},{17,25},{25,17},{2,10},{10... | collective-permute-start | bytes 1769480 | tf_op jit(solution)/shard_map/ppermute | solution.py:471
  5.2 14.8 %collective-permute-start.1 = (bf16[1152,256]{1,0:T(8,128)(2,1)}, bf16[1152,256]{1,0:T(8,128)(2,1)}, u32[]{:S(2)}, u32[]{:S(2)}) collective-permute-start(bf16[1152,256]{1,0:T(8,128)(2,1)} %bitcast.19), channel_id=1, source_target_pairs={{0,16},{8,24},{16,0},{24,8},{1,17},{9,25},{17,1},{25,9},{2,18},{10... | collective-permute-start | bytes 1769480 | tf_op jit(solution)/shard_map/ppermute | solution.py:471
  20.6 19.8 %collective-permute-start.3 = (bf16[2,128,5760]{2,1,0:T(8,128)(2,1)S(1)}, bf16[2,128,5760]{2,1,0:T(8,128)(2,1)S(1)}, u32[]{:S(2)}, u32[]{:S(2)}) collective-permute-start(bf16[2,128,5760]{2,1,0:T(8,128)(2,1)S(1)} %get-tuple-element.78), channel_id=1, source_target_pairs={{0,1},{1,0},{2,3},{3,2},{4,5},{5,4},{6,7},{7,6},{8,9},{9,8},{10,11... | collective-permute-start | bytes 8847368 | tf_op jit(solution)/shard_map/ppermute | solution.py:465
  20.6 16.0 %collective-permute-start.10 = (bf16[1152,256]{1,0:T(8,128)(2,1)}, bf16[1152,256]{1,0:T(8,128)(2,1)S(1)}, u32[]{:S(2)}, u32[]{:S(2)}) collective-permute-start(bf16[1152,256]{1,0:T(8,128)(2,1)} %collective-permute-done.2.refs_8_), channel_id=1, source_target_pairs={{0,16},{8,24},{16,0},{24,8},{1,17},{9,25},{17,1},{25,9},{2,18},{10... | collective-permute-start | bytes 1769480 | tf_op jit(solution)/shard_map/ppermute | solution.py:471
  21.8 15.7 %collective-permute-start.9 = (bf16[1152,256]{1,0:T(8,128)(2,1)}, bf16[1152,256]{1,0:T(8,128)(2,1)S(1)}, u32[]{:S(2)}, u32[]{:S(2)}) collective-permute-start(bf16[1152,256]{1,0:T(8,128)(2,1)} %collective-permute-done.2.refs_8_), channel_id=1, source_target_pairs={{0,8},{8,0},{16,24},{24,16},{1,9},{9,1},{17,25},{25,17},{2,10},{10... | collective-permute-start | bytes 1769480 | tf_op jit(solution)/shard_map/ppermute | solution.py:471
  23.2 17.2 %collective-permute-start.7 = (bf16[1152,256]{1,0:T(8,128)(2,1)}, bf16[1152,256]{1,0:T(8,128)(2,1)S(1)}, u32[]{:S(2)}, u32[]{:S(2)}) collective-permute-start(bf16[1152,256]{1,0:T(8,128)(2,1)} %collective-permute-done.2.refs_8_), channel_id=1, source_target_pairs={{0,2},{1,3},{2,4},{3,5},{4,6},{5,7},{6,0},{7,1},{8,10},{9,11},{10,... | collective-permute-start | bytes 1769480 | tf_op jit(solution)/shard_map/ppermute | solution.py:468
  40.4 14.3 %collective-permute-start.11 = (bf16[1152,256]{1,0:T(8,128)(2,1)S(1)}, bf16[1152,256]{1,0:T(8,128)(2,1)S(1)}, u32[]{:S(2)}, u32[]{:S(2)}) collective-permute-start(bf16[1152,256]{1,0:T(8,128)(2,1)S(1)} %collective-permute-done.7.refs_8_), channel_id=1, source_target_pairs={{0,8},{8,0},{16,24},{24,16},{1,9},{9,1},{17,25},{25,17},{2,10},{10... | collective-permute-start | bytes 1769480 | tf_op jit(solution)/shard_map/ppermute | solution.py:471
  41.0 16.3 %collective-permute-start.12 = (bf16[1152,256]{1,0:T(8,128)(2,1)S(1)}, bf16[1152,256]{1,0:T(8,128)(2,1)S(1)}, u32[]{:S(2)}, u32[]{:S(2)}) collective-permute-start(bf16[1152,256]{1,0:T(8,128)(2,1)S(1)} %collective-permute-done.7.refs_8_), channel_id=1, source_target_pairs={{0,16},{8,24},{16,0},{24,8},{1,17},{9,25},{17,1},{25,9},{2,18},{10... | collective-permute-start | bytes 1769480 | tf_op jit(solution)/shard_map/ppermute | solution.py:471
  41.8 18.6 %collective-permute-start.4 = (bf16[1152,256]{1,0:T(8,128)(2,1)S(1)}, bf16[1152,256]{1,0:T(8,128)(2,1)S(1)}, u32[]{:S(2)}, u32[]{:S(2)}) collective-permute-start(bf16[1152,256]{1,0:T(8,128)(2,1)S(1)} %bitcast.14), channel_id=1, source_target_pairs={{0,2},{1,3},{2,4},{3,5},{4,6},{5,7},{6,0},{7,1},{8,10},{9,11},{10,... | collective-permute-start | bytes 1769480 | tf_op jit(solution)/shard_map/ppermute | solution.py:468
  41.9 30.7 %collective-permute-start.8 = (bf16[1152,256]{1,0:T(8,128)(2,1)S(1)}, bf16[1152,256]{1,0:T(8,128)(2,1)S(1)}, u32[]{:S(2)}, u32[]{:S(2)}) collective-permute-start(bf16[1152,256]{1,0:T(8,128)(2,1)S(1)} %collective-permute-done.7.refs_8_), channel_id=1, source_target_pairs={{0,2},{1,3},{2,4},{3,5},{4,6},{5,7},{6,0},{7,1},{8,10},{9,11},{10,... | collective-permute-start | bytes 1769480 | tf_op jit(solution)/shard_map/ppermute | solution.py:468
  44.2 19.4 %collective-permute-start.13 = (bf16[576,256]{1,0:T(8,128)(2,1)S(1)}, bf16[576,256]{1,0:T(8,128)(2,1)S(1)}, u32[]{:S(2)}, u32[]{:S(2)}) collective-permute-start(bf16[576,256]{1,0:T(8,128)(2,1)S(1)} %slice.42), channel_id=1, source_target_pairs={{0,16},{8,24},{16,0},{24,8},{1,17},{9,25},{17,1},{25,9},{2,18},{10... | collective-permute-start | bytes 884744 | tf_op jit(solution)/shard_map/ppermute | solution.py:471
  58.2 7.8 %collective-permute-start.15 = (bf16[576,256]{1,0:T(8,128)(2,1)S(1)}, bf16[576,256]{1,0:T(8,128)(2,1)S(1)}, u32[]{:S(2)}, u32[]{:S(2)}) collective-permute-start(bf16[576,256]{1,0:T(8,128)(2,1)S(1)} %slice.44), channel_id=1, source_target_pairs={{0,8},{8,0},{16,24},{24,16},{1,9},{9,1},{17,25},{25,17},{2,10},{10... | collective-permute-start | bytes 884744 | tf_op jit(solution)/shard_map/ppermute | solution.py:471
  59.8 12.8 %collective-permute-start.16 = (bf16[576,256]{1,0:T(8,128)(2,1)S(1)}, bf16[576,256]{1,0:T(8,128)(2,1)S(1)}, u32[]{:S(2)}, u32[]{:S(2)}) collective-permute-start(bf16[576,256]{1,0:T(8,128)(2,1)S(1)} %slice.45), channel_id=1, source_target_pairs={{0,8},{8,0},{16,24},{24,16},{1,9},{9,1},{17,25},{25,17},{2,10},{10... | collective-permute-start | bytes 884744 | tf_op jit(solution)/shard_map/ppermute | solution.py:471
  60.5 12.1 %collective-permute-start.14 = (bf16[576,256]{1,0:T(8,128)(2,1)S(1)}, bf16[576,256]{1,0:T(8,128)(2,1)S(1)}, u32[]{:S(2)}, u32[]{:S(2)}) collective-permute-start(bf16[576,256]{1,0:T(8,128)(2,1)S(1)} %slice.43), channel_id=1, source_target_pairs={{0,16},{8,24},{16,0},{24,8},{1,17},{9,25},{17,1},{25,9},{2,18},{10... | collective-permute-start | bytes 884744 | tf_op jit(solution)/shard_map/ppermute | solution.py:471
  63.6 19.1 %collective-permute-start.5 = (bf16[1152,256]{1,0:T(8,128)(2,1)S(1)}, bf16[1152,256]{1,0:T(8,128)(2,1)S(1)}, u32[]{:S(2)}, u32[]{:S(2)}) collective-permute-start(bf16[1152,256]{1,0:T(8,128)(2,1)S(1)} %collective-permute-done.4.refs_7_.refs_12_), channel_id=1, source_target_pairs={{0,2},{1,3},{2,4},{3,5},{4,6},{5,7},{6,0},{7,1},{8,10},{9,11},{10,... | collective-permute-start | bytes 1769480 | tf_op jit(solution)/shard_map/ppermute | solution.py:468
  72.6 13.0 %collective-permute-start.17 = (bf16[1152,256]{1,0:T(8,128)(2,1)S(1)}, bf16[1152,256]{1,0:T(8,128)(2,1)S(1)}, u32[]{:S(2)}, u32[]{:S(2)}) collective-permute-start(bf16[1152,256]{1,0:T(8,128)(2,1)S(1)} %collective-permute-done.8.refs_8_), channel_id=1, source_target_pairs={{0,8},{8,0},{16,24},{24,16},{1,9},{9,1},{17,25},{25,17},{2,10},{10... | collective-permute-start | bytes 1769480 | tf_op jit(solution)/shard_map/ppermute | solution.py:471
  73.8 12.4 %collective-permute-start.18 = (bf16[1152,256]{1,0:T(8,128)(2,1)S(1)}, bf16[1152,256]{1,0:T(8,128)(2,1)S(1)}, u32[]{:S(2)}, u32[]{:S(2)}) collective-permute-start(bf16[1152,256]{1,0:T(8,128)(2,1)S(1)} %collective-permute-done.8.refs_8_), channel_id=1, source_target_pairs={{0,16},{8,24},{16,0},{24,8},{1,17},{9,25},{17,1},{25,9},{2,18},{10... | collective-permute-start | bytes 1769480 | tf_op jit(solution)/shard_map/ppermute | solution.py:471
  82.7 14.6 %collective-permute-start.6 = (bf16[1152,256]{1,0:T(8,128)(2,1)S(1)}, bf16[1152,256]{1,0:T(8,128)(2,1)S(1)}, u32[]{:S(2)}, u32[]{:S(2)}) collective-permute-start(bf16[1152,256]{1,0:T(8,128)(2,1)S(1)} %collective-permute-done.5.refs_7_.refs_12_), channel_id=1, source_target_pairs={{0,2},{1,3},{2,4},{3,5},{4,6},{5,7},{6,0},{7,1},{8,10},{9,11},{10,... | collective-permute-start | bytes 1769480 | tf_op jit(solution)/shard_map/ppermute | solution.py:468
  82.8 10.0 %collective-permute-start.21 = (bf16[576,256]{1,0:T(8,128)(2,1)S(1)}, bf16[576,256]{1,0:T(8,128)(2,1)S(1)}, u32[]{:S(2)}, u32[]{:S(2)}) collective-permute-start(bf16[576,256]{1,0:T(8,128)(2,1)S(1)} %slice.58), channel_id=1, source_target_pairs={{0,16},{8,24},{16,0},{24,8},{1,17},{9,25},{17,1},{25,9},{2,18},{10... | collective-permute-start | bytes 884744 | tf_op jit(solution)/shard_map/ppermute | solution.py:471
  84.1 9.5 %collective-permute-start.22 = (bf16[576,256]{1,0:T(8,128)(2,1)S(1)}, bf16[576,256]{1,0:T(8,128)(2,1)S(1)}, u32[]{:S(2)}, u32[]{:S(2)}) collective-permute-start(bf16[576,256]{1,0:T(8,128)(2,1)S(1)} %slice.59), channel_id=1, source_target_pairs={{0,8},{8,0},{16,24},{24,16},{1,9},{9,1},{17,25},{25,17},{2,10},{10... | collective-permute-start | bytes 884744 | tf_op jit(solution)/shard_map/ppermute | solution.py:471
  85.6 11.8 %collective-permute-start.19 = (bf16[576,256]{1,0:T(8,128)(2,1)S(1)}, bf16[576,256]{1,0:T(8,128)(2,1)S(1)}, u32[]{:S(2)}, u32[]{:S(2)}) collective-permute-start(bf16[576,256]{1,0:T(8,128)(2,1)S(1)} %slice.56), channel_id=1, source_target_pairs={{0,16},{8,24},{16,0},{24,8},{1,17},{9,25},{17,1},{25,9},{2,18},{10... | collective-permute-start | bytes 884744 | tf_op jit(solution)/shard_map/ppermute | solution.py:471
  86.3 11.1 %collective-permute-start.20 = (bf16[576,256]{1,0:T(8,128)(2,1)S(1)}, bf16[576,256]{1,0:T(8,128)(2,1)S(1)}, u32[]{:S(2)}, u32[]{:S(2)}) collective-permute-start(bf16[576,256]{1,0:T(8,128)(2,1)S(1)} %slice.57), channel_id=1, source_target_pairs={{0,8},{8,0},{16,24},{24,16},{1,9},{9,1},{17,25},{25,17},{2,10},{10... | collective-permute-start | bytes 884744 | tf_op jit(solution)/shard_map/ppermute | solution.py:471
  100.1 3.4 %collective-permute-start.24 = (f32[264,768]{1,0:T(8,128)S(1)}, f32[264,768]{1,0:T(8,128)S(1)}, u32[]{:S(2)}, u32[]{:S(2)}) collective-permute-start(f32[264,768]{1,0:T(8,128)S(1)} %get-tuple-element.107.cross), channel_id=1, source_target_pairs={{0,1},{1,0},{2,3},{3,2},{4,5},{5,4},{6,7},{7,6},{8,9},{9,8},{10,11... | collective-permute-start | bytes 2433032 | tf_op jit(solution)/shard_map/ppermute | solution.py:465
  100.2 3.3 %collective-permute-start.23 = (f32[128,1280]{1,0:T(8,128)S(1)}, f32[128,1280]{1,0:T(8,128)S(1)}, u32[]{:S(2)}, u32[]{:S(2)}) collective-permute-start(f32[128,1280]{1,0:T(8,128)S(1)} %get-tuple-element.106), channel_id=1, source_target_pairs={{0,1},{1,0},{2,3},{3,2},{4,5},{5,4},{6,7},{7,6},{8,9},{9,8},{10,11... | collective-permute-start | bytes 1966088 | tf_op jit(solution)/shard_map/ppermute | solution.py:465
  100.7 20.3 %collective-permute-start.31 = (bf16[256,1152]{1,0:T(8,128)(2,1)S(1)}, bf16[256,1152]{1,0:T(8,128)(2,1)S(1)}, u32[]{:S(2)}, u32[]{:S(2)}) collective-permute-start(bf16[256,1152]{1,0:T(8,128)(2,1)S(1)} %shard_map.106), channel_id=1, source_target_pairs={{0,6},{1,7},{2,0},{3,1},{4,2},{5,3},{6,4},{7,5},{8,14},{9,15},{10,... | collective-permute-start | bytes 1769480 | tf_op jit(solution)/shard_map/ppermute | solution.py:468
  104.6 1.7 collective-permute-start.27
  106.2 16.0 %collective-permute-start.25 = (f32[128,512]{1,0:T(8,128)S(1)}, f32[128,512]{1,0:T(8,128)S(1)}, u32[]{:S(2)}, u32[]{:S(2)}) collective-permute-start(f32[128,512]{1,0:T(8,128)S(1)} %get-tuple-element.108.refs_1_.refs_7_.refs_3_), channel_id=1, source_target_pairs={{0,1},{1,0},{2,3},{3,2},{4,5},{5,4},{6,7},{7,6},{8,9},{9,8},{10,11... | collective-permute-start | bytes 786440 | tf_op jit(solution)/shard_map/ppermute | solution.py:465
  106.5 14.3 %collective-permute-start.29 = (bf16[128,256]{1,0:T(8,128)(2,1)S(1)}, bf16[128,256]{1,0:T(8,128)(2,1)S(1)}, u32[]{:S(2)}, u32[]{:S(2)}) collective-permute-start(bf16[128,256]{1,0:T(8,128)(2,1)S(1)} %shard_map.112), channel_id=1, source_target_pairs={{8,0},{9,1},{10,2},{11,3},{12,4},{13,5},{14,6},{15,7}} | collective-permute-start | bytes 196616 | tf_op jit(solution)/shard_map/ppermute | solution.py:621
  124.6 13.7 %collective-permute-start.32 = (bf16[256,1152]{1,0:T(8,128)(2,1)}, bf16[256,1152]{1,0:T(8,128)(2,1)}, u32[]{:S(2)}, u32[]{:S(2)}) collective-permute-start(bf16[256,1152]{1,0:T(8,128)(2,1)} %shard_map.114.refs_5_), channel_id=1, source_target_pairs={{24,16},{16,24},{25,17},{17,25},{26,18},{18,26},{27,19},{19,27},{2... | collective-permute-start | bytes 1769480 | tf_op jit(solution)/shard_map/ppermute | solution.py:679
  126.1 26.7 %collective-permute-start.35 = (bf16[256,1152]{1,0:T(8,128)(2,1)}, bf16[256,1152]{1,0:T(8,128)(2,1)S(1)}, u32[]{:S(2)}, u32[]{:S(2)}) collective-permute-start(bf16[256,1152]{1,0:T(8,128)(2,1)} %shard_map.114.refs_5_), channel_id=1, source_target_pairs={{8,0},{9,1},{10,2},{11,3},{12,4},{13,5},{14,6},{15,7}} | collective-permute-start | bytes 1769480 | tf_op jit(solution)/shard_map/ppermute | solution.py:679
  133.6 23.4 %collective-permute-start.36 = (bf16[256,1152]{1,0:T(8,128)(2,1)S(1)}, bf16[256,1152]{1,0:T(8,128)(2,1)S(1)}, u32[]{:S(2)}, u32[]{:S(2)}) collective-permute-start(bf16[256,1152]{1,0:T(8,128)(2,1)S(1)} %get-tuple-element.118.refs_5_), channel_id=1, source_target_pairs={{24,16},{8,0},{16,24},{25,17},{9,1},{17,25},{26,18},{10,2},{18,26}... | collective-permute-start | bytes 1769480 | tf_op jit(solution)/shard_map/ppermute | solution.py:676
  134.9 17.2 %collective-permute-start.34 = (bf16[1152,256]{1,0:T(8,128)(2,1)S(1)}, bf16[1152,256]{1,0:T(8,128)(2,1)S(1)}, u32[]{:S(2)}, u32[]{:S(2)}) collective-permute-start(bf16[1152,256]{1,0:T(8,128)(2,1)S(1)} %get-tuple-element.121), channel_id=1, source_target_pairs={{0,2},{1,3},{2,4},{3,5},{4,6},{5,7},{6,0},{7,1},{8,10},{9,11},{10,... | collective-permute-start | bytes 1769480 | tf_op jit(solution)/shard_map/ppermute | solution.py:468
  136.9 42.8 %collective-permute-start.39 = (bf16[256,1152]{1,0:T(8,128)(2,1)S(1)}, bf16[256,1152]{1,0:T(8,128)(2,1)S(1)}, u32[]{:S(2)}, u32[]{:S(2)}) collective-permute-start(bf16[256,1152]{1,0:T(8,128)(2,1)S(1)} %get-tuple-element.119.refs_5_), channel_id=1, source_target_pairs={{24,16},{8,0},{16,24},{25,17},{9,1},{17,25},{26,18},{10,2},{18,26}... | collective-permute-start | bytes 1769480 | tf_op jit(solution)/shard_map/ppermute | solution.py:676
  139.6 36.5 %collective-permute-start.33 = (bf16[256,1152]{1,0:T(8,128)(2,1)S(1)}, bf16[256,1152]{1,0:T(8,128)(2,1)S(1)}, u32[]{:S(2)}, u32[]{:S(2)}) collective-permute-start(bf16[256,1152]{1,0:T(8,128)(2,1)S(1)} %add_convert_fusion.4), channel_id=1, source_target_pairs={{24,8},{16,0},{25,9},{17,1},{26,10},{18,2},{27,11},{19,3},{28,12},... | collective-permute-start | bytes 1769480 | tf_op jit(solution)/shard_map/ppermute | solution.py:685
  152.2 23.9 %collective-permute-start.37 = (bf16[256,256]{1,0:T(8,128)(2,1)S(1)}, bf16[256,256]{1,0:T(8,128)(2,1)S(1)}, u32[]{:S(2)}, u32[]{:S(2)}) collective-permute-start(bf16[256,256]{1,0:T(8,128)(2,1)S(1)} %pad_maximum_fusion.1), channel_id=1, source_target_pairs={{0,6},{1,7},{2,0},{3,1},{4,2},{5,3},{6,4},{7,5},{8,14},{9,15},{10,... | collective-permute-start | bytes 393224 | tf_op jit(solution)/shard_map/ppermute | solution.py:468
  153.0 31.5 %collective-permute-start.41 = (bf16[1152,256]{1,0:T(8,128)(2,1)S(1)}, bf16[1152,256]{1,0:T(8,128)(2,1)S(1)}, u32[]{:S(2)}, u32[]{:S(2)}) collective-permute-start(bf16[1152,256]{1,0:T(8,128)(2,1)S(1)} %add_convert_fusion.3), channel_id=1, source_target_pairs={{0,2},{1,3},{2,4},{3,5},{4,6},{5,7},{6,0},{7,1},{8,10},{9,11},{10,... | collective-permute-start | bytes 1769480 | tf_op jit(solution)/shard_map/ppermute | solution.py:468
  176.2 11.8 %collective-permute-start.40 = (bf16[256,1152]{1,0:T(8,128)(2,1)S(1)}, bf16[256,1152]{1,0:T(8,128)(2,1)S(1)}, u32[]{:S(2)}, u32[]{:S(2)}) collective-permute-start(bf16[256,1152]{1,0:T(8,128)(2,1)S(1)} %add_convert_fusion.2), channel_id=1, source_target_pairs={{24,8},{16,0},{25,9},{17,1},{26,10},{18,2},{27,11},{19,3},{28,12},... | collective-permute-start | bytes 1769480 | tf_op jit(solution)/shard_map/ppermute | solution.py:685
  179.7 15.5 %collective-permute-start.43 = (bf16[1152,256]{1,0:T(8,128)(2,1)S(1)}, bf16[1152,256]{1,0:T(8,128)(2,1)S(1)}, u32[]{:S(2)}, u32[]{:S(2)}) collective-permute-start(bf16[1152,256]{1,0:T(8,128)(2,1)S(1)} %get-tuple-element.128), channel_id=1, source_target_pairs={{0,2},{1,3},{2,4},{3,5},{4,6},{5,7},{6,0},{7,1},{8,10},{9,11},{10,... | collective-permute-start | bytes 1769480 | tf_op jit(solution)/shard_map/ppermute | solution.py:468
  179.9 15.8 %collective-permute-start.45 = (bf16[256,1152]{1,0:T(8,128)(2,1)S(1)}, bf16[256,1152]{1,0:T(8,128)(2,1)S(1)}, u32[]{:S(2)}, u32[]{:S(2)}) collective-permute-start(bf16[256,1152]{1,0:T(8,128)(2,1)S(1)} %add_convert_fusion.1), channel_id=1, source_target_pairs={{24,8},{16,0},{25,9},{17,1},{26,10},{18,2},{27,11},{19,3},{28,12},... | collective-permute-start | bytes 1769480 | tf_op jit(solution)/shard_map/ppermute | solution.py:685
  183.1 13.5 %collective-permute-start.38 = (bf16[256,1152]{1,0:T(8,128)(2,1)S(1)}, bf16[256,1152]{1,0:T(8,128)(2,1)S(1)}, u32[]{:S(2)}, u32[]{:S(2)}) collective-permute-start(bf16[256,1152]{1,0:T(8,128)(2,1)S(1)} %get-tuple-element.130.refs_5_), channel_id=1, source_target_pairs={{24,16},{8,0},{16,24},{25,17},{9,1},{17,25},{26,18},{10,2},{18,26}... | collective-permute-start | bytes 1769480 | tf_op jit(solution)/shard_map/ppermute | solution.py:676
  195.3 8.8 %collective-permute-start.44 = (bf16[576,256]{1,0:T(8,128)(2,1)S(1)}, bf16[576,256]{1,0:T(8,128)(2,1)S(1)}, u32[]{:S(2)}, u32[]{:S(2)}) collective-permute-start(bf16[576,256]{1,0:T(8,128)(2,1)S(1)} %get-tuple-element.151), channel_id=1, source_target_pairs={{0,2},{1,3},{2,4},{3,5},{4,6},{5,7},{6,0},{7,1},{8,10},{9,11},{10,... | collective-permute-start | bytes 884744 | tf_op jit(solution)/shard_map/ppermute | solution.py:468
  195.4 15.1 %collective-permute-start.47 = (bf16[576,256]{1,0:T(8,128)(2,1)S(1)}, bf16[576,256]{1,0:T(8,128)(2,1)S(1)}, u32[]{:S(2)}, u32[]{:S(2)}) collective-permute-start(bf16[576,256]{1,0:T(8,128)(2,1)S(1)} %get-tuple-element.150), channel_id=1, source_target_pairs={{0,2},{1,3},{2,4},{3,5},{4,6},{5,7},{6,0},{7,1},{8,10},{9,11},{10,... | collective-permute-start | bytes 884744 | tf_op jit(solution)/shard_map/ppermute | solution.py:468
  196.5 14.2 %collective-permute-start.48 = (bf16[128,3456]{1,0:T(8,128)(2,1)S(1)}, bf16[128,3456]{1,0:T(8,128)(2,1)S(1)}, u32[]{:S(2)}, u32[]{:S(2)}) collective-permute-start(bf16[128,3456]{1,0:T(8,128)(2,1)S(1)} %pad_maximum_fusion), channel_id=1, source_target_pairs={{0,1},{1,0},{2,3},{3,2},{4,5},{5,4},{6,7},{7,6},{8,9},{9,8},{10,11... | collective-permute-start | bytes 2654216 | tf_op jit(solution)/shard_map/ppermute | solution.py:465
  196.8 19.8 %collective-permute-start.42 = (bf16[256,1152]{1,0:T(8,128)(2,1)S(1)}, bf16[256,1152]{1,0:T(8,128)(2,1)S(1)}, u32[]{:S(2)}, u32[]{:S(2)}) collective-permute-start(bf16[256,1152]{1,0:T(8,128)(2,1)S(1)} %add_convert_fusion), channel_id=1, source_target_pairs={{24,8},{16,0},{25,9},{17,1},{26,10},{18,2},{27,11},{19,3},{28,12},... | collective-permute-start | bytes 1769480 | tf_op jit(solution)/shard_map/ppermute | solution.py:685
  204.2 12.3 %collective-permute-start.46 = (bf16[576,256]{1,0:T(8,128)(2,1)S(1)}, bf16[576,256]{1,0:T(8,128)(2,1)S(1)}, u32[]{:S(2)}, u32[]{:S(2)}) collective-permute-start(bf16[576,256]{1,0:T(8,128)(2,1)S(1)} %add_convert_fusion.6), channel_id=1, source_target_pairs={{0,2},{1,3},{2,4},{3,5},{4,6},{5,7},{6,0},{7,1},{8,10},{9,11},{10,... | collective-permute-start | bytes 884744 | tf_op jit(solution)/shard_map/ppermute | solution.py:468
  210.6 9.2 %collective-permute-start.50 = (bf16[576,256]{1,0:T(8,128)(2,1)S(1)}, bf16[576,256]{1,0:T(8,128)(2,1)S(1)}, u32[]{:S(2)}, u32[]{:S(2)}) collective-permute-start(bf16[576,256]{1,0:T(8,128)(2,1)S(1)} %add_convert_fusion.5), channel_id=1, source_target_pairs={{0,2},{1,3},{2,4},{3,5},{4,6},{5,7},{6,0},{7,1},{8,10},{9,11},{10,... | collective-permute-start | bytes 884744 | tf_op jit(solution)/shard_map/ppermute | solution.py:468
  217.4 4.2 %collective-permute-start.49 = (bf16[128,1152]{1,0:T(8,128)(2,1)S(1)}, bf16[128,1152]{1,0:T(8,128)(2,1)S(1)}, u32[]{:S(2)}, u32[]{:S(2)}) collective-permute-start(bf16[128,1152]{1,0:T(8,128)(2,1)S(1)} %get-tuple-element.146), channel_id=1, source_target_pairs={{0,1},{1,0},{2,3},{3,2},{4,5},{5,4},{6,7},{7,6},{8,9},{9,8},{10,11... | collective-permute-start | bytes 884744 | tf_op jit(solution)/shard_map/ppermute | solution.py:465
  (29 other events, 414.7 us)

commit v6 on v5

--- a/solution.py
+++ b/solution.py
@@ -690,10 +690,9 @@
     down_ring = along(down_grads[2][0])
     sums = {1: scan_sum(1, after(opened[1], terms[2], terms[3]))}
     more = {1: scan_more(sums[1])}
-    act_ahead = along(jnp.concatenate(after([act, act_sib], sums[1]), axis=0), -1)
     down_sum = add(after(down_ring, beside), down_grads[3][0]).astype(BF16)
     down_ring = along(down_sum)
-    sums[2] = scan_sum(2, after(opened[2], more[1], act_ahead))
+    sums[2] = scan_sum(2, after(opened[2], more[1]))
     more[2] = scan_more(sums[2])
     mines[1], theirs[1], up_grads[1] = close_block(
         1, (opened[1], after(more[1], down_sum, sums[2]), beside)
@@ -712,6 +711,7 @@
     up_ring = [along(value) for value in up_sums]
     mines[3], theirs[3], up_grads[3] = close_block(3, (opened[3], after(more[3], *up_sums)))
     up_sums = [add(up_ring[0], up_grads[3][halves[0]]).astype(BF16)]
+    act_ahead = along(jnp.concatenate(after([act, act_sib], up_sums[0]), axis=0), -1)
     second = after(up_ring[1], up_sums[0])
     up_sums.append(add(second, up_grads[3][halves[1]]).astype(BF16))
     up_ring = [along(value) for value in up_sums]

time: 224 us -> 213 us (0.951)
  waiting for transfers between devices: 121 us -> 106 us
  other arithmetic: 4.42 us -> 8.12 us
  local copies, waits for them, and re-layouts: 14.1 us -> 10.6 us
    ppermute x15, waiting for transfers between devices: 68.1 us -> 34.8 us  [along(): lax.ppermute(value, 'rep', [(r, (r + 2 * steps) % reps) for r in range(re...]
    ppermute x3, waiting for transfers between devices: 2.58 us -> 15.4 us  [scan_open(): return lax.ppermute(terms[index], 'section', [(3, 2), (1, 0), (2, 3)])]
    ppermute x4, waiting for transfers between devices: 3.58 us -> 9.39 us  [scan_more(): return lax.ppermute(value, 'section', [(3, 1), (2, 0)])]
    unnamed x52 -> x48, local copies, waits for them, and re-layouts: 11.3 us -> 7.77 us
    convert_element_type x4, other arithmetic: 1.82 us -> 4.14 us  [scan_sum(): return add(terms[index], arrived).astype(BF16)]
    ppermute x15, starting transfers between devices: 10.8 us -> 13.1 us  [along(): lax.ppermute(value, 'rep', [(r, (r + 2 * steps) % reps) for r in range(re...]
  transfers between devices with their start and end apart: 51 -> 51, of which waited for: 24 -> 24; matrix products, arithmetic and copies ran while one was open for 3% -> 5% of each run, Pallas kernels for 14% -> 16%
where the time goes in v6:
time: 213 us; the launch traced here: 212 us
  waiting for transfers between devices  106 us (50%)
  starting transfers between devices  46.6 us (22%)
  Pallas kernels  39.7 us (19%)
  local copies, waits for them, and re-layouts  10.6 us (5%)
  other arithmetic  8.12 us (4%)
    pallas_call x21, Pallas kernels, run_kernel(): pl.pallas_call(body, out_shape=out_shapes, grid_spec=pltpu.PrefetchScalar...  39.7 us
    ppermute x15, waiting for transfers between devices, along(): lax.ppermute(value, 'rep', [(r, (r + 2 * steps) % reps) for r in range(re...  34.8 us
    ppermute x16, waiting for transfers between devices, flip(): lax.ppermute(value, 'section', [(s, s ^ mask) for s in range(sections)])  32.1 us
    ppermute x16, starting transfers between devices, flip(): lax.ppermute(value, 'section', [(s, s ^ mask) for s in range(sections)])  18.1 us
    ppermute x3, waiting for transfers between devices, scan_open(): return lax.ppermute(terms[index], 'section', [(3, 2), (1, 0), (2, 3)])  15.4 us
    ppermute x15, starting transfers between devices, along(): lax.ppermute(value, 'rep', [(r, (r + 2 * steps) % reps) for r in range(re...  13.1 us
    ppermute x1, waiting for transfers between devices, per_device(): arrivals += [lax.ppermute(passed, 'section', [(1, 0)])]  13 us
    ppermute x4, waiting for transfers between devices, scan_more(): return lax.ppermute(value, 'section', [(3, 1), (2, 0)])  9.39 us
  transfers between devices with their start and end apart: 51, of which 24 were waited for; matrix products, arithmetic and copies ran while one was open for 5% of the time, Pallas kernels for 16%

profile of v6, /device:TPU:0, one launch (start us, length us, event | category | flops | bytes accessed | tf_op | source)
XLA Modules:
  0.0 212.3 jit_solution(9927306564061177470)
XLA Ops:
  0.6 3.1 %collective-permute-start.2 = (bf16[1152,256]{1,0:T(8,128)(2,1)}, bf16[1152,256]{1,0:T(8,128)(2,1)}, u32[]{:S(2)}, u32[]{:S(2)}) collective-permute-start(bf16[1152,256]{1,0:T(8,128)(2,1)} %bitcast.17), channel_id=1, source_target_pairs={{0,2},{1,3},{2,4},{3,5},{4,6},{5,7},{6,0},{7,1},{8,10},{9,11},{10,... | collective-permute-start | bytes 1769480 | tf_op jit(solution)/shard_map/ppermute | solution.py:468
  3.7 1.5 collective-permute-start
  5.2 1.5 collective-permute-start.1
  7.6 2.3 %copy-done.2 = s32[1,2,64,9216]{3,2,1,0:T(8,128)S(1)} copy-done((s32[1,2,64,9216]{3,2,1,0:T(8,128)S(1)}, s32[1,2,64,9216]{3,2,1,0:T(8,128)}, u32[]{:S(2)}) %copy-start.2) | copy-done | bytes 4718616
  9.9 1.7 copy-done.5
  11.6 1.7 copy-done.6
  13.9 5.7 %shard_map.104 = (bf16[2,128,4608]{2,1,0:T(8,128)(2,1)S(1)}, bf16[2,128,5760]{2,1,0:T(8,128)(2,1)S(1)}, f32[128,256]{1,0:T(8,128)S(1)}) custom-call(s32[8]{0:T(128)S(1)} %pad_add_fusion.blocks.refs_0_, s32[2]{0:T(128)S(1)} %bitcast.21, bf16[2,64,9216]{2,1,0:T(8,128)(2,1)S(1)} %bitcast.12, bf16[2,64,9216]{2,1,0:T(8,128)(2,1)S(1)} %bitcast.13, ...), custom_call_target="tpu_custom_call" | custom-call | tf_op jit(solution)/shard_map/pallas_call | solution.py:165
  21.8 1.4 collective-permute-start.9
  24.1 12.4 %collective-permute-done.10.refs_10_ = bf16[1152,256]{1,0:T(8,128)(2,1)S(1)} collective-permute-done((bf16[1152,256]{1,0:T(8,128)(2,1)}, bf16[1152,256]{1,0:T(8,128)(2,1)S(1)}, u32[]{:S(2)}, u32[]{:S(2)}) %collective-permute-start.10) | collective-permute-done | bytes 589856 | tf_op jit(solution)/shard_map/ppermute | solution.py:471
  37.4 3.0 %collective-permute-done.7.refs_8_ = bf16[1152,256]{1,0:T(8,128)(2,1)S(1)} collective-permute-done((bf16[1152,256]{1,0:T(8,128)(2,1)}, bf16[1152,256]{1,0:T(8,128)(2,1)S(1)}, u32[]{:S(2)}, u32[]{:S(2)}) %collective-permute-start.7) | collective-permute-done | bytes 589856 | tf_op jit(solution)/shard_map/ppermute | solution.py:468
  41.9 1.3 collective-permute-start.8
  45.3 9.5 %collective-permute-done.11.refs_9_ = bf16[1152,256]{1,0:T(8,128)(2,1)S(1)} collective-permute-done((bf16[1152,256]{1,0:T(8,128)(2,1)S(1)}, bf16[1152,256]{1,0:T(8,128)(2,1)S(1)}, u32[]{:S(2)}, u32[]{:S(2)}) %collective-permute-start.11) | collective-permute-done | bytes 589856 | tf_op jit(solution)/shard_map/ppermute | solution.py:471
  54.7 2.5 %collective-permute-done.12.refs_10_ = bf16[1152,256]{1,0:T(8,128)(2,1)S(1)} collective-permute-done((bf16[1152,256]{1,0:T(8,128)(2,1)S(1)}, bf16[1152,256]{1,0:T(8,128)(2,1)S(1)}, u32[]{:S(2)}, u32[]{:S(2)}) %collective-permute-start.12) | collective-permute-done | bytes 589856 | tf_op jit(solution)/shard_map/ppermute | solution.py:471
  58.2 1.5 collective-permute-start.15
  61.3 2.2 %collective-permute-done.13.refs_11_ = bf16[576,256]{1,0:T(8,128)(2,1)S(1)} collective-permute-done((bf16[576,256]{1,0:T(8,128)(2,1)S(1)}, bf16[576,256]{1,0:T(8,128)(2,1)S(1)}, u32[]{:S(2)}, u32[]{:S(2)}) %collective-permute-start.13) | collective-permute-done | bytes 294944 | tf_op jit(solution)/shard_map/ppermute | solution.py:471
  63.6 2.5 %collective-permute-done.15.refs_12_ = bf16[576,256]{1,0:T(8,128)(2,1)S(1)} collective-permute-done((bf16[576,256]{1,0:T(8,128)(2,1)S(1)}, bf16[576,256]{1,0:T(8,128)(2,1)S(1)}, u32[]{:S(2)}, u32[]{:S(2)}) %collective-permute-start.15) | collective-permute-done | bytes 294944 | tf_op jit(solution)/shard_map/ppermute | solution.py:471
  66.1 3.5 %shard_map.105 = (f32[128,1280]{1,0:T(8,128)S(1)}, f32[128,1280]{1,0:T(8,128)S(1)}, f32[264,768]{1,0:T(8,128)S(1)}) custom-call(s32[8]{0:T(128)S(1)} %pad_add_fusion.blocks.refs_0_, bf16[2,128,4608]{2,1,0:T(8,128)(2,1)S(1)} %get-tuple-element.76.refs_1_.own, bf16[2,128,5760]{2,1,0:T(8,128)(2,1)S(1)} %collective-permute-done.3.refs_2_.refs_4_.sib.stats_sib, ...), custom_call_target="tpu_custom_call" | custom-call | tf_op jit(solution)/shard_map/pallas_call | solution.py:165
  69.6 3.0 %collective-permute-done.8.refs_8_ = bf16[1152,256]{1,0:T(8,128)(2,1)S(1)} collective-permute-done((bf16[1152,256]{1,0:T(8,128)(2,1)S(1)}, bf16[1152,256]{1,0:T(8,128)(2,1)S(1)}, u32[]{:S(2)}, u32[]{:S(2)}) %collective-permute-start.8) | collective-permute-done | bytes 589856 | tf_op jit(solution)/shard_map/ppermute | solution.py:468
  73.8 1.4 collective-permute-start.18
  75.2 7.5 %collective-permute-done.5.refs_7_.refs_12_ = bf16[1152,256]{1,0:T(8,128)(2,1)S(1)} collective-permute-done((bf16[1152,256]{1,0:T(8,128)(2,1)S(1)}, bf16[1152,256]{1,0:T(8,128)(2,1)S(1)}, u32[]{:S(2)}, u32[]{:S(2)}) %collective-permute-start.5) | collective-permute-done | bytes 589856 | tf_op jit(solution)/shard_map/ppermute | solution.py:468
  84.1 1.5 collective-permute-start.22
  88.1 3.7 %shard_map.107 = (f32[128,1280]{1,0:T(8,128)S(1)}, f32[128,1280]{1,0:T(8,128)S(1)}, f32[264,768]{1,0:T(8,128)S(1)}) custom-call(s32[8]{0:T(128)S(1)} %pad_add_fusion.blocks.refs_0_, bf16[2,128,4608]{2,1,0:T(8,128)(2,1)S(1)} %get-tuple-element.76.refs_1_.own, ...), custom_call_target="tpu_custom_call", output_to_operand_aliasing={{0}: (13, {}), {1}: (14, {}), {2}: (15, {})} | custom-call | tf_op jit(solution)/shard_map/pallas_call | solution.py:165
  93.5 2.7 %shard_map.108 = (f32[128,1280]{1,0:T(8,128)S(1)}, f32[128,1280]{1,0:T(8,128)S(1)}, f32[264,768]{1,0:T(8,128)S(1)}) custom-call(s32[8]{0:T(128)S(1)} %pad_add_fusion.blocks.refs_0_, bf16[2,128,4608]{2,1,0:T(8,128)(2,1)S(1)} %get-tuple-element.76.refs_1_.own, ...), custom_call_target="tpu_custom_call", output_to_operand_aliasing={{0}: (13, {}), {1}: (14, {}), {2}: (15, {})} | custom-call | tf_op jit(solution)/shard_map/pallas_call | solution.py:165
  97.4 2.7 %shard_map.109 = (f32[128,1280]{1,0:T(8,128)S(1)}, f32[128,1280]{1,0:T(8,128)S(1)}, f32[264,768]{1,0:T(8,128)S(1)}) custom-call(s32[8]{0:T(128)S(1)} %pad_add_fusion.blocks.refs_0_, bf16[2,128,4608]{2,1,0:T(8,128)(2,1)S(1)} %get-tuple-element.76.refs_1_.own, ...), custom_call_target="tpu_custom_call", output_to_operand_aliasing={{0}: (13, {}), {1}: (14, {}), {2}: (15, {})} | custom-call | tf_op jit(solution)/shard_map/pallas_call | solution.py:165
  100.6 2.8 %collective-permute-start.31 = (bf16[256,1152]{1,0:T(8,128)(2,1)S(1)}, bf16[256,1152]{1,0:T(8,128)(2,1)S(1)}, u32[]{:S(2)}, u32[]{:S(2)}) collective-permute-start(bf16[256,1152]{1,0:T(8,128)(2,1)S(1)} %shard_map.106), channel_id=1, source_target_pairs={{0,6},{1,7},{2,0},{3,1},{4,2},{5,3},{6,4},{7,5},{8,14},{9,15},{10,... | collective-permute-start | bytes 1769480 | tf_op jit(solution)/shard_map/ppermute | solution.py:468
  107.7 13.0 %collective-permute-done.29.refs_9_ = bf16[128,256]{1,0:T(8,128)(2,1)S(1)} collective-permute-done((bf16[128,256]{1,0:T(8,128)(2,1)S(1)}, bf16[128,256]{1,0:T(8,128)(2,1)S(1)}, u32[]{:S(2)}, u32[]{:S(2)}) %collective-permute-start.29) | collective-permute-done | bytes 65568 | tf_op jit(solution)/shard_map/ppermute | solution.py:621
  122.1 2.4 %shard_map.114.refs_5_ = bf16[256,1152]{1,0:T(8,128)(2,1)} custom-call(s32[8]{0:T(128)S(1)} %pad_add_fusion.blocks.refs_0_, bf16[2,128,4608]{2,1,0:T(8,128)(2,1)S(1)} %get-tuple-element.76.refs_1_.own, bf16[2,128,5760]{2,1,0:T(8,128)(2,1)S(1)} %collective-permute-done.3.refs_2_.refs_4_.sib.stats_sib, ...), custom_call_target="tpu_custom_call" | custom-call | tf_op jit(solution)/shard_map/pallas_call | solution.py:165
  126.5 2.7 %shard_map.115 = (bf16[256,1152]{1,0:T(8,128)(2,1)}, bf16[1152,256]{1,0:T(8,128)(2,1)}) custom-call(s32[8]{0:T(128)S(1)} %pad_add_fusion.blocks.refs_0_, bf16[2,128,4608]{2,1,0:T(8,128)(2,1)S(1)} %get-tuple-element.76.refs_1_.own, bf16[2,128,5760]{2,1,0:T(8,128)(2,1)S(1)} %collective-permute-done.3.refs_2_.refs_4_.sib.stats_sib, ...), custom_call_target="tpu_custom_call" | custom-call | tf_op jit(solution)/shard_map/pallas_call | solution.py:165
  130.7 1.9 shard_map.116
  132.6 2.5 %add_convert_fusion.4 = bf16[256,1152]{1,0:T(8,128)(2,1)} fusion(bf16[256,1152]{1,0:T(8,128)(2,1)S(1)} %collective-permute-done.32.refs_6_, bf16[256,1152]{1,0:T(8,128)(2,1)} %shard_map.114.refs_5_), kind=kLoop, calls=%fused_computation.7 | loop fusion | flops 1179648 | bytes 1769472 | tf_op jit(solution)/shard_map/convert_element_type | solution.py:682
  138.5 8.3 %collective-permute-done.34 = bf16[1152,256]{1,0:T(8,128)(2,1)} collective-permute-done((bf16[1152,256]{1,0:T(8,128)(2,1)}, bf16[1152,256]{1,0:T(8,128)(2,1)}, u32[]{:S(2)}, u32[]{:S(2)}) %collective-permute-start.34) | collective-permute-done | bytes 589856 | tf_op jit(solution)/shard_map/ppermute | solution.py:468
  146.8 1.5 add_convert_fusion.3
  148.4 7.8 %collective-permute-done.36.refs_6_ = bf16[256,1152]{1,0:T(8,128)(2,1)} collective-permute-done((bf16[256,1152]{1,0:T(8,128)(2,1)}, bf16[256,1152]{1,0:T(8,128)(2,1)}, u32[]{:S(2)}, u32[]{:S(2)}) %collective-permute-start.36) | collective-permute-done | bytes 589856 | tf_op jit(solution)/shard_map/ppermute | solution.py:676
  156.2 1.4 add_convert_fusion.2
  157.6 1.3 collective-permute-start.39
  159.0 2.3 %shard_map.117 = (bf16[128,1152]{1,0:T(8,128)(2,1)S(1)}, bf16[128,1152]{1,0:T(8,128)(2,1)S(1)}, bf16[1152,256]{1,0:T(8,128)(2,1)S(1)}) custom-call(s32[1]{0:T(128)} %bitcast.refs_0_, bf16[2,128,4608]{2,1,0:T(8,128)(2,1)S(1)} %copy-done.1, bf16[2,128,5760]{2,1,0:T(8,128)(2,1)S(1)} %collective-permute-done.3.refs_2_.refs_4_.sib.stats_sib, ...), custom_call_target="tpu_custom_call" | custom-call | tf_op jit(solution)/shard_map/pallas_call | solution.py:165
  161.4 6.6 %collective-permute-done.38.refs_6_ = bf16[256,1152]{1,0:T(8,128)(2,1)S(1)} collective-permute-done((bf16[256,1152]{1,0:T(8,128)(2,1)}, bf16[256,1152]{1,0:T(8,128)(2,1)S(1)}, u32[]{:S(2)}, u32[]{:S(2)}) %collective-permute-start.38) | collective-permute-done | bytes 589856 | tf_op jit(solution)/shard_map/ppermute | solution.py:676
  169.5 1.9 shard_map.118
  172.7 1.8 collective-permute-done.39.refs_7_
  174.5 2.0 shard_map.119
  178.3 7.6 %collective-permute-done.44.refs_7_ = bf16[256,1152]{1,0:T(8,128)(2,1)S(1)} collective-permute-done((bf16[256,1152]{1,0:T(8,128)(2,1)S(1)}, bf16[256,1152]{1,0:T(8,128)(2,1)S(1)}, u32[]{:S(2)}, u32[]{:S(2)}) %collective-permute-start.44) | collective-permute-done | bytes 589856 | tf_op jit(solution)/shard_map/ppermute | solution.py:685
  188.0 1.4 collective-permute-start.41
  189.6 3.9 %collective-permute-start.49 = (bf16[256,256]{1,0:T(8,128)(2,1)S(1)}, bf16[256,256]{1,0:T(8,128)(2,1)S(1)}, u32[]{:S(2)}, u32[]{:S(2)}) collective-permute-start(bf16[256,256]{1,0:T(8,128)(2,1)S(1)} %pad_maximum_fusion.1), channel_id=1, source_target_pairs={{0,6},{1,7},{2,0},{3,1},{4,2},{5,3},{6,4},{7,5},{8,14},{9,15},{10,... | collective-permute-start | bytes 393224 | tf_op jit(solution)/shard_map/ppermute | solution.py:468
  193.6 8.9 %collective-permute-done.49.act = bf16[256,256]{1,0:T(8,128)(2,1)S(1)} collective-permute-done((bf16[256,256]{1,0:T(8,128)(2,1)S(1)}, bf16[256,256]{1,0:T(8,128)(2,1)S(1)}, u32[]{:S(2)}, u32[]{:S(2)}) %collective-permute-start.49) | collective-permute-done | bytes 131104 | tf_op jit(solution)/shard_map/ppermute | solution.py:468
  203.0 3.0 %shard_map.121.refs_2_ = bf16[128,9216]{1,0:T(8,128)(2,1)} custom-call(s32[8]{0:T(128)S(1)} %copy-done.22, bf16[128,1152]{1,0:T(8,128)(2,1)S(1)} %get-tuple-element.136.refs_0_, bf16[128,1152]{1,0:T(8,128)(2,1)S(1)} %get-tuple-element.137.refs_1_, bf16[128,1152]{1,0:T(8,128)(2,1)S(1)} %get-tuple-element.138.refs_2_, ...), custom_call_target="tpu_custom_call" | custom-call | tf_op jit(solution)/shard_map/pallas_call | solution.py:165
  206.9 2.1 collective-permute-done.50
  209.1 1.7 maximum_bitcast_fusion
  210.9 1.4 shard_map.123
  (147 shorter events, 40.8 us)
Async XLA Ops:
  0.6 19.1 %collective-permute-start.2 = (bf16[1152,256]{1,0:T(8,128)(2,1)}, bf16[1152,256]{1,0:T(8,128)(2,1)}, u32[]{:S(2)}, u32[]{:S(2)}) collective-permute-start(bf16[1152,256]{1,0:T(8,128)(2,1)} %bitcast.17), channel_id=1, source_target_pairs={{0,2},{1,3},{2,4},{3,5},{4,6},{5,7},{6,0},{7,1},{8,10},{9,11},{10,... | collective-permute-start | bytes 1769480 | tf_op jit(solution)/shard_map/ppermute | solution.py:468
  3.7 16.0 %collective-permute-start = (bf16[1152,256]{1,0:T(8,128)(2,1)}, bf16[1152,256]{1,0:T(8,128)(2,1)S(1)}, u32[]{:S(2)}, u32[]{:S(2)}) collective-permute-start(bf16[1152,256]{1,0:T(8,128)(2,1)} %bitcast.18), channel_id=1, source_target_pairs={{0,8},{8,0},{16,24},{24,16},{1,9},{9,1},{17,25},{25,17},{2,10},{10... | collective-permute-start | bytes 1769480 | tf_op jit(solution)/shard_map/ppermute | solution.py:471
  5.2 14.8 %collective-permute-start.1 = (bf16[1152,256]{1,0:T(8,128)(2,1)}, bf16[1152,256]{1,0:T(8,128)(2,1)}, u32[]{:S(2)}, u32[]{:S(2)}) collective-permute-start(bf16[1152,256]{1,0:T(8,128)(2,1)} %bitcast.19), channel_id=1, source_target_pairs={{0,16},{8,24},{16,0},{24,8},{1,17},{9,25},{17,1},{25,9},{2,18},{10... | collective-permute-start | bytes 1769480 | tf_op jit(solution)/shard_map/ppermute | solution.py:471
  20.6 19.8 %collective-permute-start.3 = (bf16[2,128,5760]{2,1,0:T(8,128)(2,1)S(1)}, bf16[2,128,5760]{2,1,0:T(8,128)(2,1)S(1)}, u32[]{:S(2)}, u32[]{:S(2)}) collective-permute-start(bf16[2,128,5760]{2,1,0:T(8,128)(2,1)S(1)} %get-tuple-element.78), channel_id=1, source_target_pairs={{0,1},{1,0},{2,3},{3,2},{4,5},{5,4},{6,7},{7,6},{8,9},{9,8},{10,11... | collective-permute-start | bytes 8847368 | tf_op jit(solution)/shard_map/ppermute | solution.py:465
  20.6 16.0 %collective-permute-start.10 = (bf16[1152,256]{1,0:T(8,128)(2,1)}, bf16[1152,256]{1,0:T(8,128)(2,1)S(1)}, u32[]{:S(2)}, u32[]{:S(2)}) collective-permute-start(bf16[1152,256]{1,0:T(8,128)(2,1)} %collective-permute-done.2.refs_8_), channel_id=1, source_target_pairs={{0,16},{8,24},{16,0},{24,8},{1,17},{9,25},{17,1},{25,9},{2,18},{10... | collective-permute-start | bytes 1769480 | tf_op jit(solution)/shard_map/ppermute | solution.py:471
  21.8 15.7 %collective-permute-start.9 = (bf16[1152,256]{1,0:T(8,128)(2,1)}, bf16[1152,256]{1,0:T(8,128)(2,1)S(1)}, u32[]{:S(2)}, u32[]{:S(2)}) collective-permute-start(bf16[1152,256]{1,0:T(8,128)(2,1)} %collective-permute-done.2.refs_8_), channel_id=1, source_target_pairs={{0,8},{8,0},{16,24},{24,16},{1,9},{9,1},{17,25},{25,17},{2,10},{10... | collective-permute-start | bytes 1769480 | tf_op jit(solution)/shard_map/ppermute | solution.py:471
  23.2 17.2 %collective-permute-start.7 = (bf16[1152,256]{1,0:T(8,128)(2,1)}, bf16[1152,256]{1,0:T(8,128)(2,1)S(1)}, u32[]{:S(2)}, u32[]{:S(2)}) collective-permute-start(bf16[1152,256]{1,0:T(8,128)(2,1)} %collective-permute-done.2.refs_8_), channel_id=1, source_target_pairs={{0,2},{1,3},{2,4},{3,5},{4,6},{5,7},{6,0},{7,1},{8,10},{9,11},{10,... | collective-permute-start | bytes 1769480 | tf_op jit(solution)/shard_map/ppermute | solution.py:468
  40.4 14.3 %collective-permute-start.11 = (bf16[1152,256]{1,0:T(8,128)(2,1)S(1)}, bf16[1152,256]{1,0:T(8,128)(2,1)S(1)}, u32[]{:S(2)}, u32[]{:S(2)}) collective-permute-start(bf16[1152,256]{1,0:T(8,128)(2,1)S(1)} %collective-permute-done.7.refs_8_), channel_id=1, source_target_pairs={{0,8},{8,0},{16,24},{24,16},{1,9},{9,1},{17,25},{25,17},{2,10},{10... | collective-permute-start | bytes 1769480 | tf_op jit(solution)/shard_map/ppermute | solution.py:471
  41.0 16.3 %collective-permute-start.12 = (bf16[1152,256]{1,0:T(8,128)(2,1)S(1)}, bf16[1152,256]{1,0:T(8,128)(2,1)S(1)}, u32[]{:S(2)}, u32[]{:S(2)}) collective-permute-start(bf16[1152,256]{1,0:T(8,128)(2,1)S(1)} %collective-permute-done.7.refs_8_), channel_id=1, source_target_pairs={{0,16},{8,24},{16,0},{24,8},{1,17},{9,25},{17,1},{25,9},{2,18},{10... | collective-permute-start | bytes 1769480 | tf_op jit(solution)/shard_map/ppermute | solution.py:471
  41.8 18.6 %collective-permute-start.4 = (bf16[1152,256]{1,0:T(8,128)(2,1)S(1)}, bf16[1152,256]{1,0:T(8,128)(2,1)S(1)}, u32[]{:S(2)}, u32[]{:S(2)}) collective-permute-start(bf16[1152,256]{1,0:T(8,128)(2,1)S(1)} %bitcast.14), channel_id=1, source_target_pairs={{0,2},{1,3},{2,4},{3,5},{4,6},{5,7},{6,0},{7,1},{8,10},{9,11},{10,... | collective-permute-start | bytes 1769480 | tf_op jit(solution)/shard_map/ppermute | solution.py:468
  41.9 30.7 %collective-permute-start.8 = (bf16[1152,256]{1,0:T(8,128)(2,1)S(1)}, bf16[1152,256]{1,0:T(8,128)(2,1)S(1)}, u32[]{:S(2)}, u32[]{:S(2)}) collective-permute-start(bf16[1152,256]{1,0:T(8,128)(2,1)S(1)} %collective-permute-done.7.refs_8_), channel_id=1, source_target_pairs={{0,2},{1,3},{2,4},{3,5},{4,6},{5,7},{6,0},{7,1},{8,10},{9,11},{10,... | collective-permute-start | bytes 1769480 | tf_op jit(solution)/shard_map/ppermute | solution.py:468
  44.2 19.3 %collective-permute-start.13 = (bf16[576,256]{1,0:T(8,128)(2,1)S(1)}, bf16[576,256]{1,0:T(8,128)(2,1)S(1)}, u32[]{:S(2)}, u32[]{:S(2)}) collective-permute-start(bf16[576,256]{1,0:T(8,128)(2,1)S(1)} %slice.42), channel_id=1, source_target_pairs={{0,16},{8,24},{16,0},{24,8},{1,17},{9,25},{17,1},{25,9},{2,18},{10... | collective-permute-start | bytes 884744 | tf_op jit(solution)/shard_map/ppermute | solution.py:471
  58.2 7.8 %collective-permute-start.15 = (bf16[576,256]{1,0:T(8,128)(2,1)S(1)}, bf16[576,256]{1,0:T(8,128)(2,1)S(1)}, u32[]{:S(2)}, u32[]{:S(2)}) collective-permute-start(bf16[576,256]{1,0:T(8,128)(2,1)S(1)} %slice.44), channel_id=1, source_target_pairs={{0,8},{8,0},{16,24},{24,16},{1,9},{9,1},{17,25},{25,17},{2,10},{10... | collective-permute-start | bytes 884744 | tf_op jit(solution)/shard_map/ppermute | solution.py:471
  59.8 12.8 %collective-permute-start.16 = (bf16[576,256]{1,0:T(8,128)(2,1)S(1)}, bf16[576,256]{1,0:T(8,128)(2,1)S(1)}, u32[]{:S(2)}, u32[]{:S(2)}) collective-permute-start(bf16[576,256]{1,0:T(8,128)(2,1)S(1)} %slice.45), channel_id=1, source_target_pairs={{0,8},{8,0},{16,24},{24,16},{1,9},{9,1},{17,25},{25,17},{2,10},{10... | collective-permute-start | bytes 884744 | tf_op jit(solution)/shard_map/ppermute | solution.py:471
  60.5 12.1 %collective-permute-start.14 = (bf16[576,256]{1,0:T(8,128)(2,1)S(1)}, bf16[576,256]{1,0:T(8,128)(2,1)S(1)}, u32[]{:S(2)}, u32[]{:S(2)}) collective-permute-start(bf16[576,256]{1,0:T(8,128)(2,1)S(1)} %slice.43), channel_id=1, source_target_pairs={{0,16},{8,24},{16,0},{24,8},{1,17},{9,25},{17,1},{25,9},{2,18},{10... | collective-permute-start | bytes 884744 | tf_op jit(solution)/shard_map/ppermute | solution.py:471
  63.6 19.2 %collective-permute-start.5 = (bf16[1152,256]{1,0:T(8,128)(2,1)S(1)}, bf16[1152,256]{1,0:T(8,128)(2,1)S(1)}, u32[]{:S(2)}, u32[]{:S(2)}) collective-permute-start(bf16[1152,256]{1,0:T(8,128)(2,1)S(1)} %collective-permute-done.4.refs_7_.refs_12_), channel_id=1, source_target_pairs={{0,2},{1,3},{2,4},{3,5},{4,6},{5,7},{6,0},{7,1},{8,10},{9,11},{10,... | collective-permute-start | bytes 1769480 | tf_op jit(solution)/shard_map/ppermute | solution.py:468
  72.6 13.0 %collective-permute-start.17 = (bf16[1152,256]{1,0:T(8,128)(2,1)S(1)}, bf16[1152,256]{1,0:T(8,128)(2,1)S(1)}, u32[]{:S(2)}, u32[]{:S(2)}) collective-permute-start(bf16[1152,256]{1,0:T(8,128)(2,1)S(1)} %collective-permute-done.8.refs_8_), channel_id=1, source_target_pairs={{0,8},{8,0},{16,24},{24,16},{1,9},{9,1},{17,25},{25,17},{2,10},{10... | collective-permute-start | bytes 1769480 | tf_op jit(solution)/shard_map/ppermute | solution.py:471
  73.8 12.4 %collective-permute-start.18 = (bf16[1152,256]{1,0:T(8,128)(2,1)S(1)}, bf16[1152,256]{1,0:T(8,128)(2,1)S(1)}, u32[]{:S(2)}, u32[]{:S(2)}) collective-permute-start(bf16[1152,256]{1,0:T(8,128)(2,1)S(1)} %collective-permute-done.8.refs_8_), channel_id=1, source_target_pairs={{0,16},{8,24},{16,0},{24,8},{1,17},{9,25},{17,1},{25,9},{2,18},{10... | collective-permute-start | bytes 1769480 | tf_op jit(solution)/shard_map/ppermute | solution.py:471
  82.7 14.6 %collective-permute-start.6 = (bf16[1152,256]{1,0:T(8,128)(2,1)S(1)}, bf16[1152,256]{1,0:T(8,128)(2,1)S(1)}, u32[]{:S(2)}, u32[]{:S(2)}) collective-permute-start(bf16[1152,256]{1,0:T(8,128)(2,1)S(1)} %collective-permute-done.5.refs_7_.refs_12_), channel_id=1, source_target_pairs={{0,2},{1,3},{2,4},{3,5},{4,6},{5,7},{6,0},{7,1},{8,10},{9,11},{10,... | collective-permute-start | bytes 1769480 | tf_op jit(solution)/shard_map/ppermute | solution.py:468
  82.8 10.0 %collective-permute-start.21 = (bf16[576,256]{1,0:T(8,128)(2,1)S(1)}, bf16[576,256]{1,0:T(8,128)(2,1)S(1)}, u32[]{:S(2)}, u32[]{:S(2)}) collective-permute-start(bf16[576,256]{1,0:T(8,128)(2,1)S(1)} %slice.58), channel_id=1, source_target_pairs={{0,16},{8,24},{16,0},{24,8},{1,17},{9,25},{17,1},{25,9},{2,18},{10... | collective-permute-start | bytes 884744 | tf_op jit(solution)/shard_map/ppermute | solution.py:471
  84.1 9.5 %collective-permute-start.22 = (bf16[576,256]{1,0:T(8,128)(2,1)S(1)}, bf16[576,256]{1,0:T(8,128)(2,1)S(1)}, u32[]{:S(2)}, u32[]{:S(2)}) collective-permute-start(bf16[576,256]{1,0:T(8,128)(2,1)S(1)} %slice.59), channel_id=1, source_target_pairs={{0,8},{8,0},{16,24},{24,16},{1,9},{9,1},{17,25},{25,17},{2,10},{10... | collective-permute-start | bytes 884744 | tf_op jit(solution)/shard_map/ppermute | solution.py:471
  85.6 11.8 %collective-permute-start.19 = (bf16[576,256]{1,0:T(8,128)(2,1)S(1)}, bf16[576,256]{1,0:T(8,128)(2,1)S(1)}, u32[]{:S(2)}, u32[]{:S(2)}) collective-permute-start(bf16[576,256]{1,0:T(8,128)(2,1)S(1)} %slice.56), channel_id=1, source_target_pairs={{0,16},{8,24},{16,0},{24,8},{1,17},{9,25},{17,1},{25,9},{2,18},{10... | collective-permute-start | bytes 884744 | tf_op jit(solution)/shard_map/ppermute | solution.py:471
  86.3 11.1 %collective-permute-start.20 = (bf16[576,256]{1,0:T(8,128)(2,1)S(1)}, bf16[576,256]{1,0:T(8,128)(2,1)S(1)}, u32[]{:S(2)}, u32[]{:S(2)}) collective-permute-start(bf16[576,256]{1,0:T(8,128)(2,1)S(1)} %slice.57), channel_id=1, source_target_pairs={{0,8},{8,0},{16,24},{24,16},{1,9},{9,1},{17,25},{25,17},{2,10},{10... | collective-permute-start | bytes 884744 | tf_op jit(solution)/shard_map/ppermute | solution.py:471
  100.1 3.4 %collective-permute-start.24 = (f32[264,768]{1,0:T(8,128)S(1)}, f32[264,768]{1,0:T(8,128)S(1)}, u32[]{:S(2)}, u32[]{:S(2)}) collective-permute-start(f32[264,768]{1,0:T(8,128)S(1)} %get-tuple-element.107.cross), channel_id=1, source_target_pairs={{0,1},{1,0},{2,3},{3,2},{4,5},{5,4},{6,7},{7,6},{8,9},{9,8},{10,11... | collective-permute-start | bytes 2433032 | tf_op jit(solution)/shard_map/ppermute | solution.py:465
  100.1 3.3 %collective-permute-start.23 = (f32[128,1280]{1,0:T(8,128)S(1)}, f32[128,1280]{1,0:T(8,128)S(1)}, u32[]{:S(2)}, u32[]{:S(2)}) collective-permute-start(f32[128,1280]{1,0:T(8,128)S(1)} %get-tuple-element.106), channel_id=1, source_target_pairs={{0,1},{1,0},{2,3},{3,2},{4,5},{5,4},{6,7},{7,6},{8,9},{9,8},{10,11... | collective-permute-start | bytes 1966088 | tf_op jit(solution)/shard_map/ppermute | solution.py:465
  100.6 20.3 %collective-permute-start.31 = (bf16[256,1152]{1,0:T(8,128)(2,1)S(1)}, bf16[256,1152]{1,0:T(8,128)(2,1)S(1)}, u32[]{:S(2)}, u32[]{:S(2)}) collective-permute-start(bf16[256,1152]{1,0:T(8,128)(2,1)S(1)} %shard_map.106), channel_id=1, source_target_pairs={{0,6},{1,7},{2,0},{3,1},{4,2},{5,3},{6,4},{7,5},{8,14},{9,15},{10,... | collective-permute-start | bytes 1769480 | tf_op jit(solution)/shard_map/ppermute | solution.py:468
  104.6 1.7 collective-permute-start.27
  106.1 16.0 %collective-permute-start.25 = (f32[128,512]{1,0:T(8,128)S(1)}, f32[128,512]{1,0:T(8,128)S(1)}, u32[]{:S(2)}, u32[]{:S(2)}) collective-permute-start(f32[128,512]{1,0:T(8,128)S(1)} %get-tuple-element.108.refs_1_.refs_7_.refs_3_), channel_id=1, source_target_pairs={{0,1},{1,0},{2,3},{3,2},{4,5},{5,4},{6,7},{7,6},{8,9},{9,8},{10,11... | collective-permute-start | bytes 786440 | tf_op jit(solution)/shard_map/ppermute | solution.py:465
  106.4 14.3 %collective-permute-start.29 = (bf16[128,256]{1,0:T(8,128)(2,1)S(1)}, bf16[128,256]{1,0:T(8,128)(2,1)S(1)}, u32[]{:S(2)}, u32[]{:S(2)}) collective-permute-start(bf16[128,256]{1,0:T(8,128)(2,1)S(1)} %shard_map.112), channel_id=1, source_target_pairs={{8,0},{9,1},{10,2},{11,3},{12,4},{13,5},{14,6},{15,7}} | collective-permute-start | bytes 196616 | tf_op jit(solution)/shard_map/ppermute | solution.py:621
  124.5 8.1 %collective-permute-start.32 = (bf16[256,1152]{1,0:T(8,128)(2,1)}, bf16[256,1152]{1,0:T(8,128)(2,1)S(1)}, u32[]{:S(2)}, u32[]{:S(2)}) collective-permute-start(bf16[256,1152]{1,0:T(8,128)(2,1)} %shard_map.114.refs_5_), channel_id=1, source_target_pairs={{24,16},{16,24},{25,17},{17,25},{26,18},{18,26},{27,19},{19,27},{2... | collective-permute-start | bytes 1769480 | tf_op jit(solution)/shard_map/ppermute | solution.py:679
  125.2 21.6 %collective-permute-start.35 = (bf16[256,1152]{1,0:T(8,128)(2,1)}, bf16[256,1152]{1,0:T(8,128)(2,1)}, u32[]{:S(2)}, u32[]{:S(2)}) collective-permute-start(bf16[256,1152]{1,0:T(8,128)(2,1)} %shard_map.114.refs_5_), channel_id=1, source_target_pairs={{8,0},{9,1},{10,2},{11,3},{12,4},{13,5},{14,6},{15,7}} | collective-permute-start | bytes 1769480 | tf_op jit(solution)/shard_map/ppermute | solution.py:679
  129.3 17.5 %collective-permute-start.34 = (bf16[1152,256]{1,0:T(8,128)(2,1)}, bf16[1152,256]{1,0:T(8,128)(2,1)}, u32[]{:S(2)}, u32[]{:S(2)}) collective-permute-start(bf16[1152,256]{1,0:T(8,128)(2,1)} %get-tuple-element.121), channel_id=1, source_target_pairs={{0,2},{1,3},{2,4},{3,5},{4,6},{5,7},{6,0},{7,1},{8,10},{9,11},{10,... | collective-permute-start | bytes 1769480 | tf_op jit(solution)/shard_map/ppermute | solution.py:468
  129.3 26.9 %collective-permute-start.36 = (bf16[256,1152]{1,0:T(8,128)(2,1)}, bf16[256,1152]{1,0:T(8,128)(2,1)}, u32[]{:S(2)}, u32[]{:S(2)}) collective-permute-start(bf16[256,1152]{1,0:T(8,128)(2,1)} %get-tuple-element.118.refs_5_), channel_id=1, source_target_pairs={{24,16},{8,0},{16,24},{25,17},{9,1},{17,25},{26,18},{10,2},{18,26}... | collective-permute-start | bytes 1769480 | tf_op jit(solution)/shard_map/ppermute | solution.py:676
  135.9 20.3 %collective-permute-start.33 = (bf16[256,1152]{1,0:T(8,128)(2,1)}, bf16[256,1152]{1,0:T(8,128)(2,1)}, u32[]{:S(2)}, u32[]{:S(2)}) collective-permute-start(bf16[256,1152]{1,0:T(8,128)(2,1)} %add_convert_fusion.4), channel_id=1, source_target_pairs={{24,8},{16,0},{25,9},{17,1},{26,10},{18,2},{27,11},{19,3},{28,12},... | collective-permute-start | bytes 1769480 | tf_op jit(solution)/shard_map/ppermute | solution.py:685
  137.2 30.8 %collective-permute-start.38 = (bf16[256,1152]{1,0:T(8,128)(2,1)}, bf16[256,1152]{1,0:T(8,128)(2,1)S(1)}, u32[]{:S(2)}, u32[]{:S(2)}) collective-permute-start(bf16[256,1152]{1,0:T(8,128)(2,1)} %copy-done.13), channel_id=1, source_target_pairs={{24,16},{8,0},{16,24},{25,17},{9,1},{17,25},{26,18},{10,2},{18,26}... | collective-permute-start | bytes 1769480 | tf_op jit(solution)/shard_map/ppermute | solution.py:676
  148.4 24.3 %collective-permute-start.40 = (bf16[1152,256]{1,0:T(8,128)(2,1)S(1)}, bf16[1152,256]{1,0:T(8,128)(2,1)S(1)}, u32[]{:S(2)}, u32[]{:S(2)}) collective-permute-start(bf16[1152,256]{1,0:T(8,128)(2,1)S(1)} %add_convert_fusion.3), channel_id=1, source_target_pairs={{0,2},{1,3},{2,4},{3,5},{4,6},{5,7},{6,0},{7,1},{8,10},{9,11},{10,... | collective-permute-start | bytes 1769480 | tf_op jit(solution)/shard_map/ppermute | solution.py:468
  157.6 16.9 %collective-permute-start.39 = (bf16[256,1152]{1,0:T(8,128)(2,1)S(1)}, bf16[256,1152]{1,0:T(8,128)(2,1)S(1)}, u32[]{:S(2)}, u32[]{:S(2)}) collective-permute-start(bf16[256,1152]{1,0:T(8,128)(2,1)S(1)} %add_convert_fusion.2), channel_id=1, source_target_pairs={{24,8},{16,0},{25,9},{17,1},{26,10},{18,2},{27,11},{19,3},{28,12},... | collective-permute-start | bytes 1769480 | tf_op jit(solution)/shard_map/ppermute | solution.py:685
  161.3 16.1 %collective-permute-start.42 = (bf16[1152,256]{1,0:T(8,128)(2,1)S(1)}, bf16[1152,256]{1,0:T(8,128)(2,1)S(1)}, u32[]{:S(2)}, u32[]{:S(2)}) collective-permute-start(bf16[1152,256]{1,0:T(8,128)(2,1)S(1)} %get-tuple-element.126), channel_id=1, source_target_pairs={{0,2},{1,3},{2,4},{3,5},{4,6},{5,7},{6,0},{7,1},{8,10},{9,11},{10,... | collective-permute-start | bytes 1769480 | tf_op jit(solution)/shard_map/ppermute | solution.py:468
  168.2 17.8 %collective-permute-start.44 = (bf16[256,1152]{1,0:T(8,128)(2,1)S(1)}, bf16[256,1152]{1,0:T(8,128)(2,1)S(1)}, u32[]{:S(2)}, u32[]{:S(2)}) collective-permute-start(bf16[256,1152]{1,0:T(8,128)(2,1)S(1)} %add_convert_fusion.1), channel_id=1, source_target_pairs={{24,8},{16,0},{25,9},{17,1},{26,10},{18,2},{27,11},{19,3},{28,12},... | collective-permute-start | bytes 1769480 | tf_op jit(solution)/shard_map/ppermute | solution.py:685
  171.4 16.4 %collective-permute-start.37 = (bf16[256,1152]{1,0:T(8,128)(2,1)S(1)}, bf16[256,1152]{1,0:T(8,128)(2,1)S(1)}, u32[]{:S(2)}, u32[]{:S(2)}) collective-permute-start(bf16[256,1152]{1,0:T(8,128)(2,1)S(1)} %get-tuple-element.128.refs_5_), channel_id=1, source_target_pairs={{24,16},{8,0},{16,24},{25,17},{9,1},{17,25},{26,18},{10,2},{18,26}... | collective-permute-start | bytes 1769480 | tf_op jit(solution)/shard_map/ppermute | solution.py:676
  177.6 11.9 %collective-permute-start.43 = (bf16[576,256]{1,0:T(8,128)(2,1)S(1)}, bf16[576,256]{1,0:T(8,128)(2,1)S(1)}, u32[]{:S(2)}, u32[]{:S(2)}) collective-permute-start(bf16[576,256]{1,0:T(8,128)(2,1)S(1)} %get-tuple-element.151), channel_id=1, source_target_pairs={{0,2},{1,3},{2,4},{3,5},{4,6},{5,7},{6,0},{7,1},{8,10},{9,11},{10,... | collective-permute-start | bytes 884744 | tf_op jit(solution)/shard_map/ppermute | solution.py:468
  177.6 15.8 %collective-permute-start.46 = (bf16[576,256]{1,0:T(8,128)(2,1)S(1)}, bf16[576,256]{1,0:T(8,128)(2,1)S(1)}, u32[]{:S(2)}, u32[]{:S(2)}) collective-permute-start(bf16[576,256]{1,0:T(8,128)(2,1)S(1)} %get-tuple-element.150), channel_id=1, source_target_pairs={{0,2},{1,3},{2,4},{3,5},{4,6},{5,7},{6,0},{7,1},{8,10},{9,11},{10,... | collective-permute-start | bytes 884744 | tf_op jit(solution)/shard_map/ppermute | solution.py:468
  186.8 16.2 %collective-permute-start.47 = (bf16[128,3456]{1,0:T(8,128)(2,1)S(1)}, bf16[128,3456]{1,0:T(8,128)(2,1)S(1)}, u32[]{:S(2)}, u32[]{:S(2)}) collective-permute-start(bf16[128,3456]{1,0:T(8,128)(2,1)S(1)} %pad_maximum_fusion), channel_id=1, source_target_pairs={{0,1},{1,0},{2,3},{3,2},{4,5},{5,4},{6,7},{7,6},{8,9},{9,8},{10,11... | collective-permute-start | bytes 2654216 | tf_op jit(solution)/shard_map/ppermute | solution.py:465
  188.0 18.0 %collective-permute-start.41 = (bf16[256,1152]{1,0:T(8,128)(2,1)S(1)}, bf16[256,1152]{1,0:T(8,128)(2,1)S(1)}, u32[]{:S(2)}, u32[]{:S(2)}) collective-permute-start(bf16[256,1152]{1,0:T(8,128)(2,1)S(1)} %add_convert_fusion), channel_id=1, source_target_pairs={{24,8},{16,0},{25,9},{17,1},{26,10},{18,2},{27,11},{19,3},{28,12},... | collective-permute-start | bytes 1769480 | tf_op jit(solution)/shard_map/ppermute | solution.py:685
  189.5 16.5 %collective-permute-start.45 = (bf16[576,256]{1,0:T(8,128)(2,1)S(1)}, bf16[576,256]{1,0:T(8,128)(2,1)S(1)}, u32[]{:S(2)}, u32[]{:S(2)}) collective-permute-start(bf16[576,256]{1,0:T(8,128)(2,1)S(1)} %add_convert_fusion.6), channel_id=1, source_target_pairs={{0,2},{1,3},{2,4},{3,5},{4,6},{5,7},{6,0},{7,1},{8,10},{9,11},{10,... | collective-permute-start | bytes 884744 | tf_op jit(solution)/shard_map/ppermute | solution.py:468
  189.6 12.9 %collective-permute-start.49 = (bf16[256,256]{1,0:T(8,128)(2,1)S(1)}, bf16[256,256]{1,0:T(8,128)(2,1)S(1)}, u32[]{:S(2)}, u32[]{:S(2)}) collective-permute-start(bf16[256,256]{1,0:T(8,128)(2,1)S(1)} %pad_maximum_fusion.1), channel_id=1, source_target_pairs={{0,6},{1,7},{2,0},{3,1},{4,2},{5,3},{6,4},{7,5},{8,14},{9,15},{10,... | collective-permute-start | bytes 393224 | tf_op jit(solution)/shard_map/ppermute | solution.py:468
  193.5 15.4 %collective-permute-start.50 = (bf16[576,256]{1,0:T(8,128)(2,1)S(1)}, bf16[576,256]{1,0:T(8,128)(2,1)S(1)}, u32[]{:S(2)}, u32[]{:S(2)}) collective-permute-start(bf16[576,256]{1,0:T(8,128)(2,1)S(1)} %add_convert_fusion.5), channel_id=1, source_target_pairs={{0,2},{1,3},{2,4},{3,5},{4,6},{5,7},{6,0},{7,1},{8,10},{9,11},{10,... | collective-permute-start | bytes 884744 | tf_op jit(solution)/shard_map/ppermute | solution.py:468
  206.8 4.0 %collective-permute-start.48 = (bf16[128,1152]{1,0:T(8,128)(2,1)S(1)}, bf16[128,1152]{1,0:T(8,128)(2,1)S(1)}, u32[]{:S(2)}, u32[]{:S(2)}) collective-permute-start(bf16[128,1152]{1,0:T(8,128)(2,1)S(1)} %get-tuple-element.144), channel_id=1, source_target_pairs={{0,1},{1,0},{2,3},{3,2},{4,5},{5,4},{6,7},{7,6},{8,9},{9,8},{10,11... | collective-permute-start | bytes 884744 | tf_op jit(solution)/shard_map/ppermute | solution.py:465
  (27 other events, 460.5 us)
